TPU v7x, 32 devices: a whole 2x2x4 slice. The times are simulated.
32 devices in a mesh: dp: 2 (over core), seq: 16 (over z, y, x).
Axes of the slice: x: 2, y: 2, z: 4, core: 2. Of those that a mesh axis runs over, the one named last changes fastest.
Arguments:
- queries: bfloat16 [16384, 512], P(('dp', 'seq')), parts along dimension 0, may hold values from -12 to 12
- keys: bfloat16 [16384, 512], P(('dp', 'seq')), parts along dimension 0, may hold values from -12 to 12
- values: bfloat16 [16384, 512], P(('dp', 'seq')), parts along dimension 0, may hold values from -6 to 6
- out_grad: bfloat16 [16384, 512], P(('dp', 'seq')), parts along dimension 0, may hold values from -6 to 6
- block_lists: int32 [128, 6], P(('dp', 'seq')), parts along dimension 0, may hold values from -1 to 63, as said below
Outputs:
- attended: bfloat16 [16384, 512], P(('dp', 'seq')), parts along dimension 0
- grad_queries: bfloat16 [16384, 512], P(('dp', 'seq')), parts along dimension 0
- grad_keys: bfloat16 [16384, 512], P(('dp', 'seq')), parts along dimension 0
- grad_values: bfloat16 [16384, 512], P(('dp', 'seq')), parts along dimension 0
There are 2 independent parts, one for each index of `dp`. A program takes and returns all parts, laid end to end along the dimension named above; each array names one. Nothing has to cross between parts.
Inputs may be any that keep to these rules, and one draw needn't show every extreme that they name: `block_lists`: blocks are numbered layer by layer; a calorimeter layer holds 1 to 2 consecutive blocks. Row a lists, in increasing order, every block whose layer is that of block a or next to it, so a itself and only blocks within 3 of a; the relation is symmetric; unused entries come last and are -1; some row uses all 6 entries.
All inputs are finite; a program needn't handle non-finite values.
Results may differ from a plain program's by a relative error of at most 0.02.
Values may be sent and summed in bfloat16 or wider, within the bound.
No kernel may reach another device: no remote copies, remote signals or barrier semaphores. Data moves between devices by JAX's collectives and lax.ppermute only.
A program may use at most 64 MiB of HBM per device.

v0:
```python
import jax
import jax.numpy as jnp
from jax import lax
from jax.sharding import PartitionSpec as P

HEADS = 4
HD = 128
BLOCK = 128
KB = 6
REACH = 3


def from_behind(value, axis, steps):
    count = lax.axis_size(axis)
    leading, last = (max(0, -steps), min(count, count - steps))
    return lax.ppermute(value, axis, [(source, source + steps) for source in range(leading, last)])


def with_halo(block, sides, width):
    for axis, dim in sides:
        count = lax.axis_size(axis)
        forward = [(i, i + 1) for i in range(count - 1)]
        backward = [(target, source) for source, target in forward]
        low = lax.ppermute(
            lax.slice_in_dim(block, block.shape[dim] - width, None, axis=dim), axis, forward
        )
        high = lax.ppermute(lax.slice_in_dim(block, 0, width, axis=dim), axis, backward)
        block = jnp.concatenate([low, block, high], axis=dim)
    return block


def pick_blocks(extended, slot_ids, blocks):
    tiles = extended.reshape(-1, BLOCK, HEADS, HD)
    return tiles[slot_ids].reshape(blocks, KB * BLOCK, HEADS, HD)


def send_back(payload, offset):
    return from_behind((payload[0], payload[1]), "seq", offset)


def body(queries, keys, values, out_grad, block_lists):
    score_scale = HD ** (-0.5)
    shard_rows = queries.shape[0]
    blocks = shard_rows // BLOCK
    width = HEADS * HD
    rim_rows = REACH * BLOCK
    position = lax.axis_index("seq")
    key_ext, value_ext = (
        with_halo(keys, (("seq", 0),), rim_rows),
        with_halo(values, (("seq", 0),), rim_rows),
    )
    usable = block_lists >= 0
    slot_ids = jnp.where(usable, block_lists - blocks * position + REACH, 0)
    key_mask = jnp.repeat(usable, BLOCK, axis=1)
    query_blocks = queries.reshape(blocks, BLOCK, HEADS, HD)
    grad_blocks = out_grad.reshape(blocks, BLOCK, HEADS, HD)
    key_rows = pick_blocks(key_ext, slot_ids, blocks)
    value_rows = pick_blocks(value_ext, slot_ids, blocks)
    scores = (
        jnp.einsum("bqhd,bkhd->bhqk", query_blocks, key_rows, preferred_element_type=jnp.float32)
        * score_scale
    )
    scores = jnp.where(key_mask[:, None, None, :], scores, -jnp.inf)
    peak = jnp.max(scores, axis=-1)
    log_total = peak + jnp.log(jnp.sum(jnp.exp(scores - peak[..., None]), axis=-1))
    probs = jnp.exp(scores - log_total[..., None])
    weights = probs.astype(jnp.bfloat16)
    attended = jnp.einsum(
        "bhqk,bkhd->bqhd", weights, value_rows, preferred_element_type=jnp.float32
    ).astype(jnp.bfloat16)
    row_delta = jnp.sum(grad_blocks.astype(jnp.float32) * attended.astype(jnp.float32), axis=-1)
    grad_probs = jnp.einsum(
        "bqhd,bkhd->bhqk", grad_blocks, value_rows, preferred_element_type=jnp.float32
    )
    grad_scores = (probs * (grad_probs - jnp.transpose(row_delta, (0, 2, 1))[..., None])).astype(
        jnp.bfloat16
    )
    grad_queries = (
        score_scale
        * jnp.einsum("bhqk,bkhd->bqhd", grad_scores, key_rows, preferred_element_type=jnp.float32)
    ).astype(jnp.bfloat16)
    slot_count = blocks + 2 * REACH
    slot_table = (
        (slot_ids[:, :, None] == jnp.arange(slot_count)[None, None, :]) & usable[:, :, None]
    ).astype(jnp.bfloat16)
    score_tiles = grad_scores.reshape(blocks, HEADS, BLOCK, KB, BLOCK)
    weight_tiles = weights.reshape(blocks, HEADS, BLOCK, KB, BLOCK)
    score_slots = jnp.einsum(
        "bhqkr,bks->bhqsr", score_tiles, slot_table, preferred_element_type=jnp.float32
    ).astype(jnp.bfloat16)
    weight_slots = jnp.einsum(
        "bhqkr,bks->bhqsr", weight_tiles, slot_table, preferred_element_type=jnp.float32
    ).astype(jnp.bfloat16)
    key_slots = (
        score_scale
        * jnp.einsum(
            "bhqsr,bqhd->srhd", score_slots, query_blocks, preferred_element_type=jnp.float32
        )
    ).reshape(slot_count * BLOCK, width)
    value_slots = jnp.einsum(
        "bhqsr,bqhd->srhd", weight_slots, grad_blocks, preferred_element_type=jnp.float32
    ).reshape(slot_count * BLOCK, width)
    from_upper = send_back((key_slots[:rim_rows], value_slots[:rim_rows]), -1)
    from_lower = send_back(
        (key_slots[rim_rows + shard_rows :], value_slots[rim_rows + shard_rows :]), 1
    )
    tail_pad = ((shard_rows - rim_rows, 0), (0, 0))
    head_pad = ((0, shard_rows - rim_rows), (0, 0))
    grad_keys = (
        key_slots[rim_rows : rim_rows + shard_rows]
        + jnp.pad(from_upper[0], tail_pad)
        + jnp.pad(from_lower[0], head_pad)
    )
    grad_values = (
        value_slots[rim_rows : rim_rows + shard_rows]
        + jnp.pad(from_upper[1], tail_pad)
        + jnp.pad(from_lower[1], head_pad)
    )
    return (
        attended.reshape(shard_rows, width),
        grad_queries.reshape(shard_rows, width),
        grad_keys.astype(jnp.bfloat16),
        grad_values.astype(jnp.bfloat16),
    )


def solution(mesh):
    return jax.shard_map(
        body,
        mesh=mesh,
        in_specs=(
            P(("dp", "seq"), None),
            P(("dp", "seq"), None),
            P(("dp", "seq"), None),
            P(("dp", "seq"), None),
            P(("dp", "seq"), None),
        ),
        out_specs=(
            P(("dp", "seq"), None),
            P(("dp", "seq"), None),
            P(("dp", "seq"), None),
            P(("dp", "seq"), None),
        ),
        check_vma=False,
    )
```

profile of v0, /device:TPU:8, one launch (start us, length us, event | category | flops | bytes accessed | tf_op | source)
XLA Modules:
  0.0 161.2 jit_solution(14880817502261747676)
XLA Ops:
  0.7 2.0 %fusion.58 = (bf16[384,512]{1,0:T(8,128)(2,1)}, bf16[384,512]{1,0:T(8,128)(2,1)S(1)}) fusion(bf16[512,512]{1,0:T(8,128)(2,1)} %param.6), kind=kLoop, calls=%fused_computation.69 | loop fusion | bytes 1572864 | tf_op jit(solution)/shard_map/slice | solution.py:25
  2.7 3.4 %collective-permute-start.2 = (bf16[384,512]{1,0:T(8,128)(2,1)}, bf16[384,512]{1,0:T(8,128)(2,1)S(1)}, u32[]{:S(2)}, u32[]{:S(2)}) collective-permute-start(bf16[384,512]{1,0:T(8,128)(2,1)} %get-tuple-element.12), channel_id=1, source_target_pairs={{0,1},{1,2},{2,3},{3,4},{4,5},{5,6},{6,7},{7,8},{8,9},{9,10},{10,1... | collective-permute-start | bytes 1179656 | tf_op jit(solution)/shard_map/ppermute | solution.py:24
  6.1 4.2 %collective-permute-start.3 = (bf16[384,512]{1,0:T(8,128)(2,1)S(1)}, bf16[384,512]{1,0:T(8,128)(2,1)S(1)}, u32[]{:S(2)}, u32[]{:S(2)}) collective-permute-start(bf16[384,512]{1,0:T(8,128)(2,1)S(1)} %get-tuple-element.13), channel_id=1, source_target_pairs={{1,0},{2,1},{3,2},{4,3},{5,4},{6,5},{7,6},{8,7},{9,8},{10,9},{11,1... | collective-permute-start | bytes 1179656 | tf_op jit(solution)/shard_map/ppermute | solution.py:27
  10.3 2.1 %fusion.57 = (bf16[384,512]{1,0:T(8,128)(2,1)}, bf16[384,512]{1,0:T(8,128)(2,1)}) fusion(bf16[512,512]{1,0:T(8,128)(2,1)} %param.7), kind=kLoop, calls=%fused_computation.68 | loop fusion | bytes 1572864 | tf_op jit(solution)/shard_map/slice | solution.py:25
  12.4 1.9 %collective-permute-start = (bf16[384,512]{1,0:T(8,128)(2,1)}, bf16[384,512]{1,0:T(8,128)(2,1)S(1)}, u32[]{:S(2)}, u32[]{:S(2)}) collective-permute-start(bf16[384,512]{1,0:T(8,128)(2,1)} %get-tuple-element.10), channel_id=1, source_target_pairs={{0,1},{1,2},{2,3},{3,4},{4,5},{5,6},{6,7},{7,8},{8,9},{9,10},{10,1... | collective-permute-start | bytes 1179656 | tf_op jit(solution)/shard_map/ppermute | solution.py:24
  14.3 5.7 %collective-permute-start.1 = (bf16[384,512]{1,0:T(8,128)(2,1)}, bf16[384,512]{1,0:T(8,128)(2,1)}, u32[]{:S(2)}, u32[]{:S(2)}) collective-permute-start(bf16[384,512]{1,0:T(8,128)(2,1)} %get-tuple-element.11), channel_id=1, source_target_pairs={{1,0},{2,1},{3,2},{4,3},{5,4},{6,5},{7,6},{8,7},{9,8},{10,9},{11,1... | collective-permute-start | bytes 1179656 | tf_op jit(solution)/shard_map/ppermute | solution.py:27
  20.1 0.1 broadcast_bitcast_fusion
  20.2 0.1 reshape.69
  20.3 0.9 reshape.61
  21.2 0.1 reshape.63
  21.3 1.0 copy.72
  22.4 10.4 %collective-permute-done.2 = bf16[384,512]{1,0:T(8,128)(2,1)S(1)} collective-permute-done((bf16[384,512]{1,0:T(8,128)(2,1)}, bf16[384,512]{1,0:T(8,128)(2,1)S(1)}, u32[]{:S(2)}, u32[]{:S(2)}) %collective-permute-start.2) | collective-permute-done | bytes 393248 | tf_op jit(solution)/shard_map/ppermute | solution.py:24
  32.8 0.1 pad_maximum_fusion.1
  32.9 0.3 reshape.59
  33.2 0.3 copy.63
  33.5 6.5 %collective-permute-done = bf16[384,512]{1,0:T(8,128)(2,1)S(1)} collective-permute-done((bf16[384,512]{1,0:T(8,128)(2,1)}, bf16[384,512]{1,0:T(8,128)(2,1)S(1)}, u32[]{:S(2)}, u32[]{:S(2)}) %collective-permute-start) | collective-permute-done | bytes 393248 | tf_op jit(solution)/shard_map/ppermute | solution.py:24
  40.0 1.9 %collective-permute-done.1 = bf16[384,512]{1,0:T(8,128)(2,1)} collective-permute-done((bf16[384,512]{1,0:T(8,128)(2,1)}, bf16[384,512]{1,0:T(8,128)(2,1)}, u32[]{:S(2)}, u32[]{:S(2)}) %collective-permute-start.1) | collective-permute-done | bytes 393248 | tf_op jit(solution)/shard_map/ppermute | solution.py:27
  42.0 1.1 pad_maximum_fusion
  43.1 1.2 reshape.57
  44.3 1.6 %copy.61 = bf16[10,128,4,128]{3,1,2,0:T(8,128)(2,1)S(1)} copy(bf16[10,128,4,128]{3,2,1,0:T(4,128)(2,1)} %reshape.57) | data formatting | bytes 2621440 | tf_op jit(solution)/shard_map/reshape | solution.py:33
  46.0 2.7 %gather_fusion = bf16[24,128,4,128]{3,1,2,0:T(8,128)(2,1)} fusion(bf16[10,128,4,128]{3,1,2,0:T(8,128)(2,1)S(1)} %copy.61, s32[1024]{0:T(1024)S(1)} %pad_clamp_fusion), kind=kCustom, calls=%fused_computation | custom fusion | bytes 6291552 | tf_op jit(solution)/shard_map/gather | solution.py:34
  48.7 3.9 %copy.62 = bf16[24,128,4,128]{3,1,0,2:T(8,128)(2,1)} copy(bf16[24,128,4,128]{3,1,2,0:T(8,128)(2,1)} %gather_fusion) | data formatting | bytes 6291456 | tf_op jit(solution)/shard_map/gather | solution.py:34
  52.6 2.7 %gather_fusion.1 = bf16[24,128,4,128]{3,1,2,0:T(8,128)(2,1)} fusion(bf16[10,128,4,128]{3,1,2,0:T(8,128)(2,1)S(1)} %copy.63, s32[1024]{0:T(1024)S(1)} %pad_clamp_fusion), kind=kCustom, calls=%fused_computation.1 | custom fusion | bytes 6291552 | tf_op jit(solution)/shard_map/gather | solution.py:34
  55.3 2.3 %copy.64 = bf16[24,128,4,128]{3,1,0,2:T(8,128)(2,1)S(1)} copy(bf16[24,128,4,128]{3,1,2,0:T(8,128)(2,1)} %gather_fusion.1) | data formatting | bytes 6291456 | tf_op jit(solution)/shard_map/gather | solution.py:34
  57.7 1.6 %bitcast_reduce_fusion = (f32[4,4,128]{2,1,0:T(4,128)S(1)}, f32[4,4,768,128]{3,2,1,0:T(8,128)S(1)}) fusion(pred[4,768]{1,0:T(4,128)(4,1)S(1)} %bitcast.128, bf16[4,128,4,128]{3,2,1,0:T(4,128)(2,1)S(1)} %copy-done.12, bf16[4,768,4,128]{3,1,0,2:T(8,128)(2,1)S(1)} %bitcast.112), kind=kOutput, calls=%fused_computation.8 | convolution fusion | flops 407369728 | bytes 9972736 | tf_op jit(solution)/shard_map/bqhd,bkhd->bhqk/dot_general | solution.py:60
  59.4 0.0 copy-done.5
  59.4 1.5 fusion.2
  60.9 1.5 fusion.4
  62.4 0.3 copy-done.7
  62.8 0.1 copy-done.14
  62.9 2.0 %multiply_reduce_fusion = (f32[4,128,4]{1,2,0:T(4,128)S(1)}, bf16[4,128,4,128]{1,3,2,0:T(8,128)(2,1)}) fusion(bf16[4,128,4,128]{1,3,2,0:T(8,128)(2,1)S(1)} %copy-done.14, bf16[4,4,128,768]{2,3,1,0:T(8,128)(2,1)S(1)} %fusion.4, bf16[4,768,4,128]{3,1,0,2:T(8,128)(2,1)S(1)} %bitcast.114), kind=kOutput, calls=%fused_computation.42 | convolution fusion | flops 403961856 | bytes 7348224 | tf_op jit(solution)/shard_map/bhqk,bkhd->bqhd/dot_general | solution.py:68
  64.8 3.5 %fusion = bf16[4,4,128,768]{2,3,1,0:T(8,128)(2,1)} fusion(f32[4,4,768,128]{3,2,1,0:T(8,128)S(1)} %get-tuple-element.15, f32[4,4,128]{2,1,0:T(4,128)S(1)} %bitcast.132, f32[4,4,128]{2,1,0:T(4,128)S(1)} %bitcast.125, pred[4,768]{1,0:T(4,128)(4,1)S(1)} %bitcast.131, bf16[4,128,4,128]{1,3,2,0:T(8,128)(2,1)S(1)} %copy-done.14, ...), kind=kOutput, calls=%fused_computation.5 | convolution fusion | flops 412090368 | bytes 13126656 | tf_op jit(solution)/shard_map/bqhd,bkhd->bhqk/dot_general | solution.py:72
  68.3 7.1 %copy.76 = bf16[4,4,128,6,128]{4,3,2,1,0:T(8,128)(2,1)} copy(bf16[4,4,128,6,128]{2,4,3,1,0:T(8,128)(2,1)} %bitcast.111) | data formatting | bytes 6291456 | tf_op jit(solution)/shard_map/reshape | solution.py:86
  75.5 4.8 %convert_bitcast_fusion.1 = bf16[4,4,128,10,128]{4,3,2,1,0:T(8,128)(2,1)S(1)} fusion(bf16[4,4,128,6,128]{4,3,2,1,0:T(8,128)(2,1)} %copy.76, s32[4,6]{1,0:T(4,128)S(1)} %get-tuple-element.5, pred[4,6]{1,0:T(4,128)(4,1)S(1)} %broadcast_compare_fusion), kind=kOutput, calls=%fused_computation.3 | convolution fusion | flops 34079200 | bytes 8388728 | tf_op jit(solution)/shard_map/bhqkr,bks->bhqsr/dot_general | solution.py:88
  80.3 2.2 %fusion.17 = f32[10,128,4,128]{3,1,0,2:T(8,128)S(1)} fusion(bf16[4,4,128,10,128]{4,3,2,1,0:T(8,128)(2,1)S(1)} %convert_bitcast_fusion.1, bf16[4,128,4,128,1]{3,2,1,0,4:T(4,128)(2,1)S(1)} %bitcast.123), kind=kOutput, calls=%fused_computation.27 | convolution fusion | flops 671744000 | bytes 8388608 | tf_op jit(solution)/shard_map/bhqsr,bqhd->srhd/dot_general | solution.py:96
  82.4 0.1 fusion.56
  82.6 0.5 copy.80
  83.1 1.1 copy.164
  84.2 0.5 copy.81
  84.7 1.0 copy.163
  85.7 3.4 %collective-permute-start.5 = (f32[384,512]{1,0:T(8,128)}, f32[384,512]{1,0:T(8,128)}, u32[]{:S(2)}, u32[]{:S(2)}) collective-permute-start(f32[384,512]{1,0:T(8,128)} %bitcast.102), channel_id=1, source_target_pairs={{0,1},{1,2},{2,3},{3,4},{4,5},{5,6},{6,7},{7,8},{8,9},{9,10},{10,1... | collective-permute-start | bytes 2359304 | tf_op jit(solution)/shard_map/ppermute | solution.py:16
  89.1 4.3 %collective-permute-start.4 = (f32[384,512]{1,0:T(8,128)}, f32[384,512]{1,0:T(8,128)}, u32[]{:S(2)}, u32[]{:S(2)}) collective-permute-start(f32[384,512]{1,0:T(8,128)} %bitcast.103), channel_id=1, source_target_pairs={{1,0},{2,1},{3,2},{4,3},{5,4},{6,5},{7,6},{8,7},{9,8},{10,9},{11,1... | collective-permute-start | bytes 2359304 | tf_op jit(solution)/shard_map/ppermute | solution.py:16
  93.4 4.9 %copy.82 = bf16[4,4,128,6,128]{4,3,2,1,0:T(8,128)(2,1)} copy(bf16[4,4,128,6,128]{2,4,3,1,0:T(8,128)(2,1)S(1)} %bitcast.108) | data formatting | bytes 6291456 | tf_op jit(solution)/shard_map/reshape | solution.py:87
  98.3 4.8 %convert_bitcast_fusion = bf16[4,4,128,10,128]{4,3,2,1,0:T(8,128)(2,1)S(1)} fusion(bf16[4,4,128,6,128]{4,3,2,1,0:T(8,128)(2,1)} %copy.82, s32[4,6]{1,0:T(4,128)S(1)} %get-tuple-element.5, pred[4,6]{1,0:T(4,128)(4,1)S(1)} %broadcast_compare_fusion), kind=kOutput, calls=%fused_computation.2 | convolution fusion | flops 34079200 | bytes 8388728 | tf_op jit(solution)/shard_map/bhqkr,bks->bhqsr/dot_general | solution.py:91
  103.1 2.1 %fusion.22 = f32[10,128,4,128]{3,1,0,2:T(8,128)S(1)} fusion(bf16[4,4,128,10,128]{4,3,2,1,0:T(8,128)(2,1)S(1)} %convert_bitcast_fusion, bf16[4,128,4,128,1]{3,2,1,0,4:T(4,128)(2,1)S(1)} %bitcast.120), kind=kOutput, calls=%fused_computation.28 | convolution fusion | flops 671088640 | bytes 8388608 | tf_op jit(solution)/shard_map/bhqsr,bqhd->srhd/dot_general | solution.py:100
  105.2 0.1 fusion.55
  105.3 1.4 copy-done.1
  106.7 0.5 copy.86
  107.2 1.0 copy.162
  108.2 0.5 copy.87
  108.7 0.9 copy.161
  109.6 1.9 %collective-permute-start.7 = (f32[384,512]{1,0:T(8,128)}, f32[384,512]{1,0:T(8,128)}, u32[]{:S(2)}, u32[]{:S(2)}) collective-permute-start(f32[384,512]{1,0:T(8,128)} %bitcast.100), channel_id=1, source_target_pairs={{0,1},{1,2},{2,3},{3,4},{4,5},{5,6},{6,7},{7,8},{8,9},{9,10},{10,1... | collective-permute-start | bytes 2359304 | tf_op jit(solution)/shard_map/ppermute | solution.py:16
  111.6 5.9 %collective-permute-start.6 = (f32[384,512]{1,0:T(8,128)}, f32[384,512]{1,0:T(8,128)}, u32[]{:S(2)}, u32[]{:S(2)}) collective-permute-start(f32[384,512]{1,0:T(8,128)} %bitcast.101), channel_id=1, source_target_pairs={{1,0},{2,1},{3,2},{4,3},{5,4},{6,5},{7,6},{8,7},{9,8},{10,9},{11,1... | collective-permute-start | bytes 2359304 | tf_op jit(solution)/shard_map/ppermute | solution.py:16
  117.4 1.1 fusion.34
  118.5 0.3 copy.75
  118.9 1.3 copy.69
  120.2 0.7 copy.79
  120.9 0.7 copy.85
  121.6 1.1 copy_bitcast_fusion.4
  122.7 18.4 %collective-permute-done.5 = f32[384,512]{1,0:T(8,128)} collective-permute-done((f32[384,512]{1,0:T(8,128)}, f32[384,512]{1,0:T(8,128)}, u32[]{:S(2)}, u32[]{:S(2)}) %collective-permute-start.5) | collective-permute-done | bytes 786464 | tf_op jit(solution)/shard_map/ppermute | solution.py:16
  141.1 2.4 %fusion.43 = bf16[512,512]{1,0:T(8,128)(2,1)} fusion(f32[64,8,4,128]{3,2,1,0:T(4,128)S(1)} %bitcast.110, f32[384,512]{1,0:T(8,128)} %collective-permute-done.5, f32[384,512]{1,0:T(8,128)} %collective-permute-done.4), kind=kLoop, calls=%fused_computation.41 | loop fusion | flops 786432 | bytes 3145728 | tf_op jit(solution)/shard_map/convert_element_type | solution.py:122
  143.5 12.4 %collective-permute-done.7 = f32[384,512]{1,0:T(8,128)} collective-permute-done((f32[384,512]{1,0:T(8,128)}, f32[384,512]{1,0:T(8,128)}, u32[]{:S(2)}, u32[]{:S(2)}) %collective-permute-start.7) | collective-permute-done | bytes 786464 | tf_op jit(solution)/shard_map/ppermute | solution.py:16
  155.9 2.9 %collective-permute-done.6 = f32[384,512]{1,0:T(8,128)} collective-permute-done((f32[384,512]{1,0:T(8,128)}, f32[384,512]{1,0:T(8,128)}, u32[]{:S(2)}, u32[]{:S(2)}) %collective-permute-start.6) | collective-permute-done | bytes 786464 | tf_op jit(solution)/shard_map/ppermute | solution.py:16
  158.8 2.4 %fusion.41 = bf16[512,512]{1,0:T(8,128)(2,1)} fusion(f32[64,8,4,128]{3,2,1,0:T(4,128)S(1)} %bitcast.109, f32[384,512]{1,0:T(8,128)} %collective-permute-done.7, f32[384,512]{1,0:T(8,128)} %collective-permute-done.6), kind=kLoop, calls=%fused_computation.38 | loop fusion | flops 786432 | bytes 3145728 | tf_op jit(solution)/shard_map/convert_element_type | solution.py:123
  (39 shorter events, 0.1 us)
Async XLA Ops:
  0.6 32.1 %copy-start.2 = (bf16[512,512]{1,0:T(8,128)(2,1)S(1)}, bf16[512,512]{1,0:T(8,128)(2,1)}, u32[]{:S(2)}) copy-start(bf16[512,512]{1,0:T(8,128)(2,1)} %param.6) | copy-start | bytes 1572868
  0.6 19.4 %copy-start.15 = (s32[4,6]{1,0:T(4,128)S(1)}, s32[4,6]{1,0:T(4,128)}, u32[]{:S(2)}) copy-start(s32[4,6]{1,0:T(4,128)} %param.9) | copy-start | bytes 292
  0.7 19.6 %copy-start.10 = (bf16[512,512]{1,0:T(8,128)(2,1)S(1)}, bf16[512,512]{1,0:T(8,128)(2,1)}, u32[]{:S(2)}) copy-start(bf16[512,512]{1,0:T(8,128)(2,1)} %param.5) | copy-start | bytes 1572868
  0.7 20.5 %copy-start.11 = (bf16[512,512]{1,0:T(8,128)(2,1)S(1)}, bf16[512,512]{1,0:T(8,128)(2,1)}, u32[]{:S(2)}) copy-start(bf16[512,512]{1,0:T(8,128)(2,1)} %param.8) | copy-start | bytes 1572868
  2.7 30.1 %collective-permute-start.2 = (bf16[384,512]{1,0:T(8,128)(2,1)}, bf16[384,512]{1,0:T(8,128)(2,1)S(1)}, u32[]{:S(2)}, u32[]{:S(2)}) collective-permute-start(bf16[384,512]{1,0:T(8,128)(2,1)} %get-tuple-element.12), channel_id=1, source_target_pairs={{0,1},{1,2},{2,3},{3,4},{4,5},{5,6},{6,7},{7,8},{8,9},{9,10},{10,1... | collective-permute-start | bytes 1179656 | tf_op jit(solution)/shard_map/ppermute | solution.py:24
  6.1 26.7 %collective-permute-start.3 = (bf16[384,512]{1,0:T(8,128)(2,1)S(1)}, bf16[384,512]{1,0:T(8,128)(2,1)S(1)}, u32[]{:S(2)}, u32[]{:S(2)}) collective-permute-start(bf16[384,512]{1,0:T(8,128)(2,1)S(1)} %get-tuple-element.13), channel_id=1, source_target_pairs={{1,0},{2,1},{3,2},{4,3},{5,4},{6,5},{7,6},{8,7},{9,8},{10,9},{11,1... | collective-permute-start | bytes 1179656 | tf_op jit(solution)/shard_map/ppermute | solution.py:27
  12.4 27.6 %collective-permute-start = (bf16[384,512]{1,0:T(8,128)(2,1)}, bf16[384,512]{1,0:T(8,128)(2,1)S(1)}, u32[]{:S(2)}, u32[]{:S(2)}) collective-permute-start(bf16[384,512]{1,0:T(8,128)(2,1)} %get-tuple-element.10), channel_id=1, source_target_pairs={{0,1},{1,2},{2,3},{3,4},{4,5},{5,6},{6,7},{7,8},{8,9},{9,10},{10,1... | collective-permute-start | bytes 1179656 | tf_op jit(solution)/shard_map/ppermute | solution.py:24
  14.3 27.7 %collective-permute-start.1 = (bf16[384,512]{1,0:T(8,128)(2,1)}, bf16[384,512]{1,0:T(8,128)(2,1)}, u32[]{:S(2)}, u32[]{:S(2)}) collective-permute-start(bf16[384,512]{1,0:T(8,128)(2,1)} %get-tuple-element.11), channel_id=1, source_target_pairs={{1,0},{2,1},{3,2},{4,3},{5,4},{6,5},{7,6},{8,7},{9,8},{10,9},{11,1... | collective-permute-start | bytes 1179656 | tf_op jit(solution)/shard_map/ppermute | solution.py:27
  21.3 11.5 %copy-start.8 = (bf16[4,128,4,128]{3,2,1,0:T(4,128)(2,1)}, bf16[4,128,4,128]{3,2,1,0:T(4,128)(2,1)S(1)}, u32[]{:S(2)}) copy-start(bf16[4,128,4,128]{3,2,1,0:T(4,128)(2,1)S(1)} %reshape.63) | copy-start | bytes 1572868
  32.9 9.1 %copy-start.3 = (bf16[512,512]{1,0:T(8,128)(2,1)S(1)}, bf16[512,512]{1,0:T(8,128)(2,1)}, u32[]{:S(2)}) copy-start(bf16[512,512]{1,0:T(8,128)(2,1)} %param.7) | copy-start | bytes 1572868
  55.3 2.4 %copy-start.12 = (bf16[4,128,4,128]{3,2,1,0:T(4,128)(2,1)S(1)}, bf16[4,128,4,128]{3,2,1,0:T(4,128)(2,1)}, u32[]{:S(2)}) copy-start(bf16[4,128,4,128]{3,2,1,0:T(4,128)(2,1)} %reshape.61) | copy-start | bytes 1572868
  57.7 1.7 %copy-start.5 = (bf16[24,128,4,128]{3,1,0,2:T(8,128)(2,1)}, bf16[24,128,4,128]{3,1,0,2:T(8,128)(2,1)S(1)}, u32[]{:S(2)}) copy-start(bf16[24,128,4,128]{3,1,0,2:T(8,128)(2,1)S(1)} %copy.64) | copy-start | bytes 9437188
  60.9 1.9 %copy-start.7 = (bf16[24,128,4,128]{3,1,0,2:T(8,128)(2,1)S(1)}, bf16[24,128,4,128]{3,1,0,2:T(8,128)(2,1)}, u32[]{:S(2)}) copy-start(bf16[24,128,4,128]{3,1,0,2:T(8,128)(2,1)} %copy.62) | copy-start | bytes 9437188
  60.9 2.0 %copy-start.14 = (bf16[4,128,4,128]{1,3,2,0:T(8,128)(2,1)S(1)}, bf16[4,128,4,128]{1,3,2,0:T(8,128)(2,1)}, u32[]{:S(2)}) copy-start(bf16[4,128,4,128]{1,3,2,0:T(8,128)(2,1)} %copy.72) | copy-start | bytes 1572868
  75.5 4.8 %copy-start.13 = (bf16[4,128,4,128]{3,2,1,0:T(4,128)(2,1)S(1)}, bf16[4,128,4,128]{3,2,1,0:T(4,128)(2,1)}, u32[]{:S(2)}) copy-start(bf16[4,128,4,128]{3,2,1,0:T(4,128)(2,1)} %reshape.61) | copy-start | bytes 1572868
  82.4 1.8 %copy-start = (f32[10,128,4,128]{3,1,0,2:T(8,128)}, f32[10,128,4,128]{3,1,0,2:T(8,128)S(1)}, u32[]{:S(2)}) copy-start(f32[10,128,4,128]{3,1,0,2:T(8,128)S(1)} %fusion.17) | copy-start | bytes 7864324
  85.7 55.4 %collective-permute-start.5 = (f32[384,512]{1,0:T(8,128)}, f32[384,512]{1,0:T(8,128)}, u32[]{:S(2)}, u32[]{:S(2)}) collective-permute-start(f32[384,512]{1,0:T(8,128)} %bitcast.102), channel_id=1, source_target_pairs={{0,1},{1,2},{2,3},{3,4},{4,5},{5,6},{6,7},{7,8},{8,9},{9,10},{10,1... | collective-permute-start | bytes 2359304 | tf_op jit(solution)/shard_map/ppermute | solution.py:16
  89.1 52.0 %collective-permute-start.4 = (f32[384,512]{1,0:T(8,128)}, f32[384,512]{1,0:T(8,128)}, u32[]{:S(2)}, u32[]{:S(2)}) collective-permute-start(f32[384,512]{1,0:T(8,128)} %bitcast.103), channel_id=1, source_target_pairs={{1,0},{2,1},{3,2},{4,3},{5,4},{6,5},{7,6},{8,7},{9,8},{10,9},{11,1... | collective-permute-start | bytes 2359304 | tf_op jit(solution)/shard_map/ppermute | solution.py:16
  98.3 4.8 %copy-start.9 = (bf16[4,128,4,128]{3,2,1,0:T(4,128)(2,1)S(1)}, bf16[4,128,4,128]{3,2,1,0:T(4,128)(2,1)}, u32[]{:S(2)}) copy-start(bf16[4,128,4,128]{3,2,1,0:T(4,128)(2,1)} %copy-done.8) | copy-start | bytes 1572868
  105.2 1.5 copy-start.1
  106.7 10.7 %copy-start.4 = (bf16[4,4,128,768]{2,3,1,0:T(8,128)(2,1)S(1)}, bf16[4,4,128,768]{2,3,1,0:T(8,128)(2,1)}, u32[]{:S(2)}) copy-start(bf16[4,4,128,768]{2,3,1,0:T(8,128)(2,1)} %fusion) | copy-start | bytes 9437188
  106.7 10.7 %copy-start.6 = (bf16[24,128,4,128]{3,1,0,2:T(8,128)(2,1)S(1)}, bf16[24,128,4,128]{3,1,0,2:T(8,128)(2,1)}, u32[]{:S(2)}) copy-start(bf16[24,128,4,128]{3,1,0,2:T(8,128)(2,1)} %copy-done.5) | copy-start | bytes 9437188
  109.6 46.3 %collective-permute-start.7 = (f32[384,512]{1,0:T(8,128)}, f32[384,512]{1,0:T(8,128)}, u32[]{:S(2)}, u32[]{:S(2)}) collective-permute-start(f32[384,512]{1,0:T(8,128)} %bitcast.100), channel_id=1, source_target_pairs={{0,1},{1,2},{2,3},{3,4},{4,5},{5,6},{6,7},{7,8},{8,9},{9,10},{10,1... | collective-permute-start | bytes 2359304 | tf_op jit(solution)/shard_map/ppermute | solution.py:16
  111.5 8.7 %slice-start = ((f32[10,128,4,128]{3,1,0,2:T(8,128)}), f32[4,128,4,128]{3,1,0,2:T(8,128)S(1)}, s32[]{:S(2)}) async-start(f32[10,128,4,128]{3,1,0,2:T(8,128)} %copy-done), calls=%async_computation | async-start | bytes 2097152 | tf_op jit(solution)/shard_map/slice | solution.py:110
  111.6 47.2 %collective-permute-start.6 = (f32[384,512]{1,0:T(8,128)}, f32[384,512]{1,0:T(8,128)}, u32[]{:S(2)}, u32[]{:S(2)}) collective-permute-start(f32[384,512]{1,0:T(8,128)} %bitcast.101), channel_id=1, source_target_pairs={{1,0},{2,1},{3,2},{4,3},{5,4},{6,5},{7,6},{8,7},{9,8},{10,9},{11,1... | collective-permute-start | bytes 2359304 | tf_op jit(solution)/shard_map/ppermute | solution.py:16
  118.5 2.4 %slice-start.1 = ((f32[10,128,4,128]{3,1,0,2:T(8,128)}), f32[4,128,4,128]{3,1,0,2:T(8,128)S(1)}, s32[]{:S(2)}) async-start(f32[10,128,4,128]{3,1,0,2:T(8,128)} %copy-done.1), calls=%async_computation.1 | async-start | bytes 2097152 | tf_op jit(solution)/shard_map/slice | solution.py:115
where the time goes:
time: 162 us; the launch traced here: 161 us
  waiting for transfers between devices  52.5 us (32%)
  local copies, waits for them, and re-layouts  46 us (28%)
  starting transfers between devices  30.6 us (19%)
  matrix products  22 us (14%)
  other arithmetic  8.96 us (6%)
    ppermute x4, waiting for transfers between devices, from_behind(): lax.ppermute(value, axis, [(source, source + steps) for source in range(l...  33.7 us
    ppermute x2, waiting for transfers between devices, with_halo(): lax.ppermute(lax.slice_in_dim(block, block.shape[dim] - width, None, axis...  16.9 us
    ppermute x4, starting transfers between devices, from_behind(): lax.ppermute(value, axis, [(source, source + steps) for source in range(l...  15.4 us
    gather x4, local copies, waits for them, and re-layouts, pick_blocks(): return tiles[slot_ids].reshape(blocks, KB * BLOCK, HEADS, HD)  11.7 us
    ppermute x2, starting transfers between devices, with_halo(): lax.ppermute(lax.slice_in_dim(block, 0, width, axis=dim), axis, backward)  9.96 us
    reshape x1, local copies, waits for them, and re-layouts, body(): score_tiles = grad_scores.reshape(blocks, HEADS, BLOCK, KB, BLOCK)  7.12 us
    unnamed x38, local copies, waits for them, and re-layouts  5.96 us
    ppermute x2, starting transfers between devices, with_halo(): lax.ppermute(lax.slice_in_dim(block, block.shape[dim] - width, None, axis...  5.29 us
  transfers between devices with their start and end apart: 8, of which 6 were waited for; matrix products, arithmetic and copies ran while one was open for 17% of the time, Pallas kernels for 0%

commit v1 on v0

v1 whole, which is shorter than its diff:
```python
import functools
import math

import jax
import jax.numpy as jnp
from jax import lax
from jax.experimental import pallas as pl
from jax.experimental.pallas import tpu as pltpu
from jax.sharding import PartitionSpec as P

HEADS = 4
HD = 128
BLOCK = 128
KB = 6
SCALE = HD**-0.5
SCALE2 = SCALE * math.log2(math.e)
NEG = -1e30
F32 = jnp.float32
BF16 = jnp.bfloat16


def dot(a, b, ca, cb):
    return lax.dot_general(a, b, (((ca,), (cb,)), ((), ())), preferred_element_type=F32)


def bias_of(cond):
    return jnp.where(cond, 0.0, NEG).astype(F32)


class Place:
    def __init__(self, lists, nb):
        self.nb = nb
        position = lax.axis_index("seq")
        base = position * nb
        self.has_left = position > 0
        self.has_right = position < lax.axis_size("seq") - 1
        self.lo = [lists[a, 0] - base for a in range(nb)]
        self.hi = []
        for a in range(nb):
            top = lists[a, 0]
            for e in range(1, KB):
                top = jnp.maximum(top, lists[a, e])
            self.hi.append(top - base)
        lo, hi, end = self.lo, self.hi, nb - 1
        self.cut_right = ((lo[end - 1] != lo[end]) | (hi[end - 1] != hi[end])) & (hi[end - 1] >= nb)
        self.cut_left = ((lo[0] != lo[1]) | (hi[0] != hi[1])) & (lo[1] <= -1)
        r, l = self.cut_right.astype(jnp.int32), self.cut_left.astype(jnp.int32)
        self.sent_right = [(0, end - 1 + r), (r, end)]
        self.sent_left = [(1 - l, 0), (1, 1 - l)]
        self.from_left = [(0, -2 + l), (l, -1)]
        self.from_right = [(1 - r, nb), (1, nb + 1 - r)]

    def adjacent(self, own, other):
        return (self.lo[own] <= other) & (other <= self.hi[own])

    def sides(self):
        return (
            (0, 0, self.from_left, 0, self.cut_left),
            (1, self.nb - 3, self.from_right, self.nb - 1, self.cut_right),
        )


def lane(h, half):
    start = (h + 2 * half) * HD
    return pl.ds(start if isinstance(start, int) else pl.multiple_of(start, HD), HD)


def rows_of(b):
    start = b * BLOCK
    return pl.ds(start if isinstance(start, int) else pl.multiple_of(start, BLOCK), BLOCK)


def pack_kernel(nb, lists, q, k, v, g, ra, la, rb, lb):
    at = Place(lists, nb)
    for half, (right, left) in enumerate(((ra, la), (rb, lb))):
        for message, sent in ((right, at.sent_right), (left, at.sent_left)):
            for slot, (h, b) in enumerate(sent):
                for i, array in enumerate((q, k, v, g)):
                    message[2 * i + slot] = array[rows_of(b), lane(h, half)]


def own_forward_kernel(nb, lists, q, k, v, g, stats, ot):
    at = Place(lists, nb)
    biases = [[bias_of(at.adjacent(a, b)) for b in range(nb)] for a in range(nb)]
    for h in range(HEADS):
        cols = lane(h, 0)
        kh, vh = k[:, cols], v[:, cols]
        for a in range(nb):
            rows = rows_of(a)
            s = dot(kh, q[rows, cols], 1, 1)
            s = jnp.concatenate(
                [s[b * BLOCK : (b + 1) * BLOCK] * SCALE2 + biases[a][b] for b in range(nb)], axis=0
            )
            m = jnp.max(s, axis=0, keepdims=True)
            p = jnp.exp2(s - m)
            dp = dot(vh, g[rows, cols], 1, 1)
            stats[h, 0:1, rows] = m
            stats[h, 1:2, rows] = jnp.sum(p, axis=0, keepdims=True)
            stats[h, 2:3, rows] = jnp.sum(p * dp, axis=0, keepdims=True)
            ot[h, :, rows] = dot(vh, p.astype(BF16), 0, 0)


def guest_forward_kernel(
    nb, half, lists, q, k, v, g, in_left, in_right, stats0, ot0, stats, ot, o_left, o_right, st_left, st_right
):
    at = Place(lists, nb)
    for h in range(2):
        stats[h] = stats0[2 * half + h]
        ot[h] = ot0[2 * half + h]
    for side, first, guests, shared, cut in at.sides():
        message = (in_left, in_right)[side]
        o_out = (o_left, o_right)[side]
        st_out = (st_left, st_right)[side]
        span = pl.ds(first * BLOCK, 3 * BLOCK)
        for slot, (h, number) in enumerate(guests):
            qg, kg, vg, gg = (message[2 * i + slot] for i in range(4))
            cols = lane(h, half)
            qh, kh, vh, gh = (array[span, cols] for array in (q, k, v, g))
            near = [at.adjacent(first + b, number) for b in range(3)]
            s = dot(kh, qg, 1, 1)
            s = jnp.concatenate(
                [s[b * BLOCK : (b + 1) * BLOCK] * SCALE2 + bias_of(near[b]) for b in range(3)], axis=0
            )
            m = jnp.max(s, axis=0, keepdims=True)
            p = jnp.exp2(s - m)
            dp = dot(vh, gg, 1, 1)
            total = jnp.sum(p, axis=0, keepdims=True)
            inverse = 1.0 / total
            st_out[2 * slot : 2 * slot + 1, :] = m + jnp.log2(total)
            st_out[2 * slot + 1 : 2 * slot + 2, :] = jnp.sum(p * dp, axis=0, keepdims=True) * inverse
            o_out[slot] = (dot(vh, p.astype(BF16), 0, 0) * inverse).astype(BF16)
            open_ = [
                near[b] & jnp.logical_not(cut) if first + b == shared else near[b] for b in range(3)
            ]
            s = dot(kg, qh, 1, 1)
            s = jnp.concatenate(
                [s[:, b * BLOCK : (b + 1) * BLOCK] * SCALE2 + bias_of(open_[b]) for b in range(3)], axis=1
            )
            old = stats[h, 0:1, span]
            m = jnp.maximum(old, jnp.max(s, axis=0, keepdims=True))
            shrink = jnp.exp2(old - m)
            p = jnp.exp2(s - m)
            dp = dot(vg, gh, 1, 1)
            stats[h, 0:1, span] = m
            stats[h, 1:2, span] = stats[h, 1:2, span] * shrink + jnp.sum(p, axis=0, keepdims=True)
            stats[h, 2:3, span] = stats[h, 2:3, span] * shrink + jnp.sum(p * dp, axis=0, keepdims=True)
            ot[h, :, span] = ot[h, :, span] * shrink + dot(vg, p.astype(BF16), 0, 0)
    for h in range(2):
        total = stats[h, 1:2, :]
        stats[h, 3:4, :] = stats[h, 0:1, :] + jnp.log2(total)
        stats[h, 4:5, :] = stats[h, 2:3, :] / total
    for st_out, sent in ((st_left, at.sent_left), (st_right, at.sent_right)):
        for slot, (h, b) in enumerate(sent):
            rows = rows_of(b)
            st_out[4 + 2 * slot : 5 + 2 * slot, :] = stats[h, 3:4, rows]
            st_out[5 + 2 * slot : 6 + 2 * slot, :] = stats[h, 4:5, rows]


def merged(l1, d1, l2, d2):
    m = jnp.maximum(l1, l2)
    w1, w2 = jnp.exp2(l1 - m), jnp.exp2(l2 - m)
    total = w1 + w2
    return m + jnp.log2(total), (w1 * d1 + w2 * d2) / total


def guest_backward_kernel(
    nb, half, lists, q, k, v, g, in_left, in_right, stats, st_left, st_right, got_left, got_right,
    fin, back_left, back_right, aq, ak, av,
):
    at = Place(lists, nb)
    for array in (aq, ak, av):
        array[...] = jnp.zeros_like(array)
    for h in range(2):
        fin[h, 0:2, :] = stats[h, 3:5, :]
    for got, sent, there in ((got_left, at.sent_left, at.has_left), (got_right, at.sent_right, at.has_right)):
        gone = bias_of(there)
        for slot, (h, b) in enumerate(sent):
            rows = rows_of(b)
            part = got[2 * slot : 2 * slot + 1, :] + gone
            total, delta = merged(
                fin[h, 0:1, rows], fin[h, 1:2, rows], part, got[2 * slot + 1 : 2 * slot + 2, :]
            )
            fin[h, 0:1, rows] = total
            fin[h, 1:2, rows] = delta
    for side, first, guests, shared, cut in at.sides():
        message, back = (in_left, in_right)[side], (back_left, back_right)[side]
        mine, got = (st_left, st_right)[side], (got_left, got_right)[side]
        span = pl.ds(first * BLOCK, 3 * BLOCK)
        for slot, (h, number) in enumerate(guests):
            qg, kg, vg, gg = (message[2 * i + slot] for i in range(4))
            cols = lane(h, half)
            qh, kh, vh, gh = (array[span, cols] for array in (q, k, v, g))
            near = [at.adjacent(first + b, number) for b in range(3)]
            total, delta = merged(
                mine[2 * slot : 2 * slot + 1, :],
                mine[2 * slot + 1 : 2 * slot + 2, :],
                got[4 + 2 * slot : 5 + 2 * slot, :],
                got[5 + 2 * slot : 6 + 2 * slot, :],
            )
            s = dot(kh, qg, 1, 1)
            s = jnp.concatenate(
                [s[b * BLOCK : (b + 1) * BLOCK] * SCALE2 + bias_of(near[b]) for b in range(3)], axis=0
            )
            p = jnp.exp2(s - total)
            ds = (p * (dot(vh, gg, 1, 1) - delta)).astype(BF16)
            ak[h, span, :] += dot(ds, qg, 1, 0)
            av[h, span, :] += dot(p.astype(BF16), gg, 1, 0)
            back[slot] = dot(ds, kh, 0, 0).astype(BF16)
            open_ = [
                near[b] & jnp.logical_not(cut) if first + b == shared else near[b] for b in range(3)
            ]
            s = dot(kg, qh, 1, 1)
            s = jnp.concatenate(
                [s[:, b * BLOCK : (b + 1) * BLOCK] * SCALE2 + bias_of(open_[b]) for b in range(3)], axis=1
            )
            p = jnp.exp2(s - fin[h, 0:1, span])
            ds = (p * (dot(vg, gh, 1, 1) - fin[h, 1:2, span])).astype(BF16)
            back[2 + slot] = dot(ds, qh, 1, 0).astype(BF16)
            back[4 + slot] = dot(p.astype(BF16), gh, 1, 0).astype(BF16)
            aq[h, span, :] += dot(ds, kg, 0, 0)


def own_backward_kernel(
    nb, half, lists, q, k, v, g, stats, ot, fin, o_left, o_right, got_left, got_right, aq0, ak0, av0,
    att, aq, ak, av, total_t, ps, dss,
):
    at = Place(lists, nb)
    biases = [[bias_of(at.adjacent(a, b)) for b in range(nb)] for a in range(nb)]
    for h in range(2):
        total_t[h] = ot[h] * jnp.exp2(stats[h, 0:1, :] - fin[h, 0:1, :])
    for got, o_in, sent, there in (
        (got_left, o_left, at.sent_left, at.has_left),
        (got_right, o_right, at.sent_right, at.has_right),
    ):
        gone = bias_of(there)
        for slot, (h, b) in enumerate(sent):
            rows = rows_of(b)
            weight = jnp.exp2(got[2 * slot : 2 * slot + 1, :] + gone - fin[h, 0:1, rows])
            total_t[h, :, rows] += o_in[slot].astype(F32) * weight
    for h in range(2):
        cols = lane(h, half)
        kh, vh = k[:, cols], v[:, cols]
        for a in range(nb):
            rows = rows_of(a)
            att[rows, lane(h, 0)] = total_t[h, :, rows].T.astype(BF16)
            s = dot(kh, q[rows, cols], 1, 1)
            s = jnp.concatenate(
                [s[b * BLOCK : (b + 1) * BLOCK] * SCALE2 + biases[a][b] for b in range(nb)], axis=0
            )
            p = jnp.exp2(s - fin[h, 0:1, rows])
            ps[:, rows] = p.astype(BF16)
            dss[:, rows] = (p * (dot(vh, g[rows, cols], 1, 1) - fin[h, 1:2, rows])).astype(BF16)
        av[h] = av0[h] + dot(ps[...], g[:, cols], 1, 0)
        ak[h] = ak0[h] + dot(dss[...], q[:, cols], 1, 0)
        aq[h] = aq0[h] + dot(dss[...], kh, 0, 0)


def finish_kernel(nb, lists, *refs):
    at = Place(lists, nb)
    halves = (refs[:6], refs[6:12])
    att_out, q_out, k_out, v_out, sq, sk, sv = refs[12:]
    for half, (att, aq, ak, av, back_left, back_right) in enumerate(halves):
        for h in range(2):
            att_out[:, lane(h, half)] = att[:, lane(h, 0)]
        for total, part in ((sq, aq), (sk, ak), (sv, av)):
            total[...] = part[...]
        for back, sent in ((back_left, at.sent_left), (back_right, at.sent_right)):
            for slot, (h, b) in enumerate(sent):
                rows = rows_of(b)
                for i, total in enumerate((sq, sk, sv)):
                    total[h, rows, :] += back[2 * i + slot].astype(F32)
        for h in range(2):
            cols = lane(h, half)
            q_out[:, cols] = (sq[h] * SCALE).astype(BF16)
            k_out[:, cols] = (sk[h] * SCALE).astype(BF16)
            v_out[:, cols] = sv[h].astype(BF16)


def call(kernel, name, outs, args, scratch=(), flops=0):
    moved = sum(math.prod(s.shape) * s.dtype.itemsize for s in (*outs, *args))
    vmem = pl.BlockSpec(memory_space=pltpu.VMEM)
    return pl.pallas_call(
        kernel,
        out_shape=tuple(outs),
        in_specs=[pl.BlockSpec(memory_space=pltpu.SMEM)] + [vmem] * (len(args) - 1),
        out_specs=tuple([vmem] * len(outs)),
        scratch_shapes=scratch,
        cost_estimate=pl.CostEstimate(flops=flops, bytes_accessed=moved, transcendentals=0),
        compiler_params=pltpu.CompilerParams(vmem_limit_bytes=24 << 20),
        name=name,
    )(*args)


def sds(shape, dtype):
    return jax.ShapeDtypeStruct(shape, dtype)


def body(q, k, v, g, lists):
    rows, width = q.shape
    nb = rows // BLOCK
    count = lax.axis_size("seq")
    forward = [(i, i + 1) for i in range(count - 1)]
    backward = [(i + 1, i) for i in range(count - 1)]

    def swap(to_left, to_right):
        return lax.ppermute(to_right, "seq", forward), lax.ppermute(to_left, "seq", backward)

    arrays = (lists, q, k, v, g)
    tile8 = sds((8, BLOCK, HD), BF16)
    ra, la, rb, lb = call(functools.partial(pack_kernel, nb), "pack", [tile8] * 4, arrays)
    guests = [swap(la, ra), swap(lb, rb)]
    stats0, ot0 = call(
        functools.partial(own_forward_kernel, nb), "own_forward",
        [sds((HEADS, 8, rows), F32), sds((HEADS, HD, rows), F32)], arrays, flops=3 << 30,
    )
    tile2, st = sds((2, BLOCK, HD), BF16), sds((8, HD), F32)
    tile6 = sds((6, BLOCK, HD), BF16)
    acc = sds((2, rows, HD), F32)
    pieces = []
    for half in range(2):
        gl, gr = guests[half]
        stats, ot, o_l, o_r, st_l, st_r = call(
            functools.partial(guest_forward_kernel, nb, half), "guest_forward",
            [sds((2, 8, rows), F32), sds((2, HD, rows), F32), tile2, tile2, st, st],
            (*arrays, gl, gr, stats0, ot0), flops=2 << 30,
        )
        got_l, got_r = swap(st_l, st_r)
        go_l, go_r = swap(o_l, o_r)
        fin, b_l, b_r, aq, ak, av = call(
            functools.partial(guest_backward_kernel, nb, half), "guest_backward",
            [sds((2, 8, rows), F32), tile6, tile6, acc, acc, acc],
            (*arrays, gl, gr, stats, st_l, st_r, got_l, got_r), flops=2 << 30,
        )
        back_l, back_r = swap(b_l, b_r)
        att, aq, ak, av = call(
            functools.partial(own_backward_kernel, nb, half), "own_backward",
            [sds((rows, 2 * HD), BF16), acc, acc, acc],
            (*arrays, stats, ot, fin, go_l, go_r, got_l, got_r, aq, ak, av),
            scratch=(
                pltpu.VMEM((2, HD, rows), F32), pltpu.VMEM((rows, rows), BF16), pltpu.VMEM((rows, rows), BF16),
            ), flops=3 << 30,
        )
        pieces += [att, aq, ak, av, back_l, back_r]
    return call(
        functools.partial(finish_kernel, nb), "finish", [sds((rows, width), BF16)] * 4, (lists, *pieces),
        scratch=tuple(pltpu.VMEM((2, rows, HD), F32) for _ in range(3)),
    )


def solution(mesh):
    spec = P(("dp", "seq"), None)
    return jax.shard_map(
        body, mesh=mesh, in_specs=(spec,) * 5, out_specs=(spec,) * 4, check_vma=False
    )
```

time: 162 us -> 93.2 us (0.58)
  the two profiles are of different devices: /device:TPU:8 before, /device:TPU:14 now
where the time goes in v1:
time: 93.2 us; the launch traced here: 92.5 us
  starting transfers between devices  55.2 us (59%)
  Pallas kernels  24.4 us (26%)
  waiting for transfers between devices  7.05 us (8%)
  local copies, waits for them, and re-layouts  4.84 us (5%)
    ppermute x8, starting transfers between devices, swap(): lax.ppermute(to_right, 'seq', forward)  33.9 us
    pallas_call x9, Pallas kernels, call(): pl.pallas_call(kernel, out_shape=tuple(outs), in_specs=[pl.BlockSpec(memo...  24.4 us
    ppermute x8, starting transfers between devices, swap(): lax.ppermute(to_left, 'seq', backward)  21.2 us
    ppermute x8, waiting for transfers between devices, swap(): lax.ppermute(to_left, 'seq', backward)  7.03 us
    unnamed x10, local copies, waits for them, and re-layouts  4.84 us
  transfers between devices with their start and end apart: 16, of which 2 were waited for; matrix products, arithmetic and copies ran while one was open for 0% of the time, Pallas kernels for 23%

profile of v1, /device:TPU:14, one launch (start us, length us, event | category | flops | bytes accessed | tf_op | source)
XLA Modules:
  0.0 92.5 jit_solution(10211853443956364387)
XLA Ops:
  0.6 0.0 copy-start
  0.6 1.0 %copy-done = bf16[512,512]{1,0:T(8,128)(2,1)S(1)} copy-done((bf16[512,512]{1,0:T(8,128)(2,1)S(1)}, bf16[512,512]{1,0:T(8,128)(2,1)}, u32[]{:S(2)}) %copy-start) | copy-done | bytes 524312
  1.7 0.0 copy-start.1
  1.7 1.0 %copy-done.1 = bf16[512,512]{1,0:T(8,128)(2,1)S(1)} copy-done((bf16[512,512]{1,0:T(8,128)(2,1)S(1)}, bf16[512,512]{1,0:T(8,128)(2,1)}, u32[]{:S(2)}) %copy-start.1) | copy-done | bytes 524312
  2.7 0.0 copy-start.2
  2.7 1.0 %copy-done.2 = bf16[512,512]{1,0:T(8,128)(2,1)S(1)} copy-done((bf16[512,512]{1,0:T(8,128)(2,1)S(1)}, bf16[512,512]{1,0:T(8,128)(2,1)}, u32[]{:S(2)}) %copy-start.2) | copy-done | bytes 524312
  3.8 0.0 copy-start.3
  3.8 1.0 %copy-done.3 = bf16[512,512]{1,0:T(8,128)(2,1)S(1)} copy-done((bf16[512,512]{1,0:T(8,128)(2,1)S(1)}, bf16[512,512]{1,0:T(8,128)(2,1)}, u32[]{:S(2)}) %copy-start.3) | copy-done | bytes 524312
  4.8 0.0 copy-start.4
  4.8 0.7 copy-done.4
  5.5 0.8 pack.1
  6.3 3.4 %collective-permute-start = (bf16[8,128,128]{2,1,0:T(8,128)(2,1)S(1)}, bf16[8,128,128]{2,1,0:T(8,128)(2,1)S(1)}, u32[]{:S(2)}, u32[]{:S(2)}) collective-permute-start(bf16[8,128,128]{2,1,0:T(8,128)(2,1)S(1)} %get-tuple-element.42), channel_id=1, source_target_pairs={{0,1},{1,2},{2,3},{3,4},{4,5},{5,6},{6,7},{7,8},{8,9},{9,10},{10,1... | collective-permute-start | bytes 786440 | tf_op jit(solution)/shard_map/ppermute | solution.py:306
  9.7 2.4 %collective-permute-start.1 = (bf16[8,128,128]{2,1,0:T(8,128)(2,1)S(1)}, bf16[8,128,128]{2,1,0:T(8,128)(2,1)S(1)}, u32[]{:S(2)}, u32[]{:S(2)}) collective-permute-start(bf16[8,128,128]{2,1,0:T(8,128)(2,1)S(1)} %get-tuple-element.43), channel_id=1, source_target_pairs={{1,0},{2,1},{3,2},{4,3},{5,4},{6,5},{7,6},{8,7},{9,8},{10,9},{11,1... | collective-permute-start | bytes 786440 | tf_op jit(solution)/shard_map/ppermute | solution.py:306
  12.1 5.2 %collective-permute-start.8 = (bf16[8,128,128]{2,1,0:T(8,128)(2,1)S(1)}, bf16[8,128,128]{2,1,0:T(8,128)(2,1)S(1)}, u32[]{:S(2)}, u32[]{:S(2)}) collective-permute-start(bf16[8,128,128]{2,1,0:T(8,128)(2,1)S(1)} %get-tuple-element.62), channel_id=1, source_target_pairs={{0,1},{1,2},{2,3},{3,4},{4,5},{5,6},{6,7},{7,8},{8,9},{9,10},{10,1... | collective-permute-start | bytes 786440 | tf_op jit(solution)/shard_map/ppermute | solution.py:306
  17.3 1.9 %collective-permute-start.9 = (bf16[8,128,128]{2,1,0:T(8,128)(2,1)S(1)}, bf16[8,128,128]{2,1,0:T(8,128)(2,1)S(1)}, u32[]{:S(2)}, u32[]{:S(2)}) collective-permute-start(bf16[8,128,128]{2,1,0:T(8,128)(2,1)S(1)} %get-tuple-element.63), channel_id=1, source_target_pairs={{1,0},{2,1},{3,2},{4,3},{5,4},{6,5},{7,6},{8,7},{9,8},{10,9},{11,1... | collective-permute-start | bytes 786440 | tf_op jit(solution)/shard_map/ppermute | solution.py:306
  19.3 5.1 %own_forward.1 = (f32[4,8,512]{2,1,0:T(8,128)S(1)}, f32[4,128,512]{2,1,0:T(8,128)S(1)}) custom-call(s32[4,6]{1,0:T(4,128)S(1)} %copy-done.4, bf16[512,512]{1,0:T(8,128)(2,1)S(1)} %copy-done, bf16[512,512]{1,0:T(8,128)(2,1)S(1)} %copy-done.1, bf16[512,512]{1,0:T(8,128)(2,1)S(1)} %copy-done.2, bf16[512,512]{1,0:T(8,128)(2,1)S(1)} %copy-done.3), custom_call_target="tpu_custom_call" | custom-call | flops 3221225472 | bytes 3211360 | tf_op jit(solution)/shard_map/own_forward/pallas_call | solution.py:282
  24.4 0.0 collective-permute-done.in_left
  24.4 2.0 %collective-permute-done.1.in_right = bf16[8,128,128]{2,1,0:T(8,128)(2,1)S(1)} collective-permute-done((bf16[8,128,128]{2,1,0:T(8,128)(2,1)S(1)}, bf16[8,128,128]{2,1,0:T(8,128)(2,1)S(1)}, u32[]{:S(2)}, u32[]{:S(2)}) %collective-permute-start.1) | collective-permute-done | bytes 262176 | tf_op jit(solution)/shard_map/ppermute | solution.py:306
  26.4 2.8 %guest_forward.2 = (f32[2,8,512]{2,1,0:T(8,128)S(1)}, f32[2,128,512]{2,1,0:T(8,128)S(1)}, bf16[2,128,128]{2,1,0:T(8,128)(2,1)S(1)}, bf16[2,128,128]{2,1,0:T(8,12...) custom-call(s32[4,6]{1,0:T(4,128)S(1)} %copy-done.4, bf16[512,512]{1,0:T(8,128)(2,1)S(1)} %copy-done, ...), custom_call_target="tpu_custom_call" | custom-call | flops 2147483648 | bytes 4431968 | tf_op jit(solution)/shard_map/guest_forward/pallas_call | solution.py:282
  29.3 4.4 %collective-permute-start.3 = (f32[8,128]{1,0:T(8,128)S(1)}, f32[8,128]{1,0:T(8,128)S(1)}, u32[]{:S(2)}, u32[]{:S(2)}) collective-permute-start(f32[8,128]{1,0:T(8,128)S(1)} %get-tuple-element.48.st_left), channel_id=1, source_target_pairs={{1,0},{2,1},{3,2},{4,3},{5,4},{6,5},{7,6},{8,7},{9,8},{10,9},{11,1... | collective-permute-start | bytes 12296 | tf_op jit(solution)/shard_map/ppermute | solution.py:306
  33.7 3.2 %collective-permute-start.2 = (f32[8,128]{1,0:T(8,128)S(1)}, f32[8,128]{1,0:T(8,128)S(1)}, u32[]{:S(2)}, u32[]{:S(2)}) collective-permute-start(f32[8,128]{1,0:T(8,128)S(1)} %get-tuple-element.49.st_right), channel_id=1, source_target_pairs={{0,1},{1,2},{2,3},{3,4},{4,5},{5,6},{6,7},{7,8},{8,9},{9,10},{10,1... | collective-permute-start | bytes 12296 | tf_op jit(solution)/shard_map/ppermute | solution.py:306
  36.9 0.0 collective-permute-done.8.in_left
  36.9 0.0 collective-permute-done.9.in_right
  36.9 2.8 %guest_forward.3 = (f32[2,8,512]{2,1,0:T(8,128)S(1)}, f32[2,128,512]{2,1,0:T(8,128)S(1)}, bf16[2,128,128]{2,1,0:T(8,128)(2,1)S(1)}, bf16[2,128,128]{2,1,0:T(8,12...) custom-call(s32[4,6]{1,0:T(4,128)S(1)} %copy-done.4, bf16[512,512]{1,0:T(8,128)(2,1)S(1)} %copy-done, ...), custom_call_target="tpu_custom_call" | custom-call | flops 2147483648 | bytes 4431968 | tf_op jit(solution)/shard_map/guest_forward/pallas_call | solution.py:282
  39.8 2.6 %collective-permute-start.11 = (f32[8,128]{1,0:T(8,128)S(1)}, f32[8,128]{1,0:T(8,128)S(1)}, u32[]{:S(2)}, u32[]{:S(2)}) collective-permute-start(f32[8,128]{1,0:T(8,128)S(1)} %get-tuple-element.66.st_left), channel_id=1, source_target_pairs={{1,0},{2,1},{3,2},{4,3},{5,4},{6,5},{7,6},{8,7},{9,8},{10,9},{11,1... | collective-permute-start | bytes 12296 | tf_op jit(solution)/shard_map/ppermute | solution.py:306
  42.4 5.0 %collective-permute-start.10 = (f32[8,128]{1,0:T(8,128)S(1)}, f32[8,128]{1,0:T(8,128)S(1)}, u32[]{:S(2)}, u32[]{:S(2)}) collective-permute-start(f32[8,128]{1,0:T(8,128)S(1)} %get-tuple-element.67.st_right), channel_id=1, source_target_pairs={{0,1},{1,2},{2,3},{3,4},{4,5},{5,6},{6,7},{7,8},{8,9},{9,10},{10,1... | collective-permute-start | bytes 12296 | tf_op jit(solution)/shard_map/ppermute | solution.py:306
  47.4 1.9 %collective-permute-start.12 = (bf16[2,128,128]{2,1,0:T(8,128)(2,1)S(1)}, bf16[2,128,128]{2,1,0:T(8,128)(2,1)S(1)}, u32[]{:S(2)}, u32[]{:S(2)}) collective-permute-start(bf16[2,128,128]{2,1,0:T(8,128)(2,1)S(1)} %get-tuple-element.69), channel_id=1, source_target_pairs={{0,1},{1,2},{2,3},{3,4},{4,5},{5,6},{6,7},{7,8},{8,9},{9,10},{10,1... | collective-permute-start | bytes 196616 | tf_op jit(solution)/shard_map/ppermute | solution.py:306
  49.4 0.0 collective-permute-done.3.got_right
  49.4 3.9 %collective-permute-start.13 = (bf16[2,128,128]{2,1,0:T(8,128)(2,1)S(1)}, bf16[2,128,128]{2,1,0:T(8,128)(2,1)S(1)}, u32[]{:S(2)}, u32[]{:S(2)}) collective-permute-start(bf16[2,128,128]{2,1,0:T(8,128)(2,1)S(1)} %get-tuple-element.70), channel_id=1, source_target_pairs={{1,0},{2,1},{3,2},{4,3},{5,4},{6,5},{7,6},{8,7},{9,8},{10,9},{11,1... | collective-permute-start | bytes 196616 | tf_op jit(solution)/shard_map/ppermute | solution.py:306
  53.3 0.0 collective-permute-done.2.got_left
  53.3 3.7 %collective-permute-start.4 = (bf16[2,128,128]{2,1,0:T(8,128)(2,1)S(1)}, bf16[2,128,128]{2,1,0:T(8,128)(2,1)S(1)}, u32[]{:S(2)}, u32[]{:S(2)}) collective-permute-start(bf16[2,128,128]{2,1,0:T(8,128)(2,1)S(1)} %get-tuple-element.51), channel_id=1, source_target_pairs={{0,1},{1,2},{2,3},{3,4},{4,5},{5,6},{6,7},{7,8},{8,9},{9,10},{10,1... | collective-permute-start | bytes 196616 | tf_op jit(solution)/shard_map/ppermute | solution.py:306
  57.0 2.9 %guest_backward.2 = (f32[2,8,512]{2,1,0:T(8,128)S(1)}, bf16[6,128,128]{2,1,0:T(8,128)(2,1)S(1)}, bf16[6,128,128]{2,1,0:T(8,128)(2,1)S(1)}, f32[2,512,128]{2,1,0:...) custom-call(s32[4,6]{1,0:T(4,128)S(1)} %copy-done.4, bf16[512,512]{1,0:T(8,128)(2,1)S(1)} %copy-done, ...), custom_call_target="tpu_custom_call" | custom-call | flops 2147483648 | bytes 4669536 | tf_op jit(solution)/shard_map/guest_backward/pallas_call | solution.py:282
  59.9 0.0 collective-permute-done.11.got_right
  59.9 2.1 %collective-permute-start.5 = (bf16[2,128,128]{2,1,0:T(8,128)(2,1)S(1)}, bf16[2,128,128]{2,1,0:T(8,128)(2,1)S(1)}, u32[]{:S(2)}, u32[]{:S(2)}) collective-permute-start(bf16[2,128,128]{2,1,0:T(8,128)(2,1)S(1)} %get-tuple-element.52), channel_id=1, source_target_pairs={{1,0},{2,1},{3,2},{4,3},{5,4},{6,5},{7,6},{8,7},{9,8},{10,9},{11,1... | collective-permute-start | bytes 196616 | tf_op jit(solution)/shard_map/ppermute | solution.py:306
  62.1 0.0 collective-permute-done.10.got_left
  62.1 5.7 %collective-permute-start.6 = (bf16[6,128,128]{2,1,0:T(8,128)(2,1)S(1)}, bf16[6,128,128]{2,1,0:T(8,128)(2,1)S(1)}, u32[]{:S(2)}, u32[]{:S(2)}) collective-permute-start(bf16[6,128,128]{2,1,0:T(8,128)(2,1)S(1)} %get-tuple-element.60), channel_id=1, source_target_pairs={{0,1},{1,2},{2,3},{3,4},{4,5},{5,6},{6,7},{7,8},{8,9},{9,10},{10,1... | collective-permute-start | bytes 589832 | tf_op jit(solution)/shard_map/ppermute | solution.py:306
  67.8 2.9 %guest_backward.3 = (f32[2,8,512]{2,1,0:T(8,128)S(1)}, bf16[6,128,128]{2,1,0:T(8,128)(2,1)S(1)}, bf16[6,128,128]{2,1,0:T(8,128)(2,1)S(1)}, f32[2,512,128]{2,1,0:...) custom-call(s32[4,6]{1,0:T(4,128)S(1)} %copy-done.4, bf16[512,512]{1,0:T(8,128)(2,1)S(1)} %copy-done, ...), custom_call_target="tpu_custom_call" | custom-call | flops 2147483648 | bytes 4669536 | tf_op jit(solution)/shard_map/guest_backward/pallas_call | solution.py:282
  70.7 0.0 collective-permute-done.4.o_left
  70.7 1.9 %collective-permute-start.7 = (bf16[6,128,128]{2,1,0:T(8,128)(2,1)S(1)}, bf16[6,128,128]{2,1,0:T(8,128)(2,1)S(1)}, u32[]{:S(2)}, u32[]{:S(2)}) collective-permute-start(bf16[6,128,128]{2,1,0:T(8,128)(2,1)S(1)} %get-tuple-element.61), channel_id=1, source_target_pairs={{1,0},{2,1},{3,2},{4,3},{5,4},{6,5},{7,6},{8,7},{9,8},{10,9},{11,1... | collective-permute-start | bytes 589832 | tf_op jit(solution)/shard_map/ppermute | solution.py:306
  72.6 0.0 collective-permute-done.5.o_right
  72.6 5.7 %collective-permute-start.14 = (bf16[6,128,128]{2,1,0:T(8,128)(2,1)S(1)}, bf16[6,128,128]{2,1,0:T(8,128)(2,1)S(1)}, u32[]{:S(2)}, u32[]{:S(2)}) collective-permute-start(bf16[6,128,128]{2,1,0:T(8,128)(2,1)S(1)} %get-tuple-element.78), channel_id=1, source_target_pairs={{0,1},{1,2},{2,3},{3,4},{4,5},{5,6},{6,7},{7,8},{8,9},{9,10},{10,1... | collective-permute-start | bytes 589832 | tf_op jit(solution)/shard_map/ppermute | solution.py:306
  78.4 2.4 %own_backward.2 = (bf16[512,256]{1,0:T(8,128)(2,1)S(1)}, f32[2,512,128]{2,1,0:T(8,128)S(1)}, f32[2,512,128]{2,1,0:T(8,128)S(1)}, f32[2,512,128]{2,1,0:T(8,128)S(1)}) custom-call(s32[4,6]{1,0:T(4,128)S(1)} %copy-done.4, bf16[512,512]{1,0:T(8,128)(2,1)S(1)} %copy-done, bf16[512,512]{1,0:T(8,128)(2,1)S(1)} %copy-done.1, bf16[512,512]{1,0:T(8,128)(2,1)S(1)} %copy-done.2, ...), custom_call_target="tpu_custom_call" | custom-call | flops 3221225472 | bytes 6234208 | tf_op jit(solution)/shard_map/own_backward/pallas_call | solution.py:282
  80.8 0.0 collective-permute-done.12.o_left
  80.8 1.9 %collective-permute-start.15 = (bf16[6,128,128]{2,1,0:T(8,128)(2,1)S(1)}, bf16[6,128,128]{2,1,0:T(8,128)(2,1)S(1)}, u32[]{:S(2)}, u32[]{:S(2)}) collective-permute-start(bf16[6,128,128]{2,1,0:T(8,128)(2,1)S(1)} %get-tuple-element.79), channel_id=1, source_target_pairs={{1,0},{2,1},{3,2},{4,3},{5,4},{6,5},{7,6},{8,7},{9,8},{10,9},{11,1... | collective-permute-start | bytes 589832 | tf_op jit(solution)/shard_map/ppermute | solution.py:306
  82.7 0.0 collective-permute-done.13.o_right
  82.7 2.4 %own_backward.3 = (bf16[512,256]{1,0:T(8,128)(2,1)S(1)}, f32[2,512,128]{2,1,0:T(8,128)S(1)}, f32[2,512,128]{2,1,0:T(8,128)S(1)}, f32[2,512,128]{2,1,0:T(8,128)S(1)}) custom-call(s32[4,6]{1,0:T(4,128)S(1)} %copy-done.4, bf16[512,512]{1,0:T(8,128)(2,1)S(1)} %copy-done, bf16[512,512]{1,0:T(8,128)(2,1)S(1)} %copy-done.1, bf16[512,512]{1,0:T(8,128)(2,1)S(1)} %copy-done.2, ...), custom_call_target="tpu_custom_call" | custom-call | flops 3221225472 | bytes 6234208 | tf_op jit(solution)/shard_map/own_backward/pallas_call | solution.py:282
  85.1 0.0 collective-permute-done.6.refs_4_
  85.1 0.0 collective-permute-done.7.refs_5_
  85.1 0.0 collective-permute-done.14.refs_10_
  85.1 5.0 %collective-permute-done.15.refs_11_ = bf16[6,128,128]{2,1,0:T(8,128)(2,1)S(1)} collective-permute-done((bf16[6,128,128]{2,1,0:T(8,128)(2,1)S(1)}, bf16[6,128,128]{2,1,0:T(8,128)(2,1)S(1)}, u32[]{:S(2)}, u32[]{:S(2)}) %collective-permute-start.15) | collective-permute-done | bytes 196640 | tf_op jit(solution)/shard_map/ppermute | solution.py:306
  90.1 2.3 %finish.1 = (bf16[512,512]{1,0:T(8,128)(2,1)}, bf16[512,512]{1,0:T(8,128)(2,1)}, bf16[512,512]{1,0:T(8,128)(2,1)}, bf16[512,512]{1,0:T(8,128)(2,1)}) custom-call(s32[4,6]{1,0:T(4,128)S(1)} %copy-done.4, bf16[512,256]{1,0:T(8,128)(2,1)S(1)} %get-tuple-element.56.refs_0_, f32[2,512,128]{2,1,0:T(8,128)S(1)} %get-tuple-element.57.refs_1_, ...), custom_call_target="tpu_custom_call" | custom-call | bytes 6553696 | tf_op jit(solution)/shard_map/finish/pallas_call | solution.py:282
Async XLA Ops:
  0.6 1.0 %copy-start = (bf16[512,512]{1,0:T(8,128)(2,1)S(1)}, bf16[512,512]{1,0:T(8,128)(2,1)}, u32[]{:S(2)}) copy-start(bf16[512,512]{1,0:T(8,128)(2,1)} %q.15) | copy-start | bytes 1572868
  1.7 1.0 %copy-start.1 = (bf16[512,512]{1,0:T(8,128)(2,1)S(1)}, bf16[512,512]{1,0:T(8,128)(2,1)}, u32[]{:S(2)}) copy-start(bf16[512,512]{1,0:T(8,128)(2,1)} %k.15) | copy-start | bytes 1572868
  2.7 1.0 %copy-start.2 = (bf16[512,512]{1,0:T(8,128)(2,1)S(1)}, bf16[512,512]{1,0:T(8,128)(2,1)}, u32[]{:S(2)}) copy-start(bf16[512,512]{1,0:T(8,128)(2,1)} %v.15) | copy-start | bytes 1572868
  3.8 1.0 %copy-start.3 = (bf16[512,512]{1,0:T(8,128)(2,1)S(1)}, bf16[512,512]{1,0:T(8,128)(2,1)}, u32[]{:S(2)}) copy-start(bf16[512,512]{1,0:T(8,128)(2,1)} %g.15) | copy-start | bytes 1572868
  4.8 0.7 copy-start.4
  6.3 18.1 %collective-permute-start = (bf16[8,128,128]{2,1,0:T(8,128)(2,1)S(1)}, bf16[8,128,128]{2,1,0:T(8,128)(2,1)S(1)}, u32[]{:S(2)}, u32[]{:S(2)}) collective-permute-start(bf16[8,128,128]{2,1,0:T(8,128)(2,1)S(1)} %get-tuple-element.42), channel_id=1, source_target_pairs={{0,1},{1,2},{2,3},{3,4},{4,5},{5,6},{6,7},{7,8},{8,9},{9,10},{10,1... | collective-permute-start | bytes 786440 | tf_op jit(solution)/shard_map/ppermute | solution.py:306
  9.7 16.8 %collective-permute-start.1 = (bf16[8,128,128]{2,1,0:T(8,128)(2,1)S(1)}, bf16[8,128,128]{2,1,0:T(8,128)(2,1)S(1)}, u32[]{:S(2)}, u32[]{:S(2)}) collective-permute-start(bf16[8,128,128]{2,1,0:T(8,128)(2,1)S(1)} %get-tuple-element.43), channel_id=1, source_target_pairs={{1,0},{2,1},{3,2},{4,3},{5,4},{6,5},{7,6},{8,7},{9,8},{10,9},{11,1... | collective-permute-start | bytes 786440 | tf_op jit(solution)/shard_map/ppermute | solution.py:306
  12.1 24.8 %collective-permute-start.8 = (bf16[8,128,128]{2,1,0:T(8,128)(2,1)S(1)}, bf16[8,128,128]{2,1,0:T(8,128)(2,1)S(1)}, u32[]{:S(2)}, u32[]{:S(2)}) collective-permute-start(bf16[8,128,128]{2,1,0:T(8,128)(2,1)S(1)} %get-tuple-element.62), channel_id=1, source_target_pairs={{0,1},{1,2},{2,3},{3,4},{4,5},{5,6},{6,7},{7,8},{8,9},{9,10},{10,1... | collective-permute-start | bytes 786440 | tf_op jit(solution)/shard_map/ppermute | solution.py:306
  17.3 19.6 %collective-permute-start.9 = (bf16[8,128,128]{2,1,0:T(8,128)(2,1)S(1)}, bf16[8,128,128]{2,1,0:T(8,128)(2,1)S(1)}, u32[]{:S(2)}, u32[]{:S(2)}) collective-permute-start(bf16[8,128,128]{2,1,0:T(8,128)(2,1)S(1)} %get-tuple-element.63), channel_id=1, source_target_pairs={{1,0},{2,1},{3,2},{4,3},{5,4},{6,5},{7,6},{8,7},{9,8},{10,9},{11,1... | collective-permute-start | bytes 786440 | tf_op jit(solution)/shard_map/ppermute | solution.py:306
  29.3 20.1 %collective-permute-start.3 = (f32[8,128]{1,0:T(8,128)S(1)}, f32[8,128]{1,0:T(8,128)S(1)}, u32[]{:S(2)}, u32[]{:S(2)}) collective-permute-start(f32[8,128]{1,0:T(8,128)S(1)} %get-tuple-element.48.st_left), channel_id=1, source_target_pairs={{1,0},{2,1},{3,2},{4,3},{5,4},{6,5},{7,6},{8,7},{9,8},{10,9},{11,1... | collective-permute-start | bytes 12296 | tf_op jit(solution)/shard_map/ppermute | solution.py:306
  33.7 19.7 %collective-permute-start.2 = (f32[8,128]{1,0:T(8,128)S(1)}, f32[8,128]{1,0:T(8,128)S(1)}, u32[]{:S(2)}, u32[]{:S(2)}) collective-permute-start(f32[8,128]{1,0:T(8,128)S(1)} %get-tuple-element.49.st_right), channel_id=1, source_target_pairs={{0,1},{1,2},{2,3},{3,4},{4,5},{5,6},{6,7},{7,8},{8,9},{9,10},{10,1... | collective-permute-start | bytes 12296 | tf_op jit(solution)/shard_map/ppermute | solution.py:306
  39.8 20.1 %collective-permute-start.11 = (f32[8,128]{1,0:T(8,128)S(1)}, f32[8,128]{1,0:T(8,128)S(1)}, u32[]{:S(2)}, u32[]{:S(2)}) collective-permute-start(f32[8,128]{1,0:T(8,128)S(1)} %get-tuple-element.66.st_left), channel_id=1, source_target_pairs={{1,0},{2,1},{3,2},{4,3},{5,4},{6,5},{7,6},{8,7},{9,8},{10,9},{11,1... | collective-permute-start | bytes 12296 | tf_op jit(solution)/shard_map/ppermute | solution.py:306
  42.4 19.7 %collective-permute-start.10 = (f32[8,128]{1,0:T(8,128)S(1)}, f32[8,128]{1,0:T(8,128)S(1)}, u32[]{:S(2)}, u32[]{:S(2)}) collective-permute-start(f32[8,128]{1,0:T(8,128)S(1)} %get-tuple-element.67.st_right), channel_id=1, source_target_pairs={{0,1},{1,2},{2,3},{3,4},{4,5},{5,6},{6,7},{7,8},{8,9},{9,10},{10,1... | collective-permute-start | bytes 12296 | tf_op jit(solution)/shard_map/ppermute | solution.py:306
  47.4 33.3 %collective-permute-start.12 = (bf16[2,128,128]{2,1,0:T(8,128)(2,1)S(1)}, bf16[2,128,128]{2,1,0:T(8,128)(2,1)S(1)}, u32[]{:S(2)}, u32[]{:S(2)}) collective-permute-start(bf16[2,128,128]{2,1,0:T(8,128)(2,1)S(1)} %get-tuple-element.69), channel_id=1, source_target_pairs={{0,1},{1,2},{2,3},{3,4},{4,5},{5,6},{6,7},{7,8},{8,9},{9,10},{10,1... | collective-permute-start | bytes 196616 | tf_op jit(solution)/shard_map/ppermute | solution.py:306
  49.4 33.3 %collective-permute-start.13 = (bf16[2,128,128]{2,1,0:T(8,128)(2,1)S(1)}, bf16[2,128,128]{2,1,0:T(8,128)(2,1)S(1)}, u32[]{:S(2)}, u32[]{:S(2)}) collective-permute-start(bf16[2,128,128]{2,1,0:T(8,128)(2,1)S(1)} %get-tuple-element.70), channel_id=1, source_target_pairs={{1,0},{2,1},{3,2},{4,3},{5,4},{6,5},{7,6},{8,7},{9,8},{10,9},{11,1... | collective-permute-start | bytes 196616 | tf_op jit(solution)/shard_map/ppermute | solution.py:306
  53.3 17.4 %collective-permute-start.4 = (bf16[2,128,128]{2,1,0:T(8,128)(2,1)S(1)}, bf16[2,128,128]{2,1,0:T(8,128)(2,1)S(1)}, u32[]{:S(2)}, u32[]{:S(2)}) collective-permute-start(bf16[2,128,128]{2,1,0:T(8,128)(2,1)S(1)} %get-tuple-element.51), channel_id=1, source_target_pairs={{0,1},{1,2},{2,3},{3,4},{4,5},{5,6},{6,7},{7,8},{8,9},{9,10},{10,1... | collective-permute-start | bytes 196616 | tf_op jit(solution)/shard_map/ppermute | solution.py:306
  59.9 12.7 %collective-permute-start.5 = (bf16[2,128,128]{2,1,0:T(8,128)(2,1)S(1)}, bf16[2,128,128]{2,1,0:T(8,128)(2,1)S(1)}, u32[]{:S(2)}, u32[]{:S(2)}) collective-permute-start(bf16[2,128,128]{2,1,0:T(8,128)(2,1)S(1)} %get-tuple-element.52), channel_id=1, source_target_pairs={{1,0},{2,1},{3,2},{4,3},{5,4},{6,5},{7,6},{8,7},{9,8},{10,9},{11,1... | collective-permute-start | bytes 196616 | tf_op jit(solution)/shard_map/ppermute | solution.py:306
  62.1 23.0 %collective-permute-start.6 = (bf16[6,128,128]{2,1,0:T(8,128)(2,1)S(1)}, bf16[6,128,128]{2,1,0:T(8,128)(2,1)S(1)}, u32[]{:S(2)}, u32[]{:S(2)}) collective-permute-start(bf16[6,128,128]{2,1,0:T(8,128)(2,1)S(1)} %get-tuple-element.60), channel_id=1, source_target_pairs={{0,1},{1,2},{2,3},{3,4},{4,5},{5,6},{6,7},{7,8},{8,9},{9,10},{10,1... | collective-permute-start | bytes 589832 | tf_op jit(solution)/shard_map/ppermute | solution.py:306
  70.7 14.4 %collective-permute-start.7 = (bf16[6,128,128]{2,1,0:T(8,128)(2,1)S(1)}, bf16[6,128,128]{2,1,0:T(8,128)(2,1)S(1)}, u32[]{:S(2)}, u32[]{:S(2)}) collective-permute-start(bf16[6,128,128]{2,1,0:T(8,128)(2,1)S(1)} %get-tuple-element.61), channel_id=1, source_target_pairs={{1,0},{2,1},{3,2},{4,3},{5,4},{6,5},{7,6},{8,7},{9,8},{10,9},{11,1... | collective-permute-start | bytes 589832 | tf_op jit(solution)/shard_map/ppermute | solution.py:306
  72.6 12.5 %collective-permute-start.14 = (bf16[6,128,128]{2,1,0:T(8,128)(2,1)S(1)}, bf16[6,128,128]{2,1,0:T(8,128)(2,1)S(1)}, u32[]{:S(2)}, u32[]{:S(2)}) collective-permute-start(bf16[6,128,128]{2,1,0:T(8,128)(2,1)S(1)} %get-tuple-element.78), channel_id=1, source_target_pairs={{0,1},{1,2},{2,3},{3,4},{4,5},{5,6},{6,7},{7,8},{8,9},{9,10},{10,1... | collective-permute-start | bytes 589832 | tf_op jit(solution)/shard_map/ppermute | solution.py:306
  80.8 9.4 %collective-permute-start.15 = (bf16[6,128,128]{2,1,0:T(8,128)(2,1)S(1)}, bf16[6,128,128]{2,1,0:T(8,128)(2,1)S(1)}, u32[]{:S(2)}, u32[]{:S(2)}) collective-permute-start(bf16[6,128,128]{2,1,0:T(8,128)(2,1)S(1)} %get-tuple-element.79), channel_id=1, source_target_pairs={{1,0},{2,1},{3,2},{4,3},{5,4},{6,5},{7,6},{8,7},{9,8},{10,9},{11,1... | collective-permute-start | bytes 589832 | tf_op jit(solution)/shard_map/ppermute | solution.py:306

commit v2 on v1

v2 whole, which is shorter than its diff:
```python
import functools
import math

import jax
import jax.numpy as jnp
from jax import lax
from jax.experimental import pallas as pl
from jax.experimental.pallas import tpu as pltpu
from jax.sharding import PartitionSpec as P

HEADS = 4
HD = 128
BLOCK = 128
KB = 6
SCALE = HD**-0.5
SCALE2 = SCALE * math.log2(math.e)
NEG = -1e30
F32 = jnp.float32
BF16 = jnp.bfloat16


def dot(a, b, ca, cb):
    return lax.dot_general(a, b, (((ca,), (cb,)), ((), ())), preferred_element_type=F32)


def bias_of(cond):
    return jnp.where(cond, 0.0, NEG).astype(F32)


class Place:
    def __init__(self, lists, nb):
        self.nb = nb
        position = lax.axis_index("seq")
        base = position * nb
        self.lo = lo = [lists[a, 0] - base for a in range(nb)]
        self.hi = hi = []
        for a in range(nb):
            top = lists[a, 0]
            for e in range(1, KB):
                top = jnp.maximum(top, lists[a, e])
            hi.append(top - base)
        end = nb - 1
        cut_right = ((lo[end - 1] != lo[end]) | (hi[end - 1] != hi[end])) & (hi[end - 1] >= nb)
        cut_left = ((lo[0] != lo[1]) | (hi[0] != hi[1])) & (lo[1] <= -1)
        r, l = cut_right.astype(jnp.int32), cut_left.astype(jnp.int32)
        odd = lax.rem(position, 2)
        self.partners = []
        for right in (1 - odd, odd):
            is_right = right == 1

            def pick(to_right, to_left):
                return jnp.where(is_right, to_right, to_left)

            partner = Partner()
            partner.there = pick(position < lax.axis_size("seq") - 1, position > 0)
            partner.sent = [(pick(0, 1 - l), pick(end - 1 + r, 0)), (pick(r, 1), pick(end, 1 - l))]
            guests = [(pick(1 - r, 0), pick(nb, -2 + l)), (pick(1, l), pick(nb + 1 - r, -1))]
            first = pick(nb - 3, 0)
            partner.span = pl.ds(pl.multiple_of(first * BLOCK, BLOCK), 3 * BLOCK)
            cut = pick(r, l) == 1
            partner.guests = []
            for h, number in guests:
                near, free = [], []
                for b in range(3):
                    low, high = pick(lo[nb - 3 + b], lo[b]), pick(hi[nb - 3 + b], hi[b])
                    near.append((low <= number) & (number <= high))
                    gone = cut & (is_right if b == 2 else jnp.logical_not(is_right)) if b != 1 else None
                    free.append(near[b] if b == 1 else near[b] & jnp.logical_not(gone))
                partner.guests.append((h, [bias_of(c) for c in near], [bias_of(c) for c in free]))
            self.partners.append(partner)

    def biases(self):
        return [
            [bias_of((self.lo[a] <= b) & (b <= self.hi[a])) for b in range(self.nb)] for a in range(self.nb)
        ]


class Partner:
    pass


def lane(h, half):
    start = (h + 2 * half) * HD
    return pl.ds(start if isinstance(start, int) else pl.multiple_of(start, HD), HD)


def rows_of(b):
    start = b * BLOCK
    return pl.ds(start if isinstance(start, int) else pl.multiple_of(start, BLOCK), BLOCK)


def down(s, biases):
    return jnp.concatenate(
        [s[b * BLOCK : (b + 1) * BLOCK] * SCALE2 + bias for b, bias in enumerate(biases)], axis=0
    )


def across(s, biases):
    return jnp.concatenate(
        [s[:, b * BLOCK : (b + 1) * BLOCK] * SCALE2 + bias for b, bias in enumerate(biases)], axis=1
    )


def total_of(x):
    return jnp.sum(x, axis=0, keepdims=True)


def pack_kernel(nb, half, lists, q, k, v, g, out_a, out_b, sems):
    at = Place(lists, nb)
    copies = []
    for out, partner in zip((out_a, out_b), at.partners):
        for slot, (h, b) in enumerate(partner.sent):
            for i, array in enumerate((q, k, v, g)):
                copy = pltpu.make_async_copy(
                    array.at[rows_of(b), lane(h, half)], out.at[2 * i + slot], sems.at[len(copies)]
                )
                copy.start()
                copies.append(copy)
    for copy in copies:
        copy.wait()


def own_forward_kernel(nb, lists, q, k, v, g, stats, ot):
    at = Place(lists, nb)
    biases = at.biases()
    for h in range(HEADS):
        cols = lane(h, 0)
        kh, vh = k[:, cols], v[:, cols]
        for a in range(nb):
            rows = rows_of(a)
            s = down(dot(kh, q[rows, cols], 1, 1), biases[a])
            m = jnp.max(s, axis=0, keepdims=True)
            p = jnp.exp2(s - m)
            dp = dot(vh, g[rows, cols], 1, 1)
            stats[h, 0:1, rows] = m
            stats[h, 1:2, rows] = total_of(p)
            stats[h, 2:3, rows] = total_of(p * dp)
            ot[h, :, rows] = dot(vh, p.astype(BF16), 0, 0)


def guest_kernel(nb, half, lists, q, k, v, g, in_a, in_b, stats0, ot0, stats, ot, out_a, out_b, st_a, st_b):
    at = Place(lists, nb)
    for h in range(2):
        stats[h] = stats0[2 * half + h]
        ot[h] = ot0[2 * half + h]
    kept = []
    for partner, message, out, st in zip(at.partners, (in_a, in_b), (out_a, out_b), (st_a, st_b)):
        span = partner.span
        for slot, (h, near, free) in enumerate(partner.guests):
            qg, kg, vg, gg = (message[2 * i + slot] for i in range(4))
            cols = lane(h, half)
            qh, kh, vh, gh = (array[span, cols] for array in (q, k, v, g))
            s = down(dot(kh, qg, 1, 1), near)
            m = jnp.max(s, axis=0, keepdims=True)
            p = jnp.exp2(s - m)
            dp = dot(vh, gg, 1, 1)
            total = total_of(p)
            p = p * (1.0 / total)
            delta = total_of(p * dp)
            st[2 * slot : 2 * slot + 1, :] = m + jnp.log2(total)
            st[2 * slot + 1 : 2 * slot + 2, :] = delta
            weights = p.astype(BF16)
            out[slot] = dot(vh, weights, 0, 0).astype(BF16)
            out[2 + slot] = dot(kh, (p * (dp - delta)).astype(BF16), 0, 0).astype(BF16)
            out[4 + slot] = dot(kh, weights, 0, 0).astype(BF16)
            s = across(dot(kg, qh, 1, 1), free)
            old = stats[h, 0:1, span]
            m = jnp.maximum(old, jnp.max(s, axis=0, keepdims=True))
            shrink = jnp.exp2(old - m)
            p = jnp.exp2(s - m)
            dp = dot(vg, gh, 1, 1)
            stats[h, 0:1, span] = m
            stats[h, 1:2, span] = stats[h, 1:2, span] * shrink + total_of(p)
            stats[h, 2:3, span] = stats[h, 2:3, span] * shrink + total_of(p * dp)
            ot[h, :, span] = ot[h, :, span] * shrink + dot(vg, p.astype(BF16), 0, 0)
            kept.append((s, dp, qh, gh))
    for h in range(2):
        total = stats[h, 1:2, :]
        stats[h, 3:4, :] = stats[h, 0:1, :] + jnp.log2(total)
        stats[h, 4:5, :] = stats[h, 2:3, :] / total
    for partner, out, st in zip(at.partners, (out_a, out_b), (st_a, st_b)):
        for slot, (h, near, free) in enumerate(partner.guests):
            s, dp, qh, gh = kept.pop(0)
            p = jnp.exp2(s - stats[h, 3:4, partner.span])
            ds = (p * (dp - stats[h, 4:5, partner.span])).astype(BF16)
            out[6 + slot] = dot(ds, qh, 1, 0).astype(BF16)
            out[8 + slot] = dot(p.astype(BF16), gh, 1, 0).astype(BF16)
        for slot, (h, b) in enumerate(partner.sent):
            st[4 + 2 * slot : 5 + 2 * slot, :] = stats[h, 3:4, rows_of(b)]
            st[5 + 2 * slot : 6 + 2 * slot, :] = stats[h, 4:5, rows_of(b)]


def merged(l1, d1, l2, d2):
    m = jnp.maximum(l1, l2)
    w1, w2 = jnp.exp2(l1 - m), jnp.exp2(l2 - m)
    total = w1 + w2
    return m + jnp.log2(total), (w1 * d1 + w2 * d2) / total


def backward_kernel(
    nb, half, lists, q, k, v, g, in_a, in_b, stats, ot, st_a, st_b, got_a, got_b,
    att, aq, ak, av, mix_a, mix_b, fin, ps, dss,
):
    at = Place(lists, nb)
    biases = at.biases()
    fin[:, 0:2, :] = stats[:, 3:5, :]
    for partner, got, mix in zip(at.partners, (got_a, got_b), (mix_a, mix_b)):
        gone = bias_of(partner.there)
        for slot, (h, b) in enumerate(partner.sent):
            rows = rows_of(b)
            part = got[2 * slot : 2 * slot + 1, :] + gone
            part_delta = got[2 * slot + 1 : 2 * slot + 2, :]
            total, delta = merged(fin[h, 0:1, rows], fin[h, 1:2, rows], part, part_delta)
            fin[h, 0:1, rows] = total
            fin[h, 1:2, rows] = delta
            mix[2 * slot : 2 * slot + 1, :] = jnp.exp2(part - total)
            mix[2 * slot + 1 : 2 * slot + 2, :] = delta - part_delta
    for h in range(2):
        cols = lane(h, half)
        kh, vh = k[:, cols], v[:, cols]
        for a in range(nb):
            rows = rows_of(a)
            own = ot[h, :, rows] * jnp.exp2(stats[h, 0:1, rows] - fin[h, 0:1, rows])
            att[h, rows, :] = own.T
            s = down(dot(kh, q[rows, cols], 1, 1), biases[a])
            p = jnp.exp2(s - fin[h, 0:1, rows])
            ps[:, rows] = p.astype(BF16)
            dss[:, rows] = (p * (dot(vh, g[rows, cols], 1, 1) - fin[h, 1:2, rows])).astype(BF16)
        av[h] = dot(ps[...], g[:, cols], 1, 0)
        ak[h] = dot(dss[...], q[:, cols], 1, 0)
        aq[h] = dot(dss[...], kh, 0, 0)
    for partner, message, mine, got in zip(at.partners, (in_a, in_b), (st_a, st_b), (got_a, got_b)):
        span = partner.span
        for slot, (h, near, free) in enumerate(partner.guests):
            qg, kg, vg, gg = (message[2 * i + slot] for i in range(4))
            cols = lane(h, half)
            qh, kh, vh, gh = (array[span, cols] for array in (q, k, v, g))
            total, delta = merged(
                mine[2 * slot : 2 * slot + 1, :],
                mine[2 * slot + 1 : 2 * slot + 2, :],
                got[4 + 2 * slot : 5 + 2 * slot, :],
                got[5 + 2 * slot : 6 + 2 * slot, :],
            )
            p = jnp.exp2(down(dot(kh, qg, 1, 1), near) - total)
            ds = (p * (dot(vh, gg, 1, 1) - delta)).astype(BF16)
            ak[h, span, :] += dot(ds, qg, 1, 0)
            av[h, span, :] += dot(p.astype(BF16), gg, 1, 0)
            p = jnp.exp2(across(dot(kg, qh, 1, 1), free) - fin[h, 0:1, span])
            ds = (p * (dot(vg, gh, 1, 1) - fin[h, 1:2, span])).astype(BF16)
            aq[h, span, :] += dot(ds, kg, 0, 0)


def finish_kernel(nb, lists, *refs):
    at = Place(lists, nb)
    halves = (refs[:8], refs[8:16])
    att_out, q_out, k_out, v_out, so, sq, sk, sv = refs[16:]
    for half, (att, aq, ak, av, mix_a, mix_b, back_a, back_b) in enumerate(halves):
        for total, part in ((so, att), (sq, aq), (sk, ak), (sv, av)):
            total[...] = part[...]
        for partner, mix, back in zip(at.partners, (mix_a, mix_b), (back_a, back_b)):
            for slot, (h, b) in enumerate(partner.sent):
                rows = rows_of(b)
                o, u, w, dk, dv = (back[2 * i + slot].astype(F32) for i in range(5))
                weight = mix[2 * slot : 2 * slot + 1, :]
                so[h, rows, :] += (o * weight).T
                sq[h, rows, :] += ((u - w * mix[2 * slot + 1 : 2 * slot + 2, :]) * weight).T
                sk[h, rows, :] += dk
                sv[h, rows, :] += dv
        for h in range(2):
            cols = lane(h, half)
            att_out[:, cols] = so[h].astype(BF16)
            q_out[:, cols] = (sq[h] * SCALE).astype(BF16)
            k_out[:, cols] = (sk[h] * SCALE).astype(BF16)
            v_out[:, cols] = sv[h].astype(BF16)


def call(kernel, name, outs, args, scratch=(), flops=0, space=pltpu.VMEM):
    moved = sum(math.prod(s.shape) * s.dtype.itemsize for s in (*outs, *args))
    vmem = pl.BlockSpec(memory_space=pltpu.VMEM)
    return pl.pallas_call(
        kernel,
        out_shape=tuple(outs),
        in_specs=[pl.BlockSpec(memory_space=pltpu.SMEM)]
        + [pl.BlockSpec(memory_space=space)] * (len(args) - 1),
        out_specs=tuple([vmem] * len(outs)),
        scratch_shapes=scratch,
        cost_estimate=pl.CostEstimate(flops=flops, bytes_accessed=moved, transcendentals=0),
        compiler_params=pltpu.CompilerParams(vmem_limit_bytes=24 << 20),
        name=name,
    )(*args)


def sds(shape, dtype):
    return jax.ShapeDtypeStruct(shape, dtype)


def body(q, k, v, g, lists):
    rows, width = q.shape
    nb = rows // BLOCK
    count = lax.axis_size("seq")

    def pairs(start):
        return [(i, j) for a in range(start, count - 1, 2) for i, j in ((a, a + 1), (a + 1, a))]

    def swap(to_a, to_b):
        return lax.ppermute(to_a, "seq", pairs(0)), lax.ppermute(to_b, "seq", pairs(1))

    arrays = (lists, q, k, v, g)
    tile8, tile10 = sds((8, BLOCK, HD), BF16), sds((10, BLOCK, HD), BF16)
    guests = [
        swap(*call(
            functools.partial(pack_kernel, nb, half), "pack", [tile8] * 2, arrays,
            scratch=(pltpu.SemaphoreType.DMA((16,)),), space=pltpu.HBM,
        ))
        for half in range(2)
    ]
    stats0, ot0 = call(
        functools.partial(own_forward_kernel, nb), "own_forward",
        [sds((HEADS, 8, rows), F32), sds((HEADS, HD, rows), F32)], arrays, flops=3 << 30,
    )
    st, acc = sds((8, HD), F32), sds((2, rows, HD), F32)
    forward, backs = [], []
    for half in range(2):
        *kept, out_a, out_b, st_a, st_b = call(
            functools.partial(guest_kernel, nb, half), "guest",
            [sds((2, 8, rows), F32), sds((2, HD, rows), F32), tile10, tile10, st, st],
            (*arrays, *guests[half], stats0, ot0), flops=2 << 30,
        )
        backs.append(swap(out_a, out_b))
        forward.append((*kept, st_a, st_b))
    got = swap(*(jnp.stack([forward[0][i], forward[1][i]]) for i in (2, 3)))
    pieces = []
    for half in range(2):
        outs = call(
            functools.partial(backward_kernel, nb, half), "backward", [acc] * 4 + [st] * 2,
            (*arrays, *guests[half], *forward[half], got[0][half], got[1][half]),
            scratch=(
                pltpu.VMEM((2, 8, rows), F32), pltpu.VMEM((rows, rows), BF16), pltpu.VMEM((rows, rows), BF16),
            ), flops=3 << 30,
        )
        pieces += [*outs, *backs[half]]
    return call(
        functools.partial(finish_kernel, nb), "finish", [sds((rows, width), BF16)] * 4, (lists, *pieces),
        scratch=tuple(pltpu.VMEM((2, rows, HD), F32) for _ in range(4)),
    )


def solution(mesh):
    spec = P(("dp", "seq"), None)
    return jax.shard_map(
        body, mesh=mesh, in_specs=(spec,) * 5, out_specs=(spec,) * 4, check_vma=False
    )
```

time: 93.2 us -> 74.1 us (0.80)
  the two profiles are of different devices: /device:TPU:14 before, /device:TPU:18 now
where the time goes in v2:
time: 74.1 us; the launch traced here: 73.7 us
  Pallas kernels  24.9 us (34%)
  starting transfers between devices  22.5 us (30%)
  waiting for transfers between devices  20.7 us (28%)
  local copies, waits for them, and re-layouts  4.85 us (7%)
  between operations  0.8 us (1%)
    pallas_call x8, Pallas kernels, call(): pl.pallas_call(kernel, out_shape=tuple(outs), in_specs=[pl.BlockSpec(memo...  24.9 us
    ppermute x5, starting transfers between devices, swap(): lax.ppermute(to_b, 'seq', pairs(1))  19.3 us
    ppermute x5, waiting for transfers between devices, swap(): lax.ppermute(to_a, 'seq', pairs(0))  16.8 us
    unnamed x10, local copies, waits for them, and re-layouts  4.84 us
    ppermute x5, waiting for transfers between devices, swap(): lax.ppermute(to_b, 'seq', pairs(1))  3.87 us
    ppermute x5, starting transfers between devices, swap(): lax.ppermute(to_a, 'seq', pairs(0))  3.17 us
  transfers between devices with their start and end apart: 10, of which 6 were waited for; matrix products, arithmetic and copies ran while one was open for 0% of the time, Pallas kernels for 24%

profile of v2, /device:TPU:18, one launch (start us, length us, event | category | flops | bytes accessed | tf_op | source)
XLA Modules:
  0.0 73.7 jit_solution(17686789654727702288)
XLA Ops:
  0.6 0.0 copy-start
  0.6 1.0 %copy-done = bf16[512,512]{1,0:T(8,128)(2,1)S(1)} copy-done((bf16[512,512]{1,0:T(8,128)(2,1)S(1)}, bf16[512,512]{1,0:T(8,128)(2,1)}, u32[]{:S(2)}) %copy-start) | copy-done | bytes 524312
  1.7 0.0 copy-start.1
  1.7 1.0 %copy-done.1 = bf16[512,512]{1,0:T(8,128)(2,1)S(1)} copy-done((bf16[512,512]{1,0:T(8,128)(2,1)S(1)}, bf16[512,512]{1,0:T(8,128)(2,1)}, u32[]{:S(2)}) %copy-start.1) | copy-done | bytes 524312
  2.7 0.0 copy-start.2
  2.7 1.0 %copy-done.2 = bf16[512,512]{1,0:T(8,128)(2,1)S(1)} copy-done((bf16[512,512]{1,0:T(8,128)(2,1)S(1)}, bf16[512,512]{1,0:T(8,128)(2,1)}, u32[]{:S(2)}) %copy-start.2) | copy-done | bytes 524312
  3.8 0.0 copy-start.3
  3.8 1.0 %copy-done.3 = bf16[512,512]{1,0:T(8,128)(2,1)S(1)} copy-done((bf16[512,512]{1,0:T(8,128)(2,1)S(1)}, bf16[512,512]{1,0:T(8,128)(2,1)}, u32[]{:S(2)}) %copy-start.3) | copy-done | bytes 524312
  4.8 0.0 copy-start.4
  4.8 0.7 copy-done.4
  5.5 0.9 %pack.3 = (bf16[8,128,128]{2,1,0:T(8,128)(2,1)S(1)}, bf16[8,128,128]{2,1,0:T(8,128)(2,1)S(1)}) custom-call(s32[4,6]{1,0:T(4,128)S(1)} %copy-done.4, bf16[512,512]{1,0:T(8,128)(2,1)S(1)} %copy-done, bf16[512,512]{1,0:T(8,128)(2,1)S(1)} %copy-done.1, bf16[512,512]{1,0:T(8,128)(2,1)S(1)} %copy-done.2, bf16[512,512]{1,0:T(8,128)(2,1)S(1)} %copy-done.3), custom_call_target="tpu_custom_call" | custom-call | bytes 2621536 | tf_op jit(solution)/shard_map/pack/pallas_call | solution.py:280
  6.4 0.6 collective-permute-start.2
  7.0 4.3 %collective-permute-start.3 = (bf16[8,128,128]{2,1,0:T(8,128)(2,1)S(1)}, bf16[8,128,128]{2,1,0:T(8,128)(2,1)S(1)}, u32[]{:S(2)}, u32[]{:S(2)}) collective-permute-start(bf16[8,128,128]{2,1,0:T(8,128)(2,1)S(1)} %get-tuple-element.43), channel_id=1, source_target_pairs={{1,2},{2,1},{3,4},{4,3},{5,6},{6,5},{7,8},{8,7},{9,10},{10,9},{11,... | collective-permute-start | bytes 786440 | tf_op jit(solution)/shard_map/ppermute | solution.py:306
  11.3 0.9 %pack.2 = (bf16[8,128,128]{2,1,0:T(8,128)(2,1)S(1)}, bf16[8,128,128]{2,1,0:T(8,128)(2,1)S(1)}) custom-call(s32[4,6]{1,0:T(4,128)S(1)} %copy-done.4, bf16[512,512]{1,0:T(8,128)(2,1)S(1)} %copy-done, bf16[512,512]{1,0:T(8,128)(2,1)S(1)} %copy-done.1, bf16[512,512]{1,0:T(8,128)(2,1)S(1)} %copy-done.2, bf16[512,512]{1,0:T(8,128)(2,1)S(1)} %copy-done.3), custom_call_target="tpu_custom_call" | custom-call | bytes 2621536 | tf_op jit(solution)/shard_map/pack/pallas_call | solution.py:280
  12.2 0.5 collective-permute-start
  12.7 4.5 %collective-permute-start.1 = (bf16[8,128,128]{2,1,0:T(8,128)(2,1)S(1)}, bf16[8,128,128]{2,1,0:T(8,128)(2,1)S(1)}, u32[]{:S(2)}, u32[]{:S(2)}) collective-permute-start(bf16[8,128,128]{2,1,0:T(8,128)(2,1)S(1)} %get-tuple-element.35), channel_id=1, source_target_pairs={{1,2},{2,1},{3,4},{4,3},{5,6},{6,5},{7,8},{8,7},{9,10},{10,9},{11,... | collective-permute-start | bytes 786440 | tf_op jit(solution)/shard_map/ppermute | solution.py:306
  17.2 5.1 %own_forward.1 = (f32[4,8,512]{2,1,0:T(8,128)S(1)}, f32[4,128,512]{2,1,0:T(8,128)S(1)}) custom-call(s32[4,6]{1,0:T(4,128)S(1)} %copy-done.4, bf16[512,512]{1,0:T(8,128)(2,1)S(1)} %copy-done, bf16[512,512]{1,0:T(8,128)(2,1)S(1)} %copy-done.1, bf16[512,512]{1,0:T(8,128)(2,1)S(1)} %copy-done.2, bf16[512,512]{1,0:T(8,128)(2,1)S(1)} %copy-done.3), custom_call_target="tpu_custom_call" | custom-call | flops 3221225472 | bytes 3211360 | tf_op jit(solution)/shard_map/own_forward/pallas_call | solution.py:280
  22.3 4.6 %collective-permute-done.2.in_a = bf16[8,128,128]{2,1,0:T(8,128)(2,1)S(1)} collective-permute-done((bf16[8,128,128]{2,1,0:T(8,128)(2,1)S(1)}, bf16[8,128,128]{2,1,0:T(8,128)(2,1)S(1)}, u32[]{:S(2)}, u32[]{:S(2)}) %collective-permute-start.2) | collective-permute-done | bytes 262176 | tf_op jit(solution)/shard_map/ppermute | solution.py:306
  26.9 0.0 collective-permute-done.3.in_b
  26.9 3.7 %guest.3 = (f32[2,8,512]{2,1,0:T(8,128)S(1)}, f32[2,128,512]{2,1,0:T(8,128)S(1)}, bf16[10,128,128]{2,1,0:T(8,128)(2,1)S(1)}, bf16[10,128,128]{2,1,0:T(8,128)(2,1...) custom-call(s32[4,6]{1,0:T(4,128)S(1)} %copy-done.4, bf16[512,512]{1,0:T(8,128)(2,1)S(1)} %copy-done, ...), custom_call_target="tpu_custom_call" | custom-call | flops 2147483648 | bytes 4956256 | tf_op jit(solution)/shard_map/guest/pallas_call | solution.py:280
  30.6 0.8 %collective-permute-done.in_a = bf16[8,128,128]{2,1,0:T(8,128)(2,1)S(1)} collective-permute-done((bf16[8,128,128]{2,1,0:T(8,128)(2,1)S(1)}, bf16[8,128,128]{2,1,0:T(8,128)(2,1)S(1)}, u32[]{:S(2)}, u32[]{:S(2)}) %collective-permute-start) | collective-permute-done | bytes 262176 | tf_op jit(solution)/shard_map/ppermute | solution.py:306
  31.3 1.0 %collective-permute-done.1.in_b = bf16[8,128,128]{2,1,0:T(8,128)(2,1)S(1)} collective-permute-done((bf16[8,128,128]{2,1,0:T(8,128)(2,1)S(1)}, bf16[8,128,128]{2,1,0:T(8,128)(2,1)S(1)}, u32[]{:S(2)}, u32[]{:S(2)}) %collective-permute-start.1) | collective-permute-done | bytes 262176 | tf_op jit(solution)/shard_map/ppermute | solution.py:306
  32.3 3.8 %guest.2 = (f32[2,8,512]{2,1,0:T(8,128)S(1)}, f32[2,128,512]{2,1,0:T(8,128)S(1)}, bf16[10,128,128]{2,1,0:T(8,128)(2,1)S(1)}, bf16[10,128,128]{2,1,0:T(8,128)(2,1...) custom-call(s32[4,6]{1,0:T(4,128)S(1)} %copy-done.4, bf16[512,512]{1,0:T(8,128)(2,1)S(1)} %copy-done, ...), custom_call_target="tpu_custom_call" | custom-call | flops 2147483648 | bytes 4956256 | tf_op jit(solution)/shard_map/guest/pallas_call | solution.py:280
  36.1 0.1 collective-permute-start.4
  36.2 2.5 %collective-permute-start.5 = (f32[2,8,128]{2,1,0:T(8,128)S(1)}, f32[2,8,128]{2,1,0:T(8,128)S(1)}, u32[]{:S(2)}, u32[]{:S(2)}) collective-permute-start(f32[2,8,128]{2,1,0:T(8,128)S(1)} %pad_maximum_fusion.1), channel_id=1, source_target_pairs={{1,2},{2,1},{3,4},{4,3},{5,6},{6,5},{7,8},{8,7},{9,10},{10,9},{11,... | collective-permute-start | bytes 24584 | tf_op jit(solution)/shard_map/ppermute | solution.py:306
  38.6 1.9 %collective-permute-start.6 = (bf16[10,128,128]{2,1,0:T(8,128)(2,1)S(1)}, bf16[10,128,128]{2,1,0:T(8,128)(2,1)S(1)}, u32[]{:S(2)}, u32[]{:S(2)}) collective-permute-start(bf16[10,128,128]{2,1,0:T(8,128)(2,1)S(1)} %get-tuple-element.52), channel_id=1, source_target_pairs={{0,1},{1,0},{2,3},{3,2},{4,5},{5,4},{6,7},{7,6},{8,9},{9,8},{10,11... | collective-permute-start | bytes 983048 | tf_op jit(solution)/shard_map/ppermute | solution.py:306
  40.6 5.4 %collective-permute-start.7 = (bf16[10,128,128]{2,1,0:T(8,128)(2,1)S(1)}, bf16[10,128,128]{2,1,0:T(8,128)(2,1)S(1)}, u32[]{:S(2)}, u32[]{:S(2)}) collective-permute-start(bf16[10,128,128]{2,1,0:T(8,128)(2,1)S(1)} %get-tuple-element.53), channel_id=1, source_target_pairs={{1,2},{2,1},{3,4},{4,3},{5,6},{6,5},{7,8},{8,7},{9,10},{10,9},{11,... | collective-permute-start | bytes 983048 | tf_op jit(solution)/shard_map/ppermute | solution.py:306
  46.0 0.1 collective-permute-start.8
  46.1 0.0 collective-permute-done.4
  46.1 2.6 %collective-permute-start.9 = (bf16[10,128,128]{2,1,0:T(8,128)(2,1)S(1)}, bf16[10,128,128]{2,1,0:T(8,128)(2,1)S(1)}, u32[]{:S(2)}, u32[]{:S(2)}) collective-permute-start(bf16[10,128,128]{2,1,0:T(8,128)(2,1)S(1)} %get-tuple-element.63), channel_id=1, source_target_pairs={{1,2},{2,1},{3,4},{4,3},{5,6},{6,5},{7,8},{8,7},{9,10},{10,9},{11,... | collective-permute-start | bytes 983048 | tf_op jit(solution)/shard_map/ppermute | solution.py:306
  48.7 0.0 collective-permute-done.5
  48.7 4.0 %backward.3 = (f32[2,512,128]{2,1,0:T(8,128)S(1)}, f32[2,512,128]{2,1,0:T(8,128)S(1)}, f32[2,512,128]{2,1,0:T(8,128)S(1)}, f32[2,512,128]{2,1,0:T(8,128)S(1)}, f...) custom-call(s32[4,6]{1,0:T(4,128)S(1)} %copy-done.4, bf16[512,512]{1,0:T(8,128)(2,1)S(1)} %copy-done, ...), custom_call_target="tpu_custom_call" | custom-call | flops 3221225472 | bytes 5300320 | tf_op jit(solution)/shard_map/backward/pallas_call | solution.py:280
  52.7 4.0 %backward.2 = (f32[2,512,128]{2,1,0:T(8,128)S(1)}, f32[2,512,128]{2,1,0:T(8,128)S(1)}, f32[2,512,128]{2,1,0:T(8,128)S(1)}, f32[2,512,128]{2,1,0:T(8,128)S(1)}, f...) custom-call(s32[4,6]{1,0:T(4,128)S(1)} %copy-done.4, bf16[512,512]{1,0:T(8,128)(2,1)S(1)} %copy-done, ...), custom_call_target="tpu_custom_call" | custom-call | flops 3221225472 | bytes 5300320 | tf_op jit(solution)/shard_map/backward/pallas_call | solution.py:280
  56.7 5.6 %collective-permute-done.6.refs_6_ = bf16[10,128,128]{2,1,0:T(8,128)(2,1)S(1)} collective-permute-done((bf16[10,128,128]{2,1,0:T(8,128)(2,1)S(1)}, bf16[10,128,128]{2,1,0:T(8,128)(2,1)S(1)}, u32[]{:S(2)}, u32[]{:S(2)}) %collective-permute-start.6) | collective-permute-done | bytes 327712 | tf_op jit(solution)/shard_map/ppermute | solution.py:306
  62.3 0.0 collective-permute-done.7.refs_7_
  62.4 5.9 %collective-permute-done.8.refs_14_ = bf16[10,128,128]{2,1,0:T(8,128)(2,1)S(1)} collective-permute-done((bf16[10,128,128]{2,1,0:T(8,128)(2,1)S(1)}, bf16[10,128,128]{2,1,0:T(8,128)(2,1)S(1)}, u32[]{:S(2)}, u32[]{:S(2)}) %collective-permute-start.8) | collective-permute-done | bytes 327712 | tf_op jit(solution)/shard_map/ppermute | solution.py:306
  68.2 2.9 %collective-permute-done.9.refs_15_ = bf16[10,128,128]{2,1,0:T(8,128)(2,1)S(1)} collective-permute-done((bf16[10,128,128]{2,1,0:T(8,128)(2,1)S(1)}, bf16[10,128,128]{2,1,0:T(8,128)(2,1)S(1)}, u32[]{:S(2)}, u32[]{:S(2)}) %collective-permute-start.9) | collective-permute-done | bytes 327712 | tf_op jit(solution)/shard_map/ppermute | solution.py:306
  71.1 2.6 %finish.1 = (bf16[512,512]{1,0:T(8,128)(2,1)}, bf16[512,512]{1,0:T(8,128)(2,1)}, bf16[512,512]{1,0:T(8,128)(2,1)}, bf16[512,512]{1,0:T(8,128)(2,1)}) custom-call(s32[4,6]{1,0:T(4,128)S(1)} %copy-done.4, f32[2,512,128]{2,1,0:T(8,128)S(1)} %get-tuple-element.46.refs_0_, f32[2,512,128]{2,1,0:T(8,128)S(1)} %get-tuple-element.47.refs_1_, ...), custom_call_target="tpu_custom_call" | custom-call | bytes 7618656 | tf_op jit(solution)/shard_map/finish/pallas_call | solution.py:280
  (4 shorter events, 0.0 us)
Async XLA Ops:
  0.6 1.0 %copy-start = (bf16[512,512]{1,0:T(8,128)(2,1)S(1)}, bf16[512,512]{1,0:T(8,128)(2,1)}, u32[]{:S(2)}) copy-start(bf16[512,512]{1,0:T(8,128)(2,1)} %q.13) | copy-start | bytes 1572868
  1.7 1.0 %copy-start.1 = (bf16[512,512]{1,0:T(8,128)(2,1)S(1)}, bf16[512,512]{1,0:T(8,128)(2,1)}, u32[]{:S(2)}) copy-start(bf16[512,512]{1,0:T(8,128)(2,1)} %k.13) | copy-start | bytes 1572868
  2.7 1.0 %copy-start.2 = (bf16[512,512]{1,0:T(8,128)(2,1)S(1)}, bf16[512,512]{1,0:T(8,128)(2,1)}, u32[]{:S(2)}) copy-start(bf16[512,512]{1,0:T(8,128)(2,1)} %v.13) | copy-start | bytes 1572868
  3.8 1.0 %copy-start.3 = (bf16[512,512]{1,0:T(8,128)(2,1)S(1)}, bf16[512,512]{1,0:T(8,128)(2,1)}, u32[]{:S(2)}) copy-start(bf16[512,512]{1,0:T(8,128)(2,1)} %g.13) | copy-start | bytes 1572868
  4.8 0.7 copy-start.4
  6.4 20.5 %collective-permute-start.2 = (bf16[8,128,128]{2,1,0:T(8,128)(2,1)S(1)}, bf16[8,128,128]{2,1,0:T(8,128)(2,1)S(1)}, u32[]{:S(2)}, u32[]{:S(2)}) collective-permute-start(bf16[8,128,128]{2,1,0:T(8,128)(2,1)S(1)} %get-tuple-element.42), channel_id=1, source_target_pairs={{0,1},{1,0},{2,3},{3,2},{4,5},{5,4},{6,7},{7,6},{8,9},{9,8},{10,11... | collective-permute-start | bytes 786440 | tf_op jit(solution)/shard_map/ppermute | solution.py:306
  7.0 19.9 %collective-permute-start.3 = (bf16[8,128,128]{2,1,0:T(8,128)(2,1)S(1)}, bf16[8,128,128]{2,1,0:T(8,128)(2,1)S(1)}, u32[]{:S(2)}, u32[]{:S(2)}) collective-permute-start(bf16[8,128,128]{2,1,0:T(8,128)(2,1)S(1)} %get-tuple-element.43), channel_id=1, source_target_pairs={{1,2},{2,1},{3,4},{4,3},{5,6},{6,5},{7,8},{8,7},{9,10},{10,9},{11,... | collective-permute-start | bytes 786440 | tf_op jit(solution)/shard_map/ppermute | solution.py:306
  12.2 19.1 %collective-permute-start = (bf16[8,128,128]{2,1,0:T(8,128)(2,1)S(1)}, bf16[8,128,128]{2,1,0:T(8,128)(2,1)S(1)}, u32[]{:S(2)}, u32[]{:S(2)}) collective-permute-start(bf16[8,128,128]{2,1,0:T(8,128)(2,1)S(1)} %get-tuple-element.34), channel_id=1, source_target_pairs={{0,1},{1,0},{2,3},{3,2},{4,5},{5,4},{6,7},{7,6},{8,9},{9,8},{10,11... | collective-permute-start | bytes 786440 | tf_op jit(solution)/shard_map/ppermute | solution.py:306
  12.7 19.6 %collective-permute-start.1 = (bf16[8,128,128]{2,1,0:T(8,128)(2,1)S(1)}, bf16[8,128,128]{2,1,0:T(8,128)(2,1)S(1)}, u32[]{:S(2)}, u32[]{:S(2)}) collective-permute-start(bf16[8,128,128]{2,1,0:T(8,128)(2,1)S(1)} %get-tuple-element.35), channel_id=1, source_target_pairs={{1,2},{2,1},{3,4},{4,3},{5,6},{6,5},{7,8},{8,7},{9,10},{10,9},{11,... | collective-permute-start | bytes 786440 | tf_op jit(solution)/shard_map/ppermute | solution.py:306
  36.1 10.0 %collective-permute-start.4 = (f32[2,8,128]{2,1,0:T(8,128)S(1)}, f32[2,8,128]{2,1,0:T(8,128)S(1)}, u32[]{:S(2)}, u32[]{:S(2)}) collective-permute-start(f32[2,8,128]{2,1,0:T(8,128)S(1)} %pad_maximum_fusion), channel_id=1, source_target_pairs={{0,1},{1,0},{2,3},{3,2},{4,5},{5,4},{6,7},{7,6},{8,9},{9,8},{10,11... | collective-permute-start | bytes 24584 | tf_op jit(solution)/shard_map/ppermute | solution.py:306
  36.2 12.6 %collective-permute-start.5 = (f32[2,8,128]{2,1,0:T(8,128)S(1)}, f32[2,8,128]{2,1,0:T(8,128)S(1)}, u32[]{:S(2)}, u32[]{:S(2)}) collective-permute-start(f32[2,8,128]{2,1,0:T(8,128)S(1)} %pad_maximum_fusion.1), channel_id=1, source_target_pairs={{1,2},{2,1},{3,4},{4,3},{5,6},{6,5},{7,8},{8,7},{9,10},{10,9},{11,... | collective-permute-start | bytes 24584 | tf_op jit(solution)/shard_map/ppermute | solution.py:306
  38.6 23.7 %collective-permute-start.6 = (bf16[10,128,128]{2,1,0:T(8,128)(2,1)S(1)}, bf16[10,128,128]{2,1,0:T(8,128)(2,1)S(1)}, u32[]{:S(2)}, u32[]{:S(2)}) collective-permute-start(bf16[10,128,128]{2,1,0:T(8,128)(2,1)S(1)} %get-tuple-element.52), channel_id=1, source_target_pairs={{0,1},{1,0},{2,3},{3,2},{4,5},{5,4},{6,7},{7,6},{8,9},{9,8},{10,11... | collective-permute-start | bytes 983048 | tf_op jit(solution)/shard_map/ppermute | solution.py:306
  40.6 21.8 %collective-permute-start.7 = (bf16[10,128,128]{2,1,0:T(8,128)(2,1)S(1)}, bf16[10,128,128]{2,1,0:T(8,128)(2,1)S(1)}, u32[]{:S(2)}, u32[]{:S(2)}) collective-permute-start(bf16[10,128,128]{2,1,0:T(8,128)(2,1)S(1)} %get-tuple-element.53), channel_id=1, source_target_pairs={{1,2},{2,1},{3,4},{4,3},{5,6},{6,5},{7,8},{8,7},{9,10},{10,9},{11,... | collective-permute-start | bytes 983048 | tf_op jit(solution)/shard_map/ppermute | solution.py:306
  46.0 22.2 %collective-permute-start.8 = (bf16[10,128,128]{2,1,0:T(8,128)(2,1)S(1)}, bf16[10,128,128]{2,1,0:T(8,128)(2,1)S(1)}, u32[]{:S(2)}, u32[]{:S(2)}) collective-permute-start(bf16[10,128,128]{2,1,0:T(8,128)(2,1)S(1)} %get-tuple-element.62), channel_id=1, source_target_pairs={{0,1},{1,0},{2,3},{3,2},{4,5},{5,4},{6,7},{7,6},{8,9},{9,8},{10,11... | collective-permute-start | bytes 983048 | tf_op jit(solution)/shard_map/ppermute | solution.py:306
  46.1 25.0 %collective-permute-start.9 = (bf16[10,128,128]{2,1,0:T(8,128)(2,1)S(1)}, bf16[10,128,128]{2,1,0:T(8,128)(2,1)S(1)}, u32[]{:S(2)}, u32[]{:S(2)}) collective-permute-start(bf16[10,128,128]{2,1,0:T(8,128)(2,1)S(1)} %get-tuple-element.63), channel_id=1, source_target_pairs={{1,2},{2,1},{3,4},{4,3},{5,6},{6,5},{7,8},{8,7},{9,10},{10,9},{11,... | collective-permute-start | bytes 983048 | tf_op jit(solution)/shard_map/ppermute | solution.py:306

commit v3 on v2

--- a/solution.py
+++ b/solution.py
@@ -105,14 +105,14 @@
     return jnp.sum(x, axis=0, keepdims=True)
 
 
-def pack_kernel(nb, half, lists, q, k, v, g, out_a, out_b, sems):
+def pack_kernel(nb, lists, q, k, v, g, out_a, out_b, sems):
     at = Place(lists, nb)
     copies = []
     for out, partner in zip((out_a, out_b), at.partners):
         for slot, (h, b) in enumerate(partner.sent):
             for i, array in enumerate((q, k, v, g)):
                 copy = pltpu.make_async_copy(
-                    array.at[rows_of(b), lane(h, half)], out.at[2 * i + slot], sems.at[len(copies)]
+                    array.at[rows_of(b), lane(h, 0)], out.at[2 * i + slot], sems.at[len(copies)]
                 )
                 copy.start()
                 copies.append(copy)
@@ -120,9 +120,13 @@
         copy.wait()
 
 
-def own_forward_kernel(nb, lists, q, k, v, g, stats, ot):
+def own_forward_kernel(nb, lists, q, k, v, g, stats, ot, out_a, out_b):
     at = Place(lists, nb)
     biases = at.biases()
+    for out, partner in zip((out_a, out_b), at.partners):
+        for slot, (h, b) in enumerate(partner.sent):
+            for i, array in enumerate((q, k, v, g)):
+                out[2 * i + slot] = array[rows_of(b), lane(h, 1)]
     for h in range(HEADS):
         cols = lane(h, 0)
         kh, vh = k[:, cols], v[:, cols]
@@ -136,6 +140,18 @@
             stats[h, 1:2, rows] = total_of(p)
             stats[h, 2:3, rows] = total_of(p * dp)
             ot[h, :, rows] = dot(vh, p.astype(BF16), 0, 0)
+
+
+def split(x):
+    parts = []
+    for _ in range(3):
+        part = x.astype(BF16)
+        parts.append(part)
+        x = x - part.astype(F32)
+    return parts
+
+
+TILES = 10 * BLOCK
 
 
 def guest_kernel(nb, half, lists, q, k, v, g, in_a, in_b, stats0, ot0, stats, ot, out_a, out_b, st_a, st_b):
@@ -160,9 +176,9 @@
             st[2 * slot : 2 * slot + 1, :] = m + jnp.log2(total)
             st[2 * slot + 1 : 2 * slot + 2, :] = delta
             weights = p.astype(BF16)
-            out[slot] = dot(vh, weights, 0, 0).astype(BF16)
-            out[2 + slot] = dot(kh, (p * (dp - delta)).astype(BF16), 0, 0).astype(BF16)
-            out[4 + slot] = dot(kh, weights, 0, 0).astype(BF16)
+            out[rows_of(slot), :] = dot(vh, weights, 0, 0).astype(BF16)
+            out[rows_of(2 + slot), :] = dot(kh, (p * (dp - delta)).astype(BF16), 0, 0).astype(BF16)
+            out[rows_of(4 + slot), :] = dot(kh, weights, 0, 0).astype(BF16)
             s = across(dot(kg, qh, 1, 1), free)
             old = stats[h, 0:1, span]
             m = jnp.maximum(old, jnp.max(s, axis=0, keepdims=True))
@@ -183,11 +199,14 @@
             s, dp, qh, gh = kept.pop(0)
             p = jnp.exp2(s - stats[h, 3:4, partner.span])
             ds = (p * (dp - stats[h, 4:5, partner.span])).astype(BF16)
-            out[6 + slot] = dot(ds, qh, 1, 0).astype(BF16)
-            out[8 + slot] = dot(p.astype(BF16), gh, 1, 0).astype(BF16)
+            out[rows_of(6 + slot), :] = dot(ds, qh, 1, 0).astype(BF16)
+            out[rows_of(8 + slot), :] = dot(p.astype(BF16), gh, 1, 0).astype(BF16)
         for slot, (h, b) in enumerate(partner.sent):
             st[4 + 2 * slot : 5 + 2 * slot, :] = stats[h, 3:4, rows_of(b)]
             st[5 + 2 * slot : 6 + 2 * slot, :] = stats[h, 4:5, rows_of(b)]
+        if half == 0:
+            for i, part in enumerate(split(st[...])):
+                out[TILES + 8 * i : TILES + 8 * i + 8, :] = part
 
 
 def merged(l1, d1, l2, d2):
@@ -198,9 +217,15 @@
 
 
 def backward_kernel(
-    nb, half, lists, q, k, v, g, in_a, in_b, stats, ot, st_a, st_b, got_a, got_b,
-    att, aq, ak, av, mix_a, mix_b, fin, ps, dss,
+    nb, half, lists, q, k, v, g, in_a, in_b, stats, ot, st_a, st_b, came_a, came_b, *refs
 ):
+    att, aq, ak, av, mix_a, mix_b, fin, ps, dss, got_a, got_b = refs[-11:]
+    for came, got in ((came_a, got_a), (came_b, got_b)):
+        if half == 0:
+            parts = [came[TILES + 8 * i : TILES + 8 * i + 8, :].astype(F32) for i in range(3)]
+            got[...] = parts[0] + (parts[1] + parts[2])
+        else:
+            got[...] = came[...]
     at = Place(lists, nb)
     biases = at.biases()
     fin[:, 0:2, :] = stats[:, 3:5, :]
@@ -260,7 +285,7 @@
         for partner, mix, back in zip(at.partners, (mix_a, mix_b), (back_a, back_b)):
             for slot, (h, b) in enumerate(partner.sent):
                 rows = rows_of(b)
-                o, u, w, dk, dv = (back[2 * i + slot].astype(F32) for i in range(5))
+                o, u, w, dk, dv = (back[rows_of(2 * i + slot), :].astype(F32) for i in range(5))
                 weight = mix[2 * slot : 2 * slot + 1, :]
                 so[h, rows, :] += (o * weight).T
                 sq[h, rows, :] += ((u - w * mix[2 * slot + 1 : 2 * slot + 2, :]) * weight).T
@@ -274,18 +299,17 @@
             v_out[:, cols] = sv[h].astype(BF16)
 
 
-def call(kernel, name, outs, args, scratch=(), flops=0, space=pltpu.VMEM):
+def call(kernel, name, outs, args, scratch=(), flops=0, spaces=None, limit=24 << 20, out=pltpu.VMEM):
     moved = sum(math.prod(s.shape) * s.dtype.itemsize for s in (*outs, *args))
-    vmem = pl.BlockSpec(memory_space=pltpu.VMEM)
+    spaces = spaces or (pltpu.SMEM,) + (pltpu.VMEM,) * (len(args) - 1)
     return pl.pallas_call(
         kernel,
         out_shape=tuple(outs),
-        in_specs=[pl.BlockSpec(memory_space=pltpu.SMEM)]
-        + [pl.BlockSpec(memory_space=space)] * (len(args) - 1),
-        out_specs=tuple([vmem] * len(outs)),
+        in_specs=[pl.BlockSpec(memory_space=space) for space in spaces],
+        out_specs=tuple([pl.BlockSpec(memory_space=out)] * len(outs)),
         scratch_shapes=scratch,
-        cost_estimate=pl.CostEstimate(flops=flops, bytes_accessed=moved, transcendentals=0),
-        compiler_params=pltpu.CompilerParams(vmem_limit_bytes=24 << 20),
+        cost_estimate=pl.CostEstimate(flops=flops, bytes_accessed=moved if flops else 1, transcendentals=0),
+        compiler_params=pltpu.CompilerParams(vmem_limit_bytes=limit),
         name=name,
     )(*args)
 
@@ -306,37 +330,40 @@
         return lax.ppermute(to_a, "seq", pairs(0)), lax.ppermute(to_b, "seq", pairs(1))
 
     arrays = (lists, q, k, v, g)
-    tile8, tile10 = sds((8, BLOCK, HD), BF16), sds((10, BLOCK, HD), BF16)
-    guests = [
-        swap(*call(
-            functools.partial(pack_kernel, nb, half), "pack", [tile8] * 2, arrays,
-            scratch=(pltpu.SemaphoreType.DMA((16,)),), space=pltpu.HBM,
-        ))
-        for half in range(2)
-    ]
-    stats0, ot0 = call(
+    tile8 = sds((8, BLOCK, HD), BF16)
+    st, acc = sds((8, HD), F32), sds((2, rows, HD), F32)
+    first = call(
+        functools.partial(pack_kernel, nb), "pack", [tile8] * 2, arrays,
+        scratch=(pltpu.SemaphoreType.DMA((16,)),), spaces=(pltpu.SMEM,) + (pl.ANY,) * 4, limit=60 << 20,
+    )
+    guests = [swap(*first)]
+    stats0, ot0, *second = call(
         functools.partial(own_forward_kernel, nb), "own_forward",
-        [sds((HEADS, 8, rows), F32), sds((HEADS, HD, rows), F32)], arrays, flops=3 << 30,
-    )
-    st, acc = sds((8, HD), F32), sds((2, rows, HD), F32)
+        [sds((HEADS, 8, rows), F32), sds((HEADS, HD, rows), F32), tile8, tile8], arrays, flops=6 << 30,
+    )
+    guests.append(swap(*second))
     forward, backs = [], []
     for half in range(2):
+        result = sds((TILES + 32 * (1 - half), HD), BF16)
         *kept, out_a, out_b, st_a, st_b = call(
             functools.partial(guest_kernel, nb, half), "guest",
-            [sds((2, 8, rows), F32), sds((2, HD, rows), F32), tile10, tile10, st, st],
-            (*arrays, *guests[half], stats0, ot0), flops=2 << 30,
+            [sds((2, 8, rows), F32), sds((2, HD, rows), F32), result, result, st, st],
+            (*arrays, *guests[half], stats0, ot0), flops=4 << 30,
         )
+        got = () if half == 0 else swap(st_a, st_b)
         backs.append(swap(out_a, out_b))
-        forward.append((*kept, st_a, st_b))
-    got = swap(*(jnp.stack([forward[0][i], forward[1][i]]) for i in (2, 3)))
-    pieces = []
+        forward.append((*kept, st_a, st_b, *(got or backs[0])))
+    pieces, outs = [], ()
     for half in range(2):
+        after = outs[-2:]
         outs = call(
             functools.partial(backward_kernel, nb, half), "backward", [acc] * 4 + [st] * 2,
-            (*arrays, *guests[half], *forward[half], got[0][half], got[1][half]),
+            (*arrays, *guests[half], *forward[half], *after),
             scratch=(
                 pltpu.VMEM((2, 8, rows), F32), pltpu.VMEM((rows, rows), BF16), pltpu.VMEM((rows, rows), BF16),
-            ), flops=3 << 30,
+                pltpu.VMEM((8, HD), F32), pltpu.VMEM((8, HD), F32),
+            ), flops=(40 << 30, 1 << 30)[half],
+            spaces=(pltpu.SMEM,) + (pltpu.VMEM,) * 12 + (pl.ANY,) * len(after),
         )
         pieces += [*outs, *backs[half]]
     return call(

time: 74.1 us -> 61.7 us (0.83)
  the two profiles are of different devices: /device:TPU:18 before, /device:TPU:8 now
where the time goes in v3:
time: 61.7 us; the launch traced here: 60.8 us
  Pallas kernels  26 us (42%)
  starting transfers between devices  24.7 us (40%)
  waiting for transfers between devices  9.33 us (15%)
  between operations  0.85 us (1%)
    pallas_call x7, Pallas kernels, call(): pl.pallas_call(kernel, out_shape=tuple(outs), in_specs=[pl.BlockSpec(memo...  26 us
    ppermute x5, starting transfers between devices, swap(): lax.ppermute(to_b, 'seq', pairs(1))  14.3 us
    ppermute x5, starting transfers between devices, swap(): lax.ppermute(to_a, 'seq', pairs(0))  10.4 us
    ppermute x5, waiting for transfers between devices, swap(): lax.ppermute(to_a, 'seq', pairs(0))  9.32 us
  transfers between devices with their start and end apart: 10, of which 1 were waited for; matrix products, arithmetic and copies ran while one was open for 0% of the time, Pallas kernels for 34%

profile of v3, /device:TPU:8, one launch (start us, length us, event | category | flops | bytes accessed | tf_op | source)
XLA Modules:
  0.0 60.8 jit_solution(14923476377444999167)
XLA Ops:
  0.6 0.0 copy-start.3
  0.6 0.0 copy-start.2
  0.7 0.0 copy-start.1
  0.7 0.0 copy-start
  0.7 2.8 %pack.1 = (bf16[8,128,128]{2,1,0:T(8,128)(2,1)}, bf16[8,128,128]{2,1,0:T(8,128)(2,1)}) custom-call(s32[4,6]{1,0:T(4,128)} %lists.13, bf16[512,512]{1,0:T(8,128)(2,1)} %q.11, bf16[512,512]{1,0:T(8,128)(2,1)} %k.11, bf16[512,512]{1,0:T(8,128)(2,1)} %v.11, bf16[512,512]{1,0:T(8,128)(2,1)} %g.11), custom_call_target="tpu_custom_call" | custom-call | bytes 1 | tf_op jit(solution)/shard_map/pack/pallas_call | solution.py:305
  3.5 0.0 copy-start.4
  3.5 1.6 %collective-permute-start = (bf16[8,128,128]{2,1,0:T(8,128)(2,1)}, bf16[8,128,128]{2,1,0:T(8,128)(2,1)S(1)}, u32[]{:S(2)}, u32[]{:S(2)}) collective-permute-start(bf16[8,128,128]{2,1,0:T(8,128)(2,1)} %get-tuple-element.34), channel_id=1, source_target_pairs={{0,1},{1,0},{2,3},{3,2},{4,5},{5,4},{6,7},{7,6},{8,9},{9,8},{10,11... | collective-permute-start | bytes 786440 | tf_op jit(solution)/shard_map/ppermute | solution.py:330
  5.0 3.3 %collective-permute-start.1 = (bf16[8,128,128]{2,1,0:T(8,128)(2,1)}, bf16[8,128,128]{2,1,0:T(8,128)(2,1)S(1)}, u32[]{:S(2)}, u32[]{:S(2)}) collective-permute-start(bf16[8,128,128]{2,1,0:T(8,128)(2,1)} %get-tuple-element.35), channel_id=1, source_target_pairs={{1,2},{2,1},{3,4},{4,3},{5,6},{6,5},{7,8},{8,7},{9,10},{10,9},{11,... | collective-permute-start | bytes 786440 | tf_op jit(solution)/shard_map/ppermute | solution.py:330
  8.3 0.0 copy-done.3
  8.3 0.0 copy-done.2
  8.3 0.0 copy-done.1
  8.4 0.0 copy-done
  8.4 0.0 copy-done.4
  8.4 5.2 %own_forward.1 = (f32[4,8,512]{2,1,0:T(8,128)S(1)}, f32[4,128,512]{2,1,0:T(8,128)S(1)}, bf16[8,128,128]{2,1,0:T(8,128)(2,1)S(1)}, bf16[8,128,128]{2,1,0:T(8,128)(2,1)S(1)}) custom-call(s32[4,6]{1,0:T(4,128)S(1)} %copy-done.4, bf16[512,512]{1,0:T(8,128)(2,1)S(1)} %copy-done, bf16[512,512]{1,0:T(8,128)(2,1)S(1)} %copy-done.1, bf16[512,512]{1,0:T(8,128)(2,1)S(1)} %copy-done.2, ...), custom_call_target="tpu_custom_call" | custom-call | flops 6442450944 | bytes 3735648 | tf_op jit(solution)/shard_map/own_forward/pallas_call | solution.py:305
  13.6 1.7 %collective-permute-start.4 = (bf16[8,128,128]{2,1,0:T(8,128)(2,1)S(1)}, bf16[8,128,128]{2,1,0:T(8,128)(2,1)S(1)}, u32[]{:S(2)}, u32[]{:S(2)}) collective-permute-start(bf16[8,128,128]{2,1,0:T(8,128)(2,1)S(1)} %get-tuple-element.50), channel_id=1, source_target_pairs={{0,1},{1,0},{2,3},{3,2},{4,5},{5,4},{6,7},{7,6},{8,9},{9,8},{10,11... | collective-permute-start | bytes 786440 | tf_op jit(solution)/shard_map/ppermute | solution.py:330
  15.2 2.8 %collective-permute-start.5 = (bf16[8,128,128]{2,1,0:T(8,128)(2,1)S(1)}, bf16[8,128,128]{2,1,0:T(8,128)(2,1)S(1)}, u32[]{:S(2)}, u32[]{:S(2)}) collective-permute-start(bf16[8,128,128]{2,1,0:T(8,128)(2,1)S(1)} %get-tuple-element.51), channel_id=1, source_target_pairs={{1,2},{2,1},{3,4},{4,3},{5,6},{6,5},{7,8},{8,7},{9,10},{10,9},{11,... | collective-permute-start | bytes 786440 | tf_op jit(solution)/shard_map/ppermute | solution.py:330
  18.0 0.0 collective-permute-done.in_a
  18.0 0.0 collective-permute-done.1.in_b
  18.0 3.7 %guest.2 = (f32[2,8,512]{2,1,0:T(8,128)S(1)}, f32[2,128,512]{2,1,0:T(8,128)S(1)}, bf16[1312,128]{1,0:T(8,128)(2,1)S(1)}, bf16[1312,128]{1,0:T(8,128)(2,1)S(1)}, ...) custom-call(s32[4,6]{1,0:T(4,128)S(1)} %copy-done.4, bf16[512,512]{1,0:T(8,128)(2,1)S(1)} %copy-done, ...), custom_call_target="tpu_custom_call" | custom-call | flops 4294967296 | bytes 4972640 | tf_op jit(solution)/shard_map/guest/pallas_call | solution.py:305
  21.8 3.0 %collective-permute-start.2 = (bf16[1312,128]{1,0:T(8,128)(2,1)S(1)}, bf16[1312,128]{1,0:T(8,128)(2,1)S(1)}, u32[]{:S(2)}, u32[]{:S(2)}) collective-permute-start(bf16[1312,128]{1,0:T(8,128)(2,1)S(1)} %get-tuple-element.42), channel_id=1, source_target_pairs={{0,1},{1,0},{2,3},{3,2},{4,5},{5,4},{6,7},{7,6},{8,9},{9,8},{10,11... | collective-permute-start | bytes 1007624 | tf_op jit(solution)/shard_map/ppermute | solution.py:330
  24.8 1.9 %collective-permute-start.3 = (bf16[1312,128]{1,0:T(8,128)(2,1)S(1)}, bf16[1312,128]{1,0:T(8,128)(2,1)S(1)}, u32[]{:S(2)}, u32[]{:S(2)}) collective-permute-start(bf16[1312,128]{1,0:T(8,128)(2,1)S(1)} %get-tuple-element.43), channel_id=1, source_target_pairs={{1,2},{2,1},{3,4},{4,3},{5,6},{6,5},{7,8},{8,7},{9,10},{10,9},{11,... | collective-permute-start | bytes 1007624 | tf_op jit(solution)/shard_map/ppermute | solution.py:330
  26.7 9.3 %collective-permute-done.4.in_a = bf16[8,128,128]{2,1,0:T(8,128)(2,1)S(1)} collective-permute-done((bf16[8,128,128]{2,1,0:T(8,128)(2,1)S(1)}, bf16[8,128,128]{2,1,0:T(8,128)(2,1)S(1)}, u32[]{:S(2)}, u32[]{:S(2)}) %collective-permute-start.4) | collective-permute-done | bytes 262176 | tf_op jit(solution)/shard_map/ppermute | solution.py:330
  36.0 0.0 collective-permute-done.5.in_b
  36.0 3.8 %guest.3 = (f32[2,8,512]{2,1,0:T(8,128)S(1)}, f32[2,128,512]{2,1,0:T(8,128)S(1)}, bf16[1280,128]{1,0:T(8,128)(2,1)S(1)}, bf16[1280,128]{1,0:T(8,128)(2,1)S(1)}, ...) custom-call(s32[4,6]{1,0:T(4,128)S(1)} %copy-done.4, bf16[512,512]{1,0:T(8,128)(2,1)S(1)} %copy-done, ...), custom_call_target="tpu_custom_call" | custom-call | flops 4294967296 | bytes 4956256 | tf_op jit(solution)/shard_map/guest/pallas_call | solution.py:305
  39.8 2.6 %collective-permute-start.6 = (f32[8,128]{1,0:T(8,128)S(1)}, f32[8,128]{1,0:T(8,128)S(1)}, u32[]{:S(2)}, u32[]{:S(2)}) collective-permute-start(f32[8,128]{1,0:T(8,128)S(1)} %get-tuple-element.54.st_a), channel_id=1, source_target_pairs={{0,1},{1,0},{2,3},{3,2},{4,5},{5,4},{6,7},{7,6},{8,9},{9,8},{10,11... | collective-permute-start | bytes 12296 | tf_op jit(solution)/shard_map/ppermute | solution.py:330
  42.3 1.9 %collective-permute-start.7 = (f32[8,128]{1,0:T(8,128)S(1)}, f32[8,128]{1,0:T(8,128)S(1)}, u32[]{:S(2)}, u32[]{:S(2)}) collective-permute-start(f32[8,128]{1,0:T(8,128)S(1)} %get-tuple-element.55.st_b), channel_id=1, source_target_pairs={{1,2},{2,1},{3,4},{4,3},{5,6},{6,5},{7,8},{8,7},{9,10},{10,9},{11,... | collective-permute-start | bytes 12296 | tf_op jit(solution)/shard_map/ppermute | solution.py:330
  44.2 1.6 %collective-permute-start.8 = (bf16[1280,128]{1,0:T(8,128)(2,1)S(1)}, bf16[1280,128]{1,0:T(8,128)(2,1)S(1)}, u32[]{:S(2)}, u32[]{:S(2)}) collective-permute-start(bf16[1280,128]{1,0:T(8,128)(2,1)S(1)} %get-tuple-element.62), channel_id=1, source_target_pairs={{0,1},{1,0},{2,3},{3,2},{4,5},{5,4},{6,7},{7,6},{8,9},{9,8},{10,11... | collective-permute-start | bytes 983048 | tf_op jit(solution)/shard_map/ppermute | solution.py:330
  45.8 0.0 collective-permute-done.2.came_a.refs_6_
  45.8 4.4 %collective-permute-start.9 = (bf16[1280,128]{1,0:T(8,128)(2,1)S(1)}, bf16[1280,128]{1,0:T(8,128)(2,1)S(1)}, u32[]{:S(2)}, u32[]{:S(2)}) collective-permute-start(bf16[1280,128]{1,0:T(8,128)(2,1)S(1)} %get-tuple-element.63), channel_id=1, source_target_pairs={{1,2},{2,1},{3,4},{4,3},{5,6},{6,5},{7,8},{8,7},{9,10},{10,9},{11,... | collective-permute-start | bytes 983048 | tf_op jit(solution)/shard_map/ppermute | solution.py:330
  50.2 0.0 collective-permute-done.3.came_b.refs_7_
  50.3 4.0 %backward.2 = (f32[2,512,128]{2,1,0:T(8,128)S(1)}, f32[2,512,128]{2,1,0:T(8,128)S(1)}, f32[2,512,128]{2,1,0:T(8,128)S(1)}, f32[2,512,128]{2,1,0:T(8,128)S(1)}, f...) custom-call(s32[4,6]{1,0:T(4,128)S(1)} %copy-done.4, bf16[512,512]{1,0:T(8,128)(2,1)S(1)} %copy-done, ...), custom_call_target="tpu_custom_call" | custom-call | flops 42949672960 | bytes 5963872 | tf_op jit(solution)/shard_map/backward/pallas_call | solution.py:305
  54.2 0.0 collective-permute-done.6.came_a
  54.2 0.0 collective-permute-done.7.came_b
  54.3 4.0 %backward.3 = (f32[2,512,128]{2,1,0:T(8,128)S(1)}, f32[2,512,128]{2,1,0:T(8,128)S(1)}, f32[2,512,128]{2,1,0:T(8,128)S(1)}, f32[2,512,128]{2,1,0:T(8,128)S(1)}, f...) custom-call(s32[4,6]{1,0:T(4,128)S(1)} %copy-done.4, bf16[512,512]{1,0:T(8,128)(2,1)S(1)} %copy-done, ...), custom_call_target="tpu_custom_call" | custom-call | flops 1073741824 | bytes 5308512 | tf_op jit(solution)/shard_map/backward/pallas_call | solution.py:305
  58.2 0.0 collective-permute-done.8.refs_14_
  58.2 0.0 collective-permute-done.9.refs_15_
  58.3 2.6 %finish.1 = (bf16[512,512]{1,0:T(8,128)(2,1)}, bf16[512,512]{1,0:T(8,128)(2,1)}, bf16[512,512]{1,0:T(8,128)(2,1)}, bf16[512,512]{1,0:T(8,128)(2,1)}) custom-call(s32[4,6]{1,0:T(4,128)S(1)} %copy-done.4, f32[2,512,128]{2,1,0:T(8,128)S(1)} %get-tuple-element.44.refs_0_, f32[2,512,128]{2,1,0:T(8,128)S(1)} %get-tuple-element.45.refs_1_, ...), custom_call_target="tpu_custom_call" | custom-call | bytes 1 | tf_op jit(solution)/shard_map/finish/pallas_call | solution.py:305
Async XLA Ops:
  0.6 7.7 %copy-start.3 = (bf16[512,512]{1,0:T(8,128)(2,1)S(1)}, bf16[512,512]{1,0:T(8,128)(2,1)}, u32[]{:S(2)}) copy-start(bf16[512,512]{1,0:T(8,128)(2,1)} %g.11) | copy-start | bytes 1572868
  0.6 7.7 %copy-start.2 = (bf16[512,512]{1,0:T(8,128)(2,1)S(1)}, bf16[512,512]{1,0:T(8,128)(2,1)}, u32[]{:S(2)}) copy-start(bf16[512,512]{1,0:T(8,128)(2,1)} %v.11) | copy-start | bytes 1572868
  0.7 7.7 %copy-start.1 = (bf16[512,512]{1,0:T(8,128)(2,1)S(1)}, bf16[512,512]{1,0:T(8,128)(2,1)}, u32[]{:S(2)}) copy-start(bf16[512,512]{1,0:T(8,128)(2,1)} %k.11) | copy-start | bytes 1572868
  0.7 7.7 %copy-start = (bf16[512,512]{1,0:T(8,128)(2,1)S(1)}, bf16[512,512]{1,0:T(8,128)(2,1)}, u32[]{:S(2)}) copy-start(bf16[512,512]{1,0:T(8,128)(2,1)} %q.11) | copy-start | bytes 1572868
  3.5 4.9 %copy-start.4 = (s32[4,6]{1,0:T(4,128)S(1)}, s32[4,6]{1,0:T(4,128)}, u32[]{:S(2)}) copy-start(s32[4,6]{1,0:T(4,128)} %lists.13) | copy-start | bytes 292
  3.5 14.5 %collective-permute-start = (bf16[8,128,128]{2,1,0:T(8,128)(2,1)}, bf16[8,128,128]{2,1,0:T(8,128)(2,1)S(1)}, u32[]{:S(2)}, u32[]{:S(2)}) collective-permute-start(bf16[8,128,128]{2,1,0:T(8,128)(2,1)} %get-tuple-element.34), channel_id=1, source_target_pairs={{0,1},{1,0},{2,3},{3,2},{4,5},{5,4},{6,7},{7,6},{8,9},{9,8},{10,11... | collective-permute-start | bytes 786440 | tf_op jit(solution)/shard_map/ppermute | solution.py:330
  5.0 13.0 %collective-permute-start.1 = (bf16[8,128,128]{2,1,0:T(8,128)(2,1)}, bf16[8,128,128]{2,1,0:T(8,128)(2,1)S(1)}, u32[]{:S(2)}, u32[]{:S(2)}) collective-permute-start(bf16[8,128,128]{2,1,0:T(8,128)(2,1)} %get-tuple-element.35), channel_id=1, source_target_pairs={{1,2},{2,1},{3,4},{4,3},{5,6},{6,5},{7,8},{8,7},{9,10},{10,9},{11,... | collective-permute-start | bytes 786440 | tf_op jit(solution)/shard_map/ppermute | solution.py:330
  13.6 22.4 %collective-permute-start.4 = (bf16[8,128,128]{2,1,0:T(8,128)(2,1)S(1)}, bf16[8,128,128]{2,1,0:T(8,128)(2,1)S(1)}, u32[]{:S(2)}, u32[]{:S(2)}) collective-permute-start(bf16[8,128,128]{2,1,0:T(8,128)(2,1)S(1)} %get-tuple-element.50), channel_id=1, source_target_pairs={{0,1},{1,0},{2,3},{3,2},{4,5},{5,4},{6,7},{7,6},{8,9},{9,8},{10,11... | collective-permute-start | bytes 786440 | tf_op jit(solution)/shard_map/ppermute | solution.py:330
  15.2 20.8 %collective-permute-start.5 = (bf16[8,128,128]{2,1,0:T(8,128)(2,1)S(1)}, bf16[8,128,128]{2,1,0:T(8,128)(2,1)S(1)}, u32[]{:S(2)}, u32[]{:S(2)}) collective-permute-start(bf16[8,128,128]{2,1,0:T(8,128)(2,1)S(1)} %get-tuple-element.51), channel_id=1, source_target_pairs={{1,2},{2,1},{3,4},{4,3},{5,6},{6,5},{7,8},{8,7},{9,10},{10,9},{11,... | collective-permute-start | bytes 786440 | tf_op jit(solution)/shard_map/ppermute | solution.py:330
  21.8 24.1 %collective-permute-start.2 = (bf16[1312,128]{1,0:T(8,128)(2,1)S(1)}, bf16[1312,128]{1,0:T(8,128)(2,1)S(1)}, u32[]{:S(2)}, u32[]{:S(2)}) collective-permute-start(bf16[1312,128]{1,0:T(8,128)(2,1)S(1)} %get-tuple-element.42), channel_id=1, source_target_pairs={{0,1},{1,0},{2,3},{3,2},{4,5},{5,4},{6,7},{7,6},{8,9},{9,8},{10,11... | collective-permute-start | bytes 1007624 | tf_op jit(solution)/shard_map/ppermute | solution.py:330
  24.8 25.5 %collective-permute-start.3 = (bf16[1312,128]{1,0:T(8,128)(2,1)S(1)}, bf16[1312,128]{1,0:T(8,128)(2,1)S(1)}, u32[]{:S(2)}, u32[]{:S(2)}) collective-permute-start(bf16[1312,128]{1,0:T(8,128)(2,1)S(1)} %get-tuple-element.43), channel_id=1, source_target_pairs={{1,2},{2,1},{3,4},{4,3},{5,6},{6,5},{7,8},{8,7},{9,10},{10,9},{11,... | collective-permute-start | bytes 1007624 | tf_op jit(solution)/shard_map/ppermute | solution.py:330
  39.8 14.5 %collective-permute-start.6 = (f32[8,128]{1,0:T(8,128)S(1)}, f32[8,128]{1,0:T(8,128)S(1)}, u32[]{:S(2)}, u32[]{:S(2)}) collective-permute-start(f32[8,128]{1,0:T(8,128)S(1)} %get-tuple-element.54.st_a), channel_id=1, source_target_pairs={{0,1},{1,0},{2,3},{3,2},{4,5},{5,4},{6,7},{7,6},{8,9},{9,8},{10,11... | collective-permute-start | bytes 12296 | tf_op jit(solution)/shard_map/ppermute | solution.py:330
  42.3 11.9 %collective-permute-start.7 = (f32[8,128]{1,0:T(8,128)S(1)}, f32[8,128]{1,0:T(8,128)S(1)}, u32[]{:S(2)}, u32[]{:S(2)}) collective-permute-start(f32[8,128]{1,0:T(8,128)S(1)} %get-tuple-element.55.st_b), channel_id=1, source_target_pairs={{1,2},{2,1},{3,4},{4,3},{5,6},{6,5},{7,8},{8,7},{9,10},{10,9},{11,... | collective-permute-start | bytes 12296 | tf_op jit(solution)/shard_map/ppermute | solution.py:330
  44.2 14.0 %collective-permute-start.8 = (bf16[1280,128]{1,0:T(8,128)(2,1)S(1)}, bf16[1280,128]{1,0:T(8,128)(2,1)S(1)}, u32[]{:S(2)}, u32[]{:S(2)}) collective-permute-start(bf16[1280,128]{1,0:T(8,128)(2,1)S(1)} %get-tuple-element.62), channel_id=1, source_target_pairs={{0,1},{1,0},{2,3},{3,2},{4,5},{5,4},{6,7},{7,6},{8,9},{9,8},{10,11... | collective-permute-start | bytes 983048 | tf_op jit(solution)/shard_map/ppermute | solution.py:330
  45.8 12.4 %collective-permute-start.9 = (bf16[1280,128]{1,0:T(8,128)(2,1)S(1)}, bf16[1280,128]{1,0:T(8,128)(2,1)S(1)}, u32[]{:S(2)}, u32[]{:S(2)}) collective-permute-start(bf16[1280,128]{1,0:T(8,128)(2,1)S(1)} %get-tuple-element.63), channel_id=1, source_target_pairs={{1,2},{2,1},{3,4},{4,3},{5,6},{6,5},{7,8},{8,7},{9,10},{10,9},{11,... | collective-permute-start | bytes 983048 | tf_op jit(solution)/shard_map/ppermute | solution.py:330

commit v4 on v3

--- a/solution.py
+++ b/solution.py
@@ -105,22 +105,24 @@
     return jnp.sum(x, axis=0, keepdims=True)
 
 
-def pack_kernel(nb, lists, q, k, v, g, out_a, out_b, sems):
+def pack_kernel(nb, lists, q, k, v, g, out_a, out_b, tiles, sems):
     at = Place(lists, nb)
     copies = []
     for out, partner in zip((out_a, out_b), at.partners):
         for slot, (h, b) in enumerate(partner.sent):
             for i, array in enumerate((q, k, v, g)):
-                copy = pltpu.make_async_copy(
-                    array.at[rows_of(b), lane(h, 0)], out.at[2 * i + slot], sems.at[len(copies)]
-                )
+                n = len(copies)
+                copy = pltpu.make_async_copy(array.at[rows_of(b), lane(h, 0)], tiles.at[n], sems.at[0, n])
                 copy.start()
-                copies.append(copy)
-    for copy in copies:
-        copy.wait()
-
-
-def own_forward_kernel(nb, lists, q, k, v, g, stats, ot, out_a, out_b):
+                copies.append((copy, pltpu.make_async_copy(tiles.at[n], out.at[2 * i + slot], sems.at[1, n])))
+    for arrival, departure in copies:
+        arrival.wait()
+        departure.start()
+    for _, departure in copies:
+        departure.wait()
+
+
+def own_forward_kernel(nb, lists, q, k, v, g, stats, ot, out_a, out_b, ps):
     at = Place(lists, nb)
     biases = at.biases()
     for out, partner in zip((out_a, out_b), at.partners):
@@ -130,16 +132,17 @@
     for h in range(HEADS):
         cols = lane(h, 0)
         kh, vh = k[:, cols], v[:, cols]
+        scores, grads = dot(kh, q[:, cols], 1, 1), dot(vh, g[:, cols], 1, 1)
         for a in range(nb):
             rows = rows_of(a)
-            s = down(dot(kh, q[rows, cols], 1, 1), biases[a])
+            s = down(scores[:, a * BLOCK : (a + 1) * BLOCK], biases[a])
             m = jnp.max(s, axis=0, keepdims=True)
             p = jnp.exp2(s - m)
-            dp = dot(vh, g[rows, cols], 1, 1)
             stats[h, 0:1, rows] = m
             stats[h, 1:2, rows] = total_of(p)
-            stats[h, 2:3, rows] = total_of(p * dp)
-            ot[h, :, rows] = dot(vh, p.astype(BF16), 0, 0)
+            stats[h, 2:3, rows] = total_of(p * grads[:, a * BLOCK : (a + 1) * BLOCK])
+            ps[:, rows] = p.astype(BF16)
+        ot[h] = dot(vh, ps[...], 0, 0)
 
 
 def split(x):
@@ -154,13 +157,17 @@
 TILES = 10 * BLOCK
 
 
-def guest_kernel(nb, half, lists, q, k, v, g, in_a, in_b, stats0, ot0, stats, ot, out_a, out_b, st_a, st_b):
+def guest_kernel(nb, half, lists, q, k, v, g, in_a, in_b, stats0, ot0,
+                 stats, ot, out_a, out_b, st_a, st_b, aq, pg, dpg):
     at = Place(lists, nb)
     for h in range(2):
         stats[h] = stats0[2 * half + h]
         ot[h] = ot0[2 * half + h]
+    aq[...] = jnp.zeros_like(aq)
     kept = []
-    for partner, message, out, st in zip(at.partners, (in_a, in_b), (out_a, out_b), (st_a, st_b)):
+    for n, (partner, message, out, st) in enumerate(
+        zip(at.partners, (in_a, in_b), (out_a, out_b), (st_a, st_b))
+    ):
         span = partner.span
         for slot, (h, near, free) in enumerate(partner.guests):
             qg, kg, vg, gg = (message[2 * i + slot] for i in range(4))
@@ -176,6 +183,8 @@
             st[2 * slot : 2 * slot + 1, :] = m + jnp.log2(total)
             st[2 * slot + 1 : 2 * slot + 2, :] = delta
             weights = p.astype(BF16)
+            pg[2 * n + slot] = p
+            dpg[2 * n + slot] = dp
             out[rows_of(slot), :] = dot(vh, weights, 0, 0).astype(BF16)
             out[rows_of(2 + slot), :] = dot(kh, (p * (dp - delta)).astype(BF16), 0, 0).astype(BF16)
             out[rows_of(4 + slot), :] = dot(kh, weights, 0, 0).astype(BF16)
@@ -189,17 +198,18 @@
             stats[h, 1:2, span] = stats[h, 1:2, span] * shrink + total_of(p)
             stats[h, 2:3, span] = stats[h, 2:3, span] * shrink + total_of(p * dp)
             ot[h, :, span] = ot[h, :, span] * shrink + dot(vg, p.astype(BF16), 0, 0)
-            kept.append((s, dp, qh, gh))
+            kept.append((s, dp, qh, gh, kg))
     for h in range(2):
         total = stats[h, 1:2, :]
         stats[h, 3:4, :] = stats[h, 0:1, :] + jnp.log2(total)
         stats[h, 4:5, :] = stats[h, 2:3, :] / total
     for partner, out, st in zip(at.partners, (out_a, out_b), (st_a, st_b)):
         for slot, (h, near, free) in enumerate(partner.guests):
-            s, dp, qh, gh = kept.pop(0)
+            s, dp, qh, gh, kg = kept.pop(0)
             p = jnp.exp2(s - stats[h, 3:4, partner.span])
             ds = (p * (dp - stats[h, 4:5, partner.span])).astype(BF16)
             out[rows_of(6 + slot), :] = dot(ds, qh, 1, 0).astype(BF16)
+            aq[h, partner.span, :] += dot(ds, kg, 0, 0)
             out[rows_of(8 + slot), :] = dot(p.astype(BF16), gh, 1, 0).astype(BF16)
         for slot, (h, b) in enumerate(partner.sent):
             st[4 + 2 * slot : 5 + 2 * slot, :] = stats[h, 3:4, rows_of(b)]
@@ -217,9 +227,10 @@
 
 
 def backward_kernel(
-    nb, half, lists, q, k, v, g, in_a, in_b, stats, ot, st_a, st_b, came_a, came_b, *refs
+    nb, half, lists, q, k, v, g, in_a, in_b, stats, ot, st_a, st_b, aq0, pg, dpg, came_a, came_b, *refs
 ):
-    att, aq, ak, av, mix_a, mix_b, fin, ps, dss, got_a, got_b = refs[-11:]
+    att_out, q_out, k_out, v_out, kept, mix_a, mix_b = refs[-16:-9]
+    att, aq, ak, av, fin, ps, dss, got_a, got_b = refs[-9:]
     for came, got in ((came_a, got_a), (came_b, got_b)):
         if half == 0:
             parts = [came[TILES + 8 * i : TILES + 8 * i + 8, :].astype(F32) for i in range(3)]
@@ -242,64 +253,82 @@
             mix[2 * slot + 1 : 2 * slot + 2, :] = delta - part_delta
     for h in range(2):
         cols = lane(h, half)
-        kh, vh = k[:, cols], v[:, cols]
+        kh = k[:, cols]
+        scores, grads = dot(kh, q[:, cols], 1, 1), dot(v[:, cols], g[:, cols], 1, 1)
+        own = ot[h] * jnp.exp2(stats[h, 0:1, :] - fin[h, 0:1, :])
         for a in range(nb):
             rows = rows_of(a)
-            own = ot[h, :, rows] * jnp.exp2(stats[h, 0:1, rows] - fin[h, 0:1, rows])
-            att[h, rows, :] = own.T
-            s = down(dot(kh, q[rows, cols], 1, 1), biases[a])
-            p = jnp.exp2(s - fin[h, 0:1, rows])
+            here = slice(a * BLOCK, (a + 1) * BLOCK)
+            att[h, rows, :] = own[:, here].T
+            p = jnp.exp2(down(scores[:, here], biases[a]) - fin[h, 0:1, rows])
             ps[:, rows] = p.astype(BF16)
-            dss[:, rows] = (p * (dot(vh, g[rows, cols], 1, 1) - fin[h, 1:2, rows])).astype(BF16)
+            dss[:, rows] = (p * (grads[:, here] - fin[h, 1:2, rows])).astype(BF16)
         av[h] = dot(ps[...], g[:, cols], 1, 0)
         ak[h] = dot(dss[...], q[:, cols], 1, 0)
-        aq[h] = dot(dss[...], kh, 0, 0)
-    for partner, message, mine, got in zip(at.partners, (in_a, in_b), (st_a, st_b), (got_a, got_b)):
-        span = partner.span
+        aq[h] = aq0[h] + dot(dss[...], kh, 0, 0)
+    for n, (partner, message, mine, got) in enumerate(
+        zip(at.partners, (in_a, in_b), (st_a, st_b), (got_a, got_b))
+    ):
         for slot, (h, near, free) in enumerate(partner.guests):
-            qg, kg, vg, gg = (message[2 * i + slot] for i in range(4))
-            cols = lane(h, half)
-            qh, kh, vh, gh = (array[span, cols] for array in (q, k, v, g))
+            qg, gg = message[slot], message[6 + slot]
+            part = mine[2 * slot : 2 * slot + 1, :]
             total, delta = merged(
-                mine[2 * slot : 2 * slot + 1, :],
+                part,
                 mine[2 * slot + 1 : 2 * slot + 2, :],
                 got[4 + 2 * slot : 5 + 2 * slot, :],
                 got[5 + 2 * slot : 6 + 2 * slot, :],
             )
-            p = jnp.exp2(down(dot(kh, qg, 1, 1), near) - total)
-            ds = (p * (dot(vh, gg, 1, 1) - delta)).astype(BF16)
-            ak[h, span, :] += dot(ds, qg, 1, 0)
-            av[h, span, :] += dot(p.astype(BF16), gg, 1, 0)
-            p = jnp.exp2(across(dot(kg, qh, 1, 1), free) - fin[h, 0:1, span])
-            ds = (p * (dot(vg, gh, 1, 1) - fin[h, 1:2, span])).astype(BF16)
-            aq[h, span, :] += dot(ds, kg, 0, 0)
-
-
-def finish_kernel(nb, lists, *refs):
-    at = Place(lists, nb)
-    halves = (refs[:8], refs[8:16])
-    att_out, q_out, k_out, v_out, so, sq, sk, sv = refs[16:]
-    for half, (att, aq, ak, av, mix_a, mix_b, back_a, back_b) in enumerate(halves):
-        for total, part in ((so, att), (sq, aq), (sk, ak), (sv, av)):
-            total[...] = part[...]
-        for partner, mix, back in zip(at.partners, (mix_a, mix_b), (back_a, back_b)):
-            for slot, (h, b) in enumerate(partner.sent):
-                rows = rows_of(b)
-                o, u, w, dk, dv = (back[rows_of(2 * i + slot), :].astype(F32) for i in range(5))
-                weight = mix[2 * slot : 2 * slot + 1, :]
-                so[h, rows, :] += (o * weight).T
-                sq[h, rows, :] += ((u - w * mix[2 * slot + 1 : 2 * slot + 2, :]) * weight).T
-                sk[h, rows, :] += dk
-                sv[h, rows, :] += dv
-        for h in range(2):
-            cols = lane(h, half)
-            att_out[:, cols] = so[h].astype(BF16)
-            q_out[:, cols] = (sq[h] * SCALE).astype(BF16)
-            k_out[:, cols] = (sk[h] * SCALE).astype(BF16)
-            v_out[:, cols] = sv[h].astype(BF16)
-
-
-def call(kernel, name, outs, args, scratch=(), flops=0, spaces=None, limit=24 << 20, out=pltpu.VMEM):
+            p = pg[2 * n + slot] * jnp.exp2(part - total)
+            ds = (p * (dpg[2 * n + slot] - delta)).astype(BF16)
+            ak[h, partner.span, :] += dot(ds, qg, 1, 0)
+            av[h, partner.span, :] += dot(p.astype(BF16), gg, 1, 0)
+    for h in range(2):
+        cols = lane(h, 0)
+        att_out[:, cols] = att[h].astype(BF16)
+        q_out[:, cols] = (aq[h] * SCALE).astype(BF16)
+        k_out[:, cols] = (ak[h] * SCALE).astype(BF16)
+        v_out[:, cols] = av[h].astype(BF16)
+    for n, partner in enumerate(at.partners):
+        for slot, (h, b) in enumerate(partner.sent):
+            for i, total in enumerate((att, aq, ak, av)):
+                kept[8 * n + 4 * slot + i] = total[h, rows_of(b), :]
+
+
+def patches(at, kept, mixes, backs):
+    for n, (partner, mix, back) in enumerate(zip(at.partners, mixes, backs)):
+        for slot, (h, b) in enumerate(partner.sent):
+            o, u, w, dk, dv = (back[rows_of(2 * i + slot), :].astype(F32) for i in range(5))
+            weight = mix[2 * slot : 2 * slot + 1, :]
+            more = mix[2 * slot + 1 : 2 * slot + 2, :]
+            whole = ((o * weight).T, ((u - w * more) * weight).T, dk, dv)
+            for i, scale in enumerate((1.0, SCALE, SCALE, 1.0)):
+                yield h, b, i, ((kept[8 * n + 4 * slot + i] + whole[i]) * scale).astype(BF16)
+
+
+def finish_first_kernel(nb, lists, *refs):
+    at = Place(lists, nb)
+    parts, kept, mixes, backs, others, outs = refs[:4], refs[4], refs[5:7], refs[7:9], refs[9:13], refs[13:17]
+    for out, part, other in zip(outs, parts, others):
+        out[:, : 2 * HD] = part[...]
+        out[:, 2 * HD :] = other[...]
+    for h, b, i, value in patches(at, kept, mixes, backs):
+        outs[i][rows_of(b), lane(h, 0)] = value
+
+
+def finish_second_kernel(nb, lists, *refs):
+    at = Place(lists, nb)
+    kept, mixes, backs, outs, tiles, sems = refs[4], refs[5:7], refs[7:9], refs[9:13], refs[13], refs[14]
+    copies = []
+    for h, b, i, value in patches(at, kept, mixes, backs):
+        n = len(copies)
+        tiles[n] = value
+        copies.append(pltpu.make_async_copy(tiles.at[n], outs[i].at[rows_of(b), lane(h, 1)], sems.at[n]))
+        copies[-1].start()
+    for copy in copies:
+        copy.wait()
+
+
+def call(kernel, name, outs, args, scratch=(), flops=0, spaces=None, limit=24 << 20, out=pltpu.VMEM, aliases=None):
     moved = sum(math.prod(s.shape) * s.dtype.itemsize for s in (*outs, *args))
     spaces = spaces or (pltpu.SMEM,) + (pltpu.VMEM,) * (len(args) - 1)
     return pl.pallas_call(
@@ -308,6 +337,7 @@
         in_specs=[pl.BlockSpec(memory_space=space) for space in spaces],
         out_specs=tuple([pl.BlockSpec(memory_space=out)] * len(outs)),
         scratch_shapes=scratch,
+        input_output_aliases=aliases or {},
         cost_estimate=pl.CostEstimate(flops=flops, bytes_accessed=moved if flops else 1, transcendentals=0),
         compiler_params=pltpu.CompilerParams(vmem_limit_bytes=limit),
         name=name,
@@ -334,41 +364,55 @@
     st, acc = sds((8, HD), F32), sds((2, rows, HD), F32)
     first = call(
         functools.partial(pack_kernel, nb), "pack", [tile8] * 2, arrays,
-        scratch=(pltpu.SemaphoreType.DMA((16,)),), spaces=(pltpu.SMEM,) + (pl.ANY,) * 4, limit=60 << 20,
+        scratch=(pltpu.VMEM((16, BLOCK, HD), BF16), pltpu.SemaphoreType.DMA((2, 16))),
+        spaces=(pltpu.SMEM,) + (pl.ANY,) * 4, limit=60 << 20, out=pl.ANY,
     )
     guests = [swap(*first)]
     stats0, ot0, *second = call(
         functools.partial(own_forward_kernel, nb), "own_forward",
         [sds((HEADS, 8, rows), F32), sds((HEADS, HD, rows), F32), tile8, tile8], arrays, flops=6 << 30,
+        scratch=(pltpu.VMEM((rows, rows), BF16),),
     )
     guests.append(swap(*second))
     forward, backs = [], []
     for half in range(2):
         result = sds((TILES + 32 * (1 - half), HD), BF16)
-        *kept, out_a, out_b, st_a, st_b = call(
+        span = (4, 3 * BLOCK, BLOCK)
+        *kept, out_a, out_b, st_a, st_b, aq, pg, dpg = call(
             functools.partial(guest_kernel, nb, half), "guest",
-            [sds((2, 8, rows), F32), sds((2, HD, rows), F32), result, result, st, st],
+            [
+                sds((2, 8, rows), F32), sds((2, HD, rows), F32), result, result, st, st,
+                acc, sds(span, F32), sds(span, F32),
+            ],
             (*arrays, *guests[half], stats0, ot0), flops=4 << 30,
         )
         got = () if half == 0 else swap(st_a, st_b)
         backs.append(swap(out_a, out_b))
-        forward.append((*kept, st_a, st_b, *(got or backs[0])))
+        forward.append((*kept, st_a, st_b, aq, pg, dpg, *(got or backs[0])))
     pieces, outs = [], ()
     for half in range(2):
         after = outs[-2:]
         outs = call(
-            functools.partial(backward_kernel, nb, half), "backward", [acc] * 4 + [st] * 2,
+            functools.partial(backward_kernel, nb, half), "backward",
+            [sds((rows, 2 * HD), BF16)] * 4 + [sds((16, BLOCK, HD), F32), st, st],
             (*arrays, *guests[half], *forward[half], *after),
             scratch=(
-                pltpu.VMEM((2, 8, rows), F32), pltpu.VMEM((rows, rows), BF16), pltpu.VMEM((rows, rows), BF16),
+                *(pltpu.VMEM((2, rows, HD), F32) for _ in range(4)), pltpu.VMEM((2, 8, rows), F32),
+                pltpu.VMEM((rows, rows), BF16), pltpu.VMEM((rows, rows), BF16),
                 pltpu.VMEM((8, HD), F32), pltpu.VMEM((8, HD), F32),
             ), flops=(40 << 30, 1 << 30)[half],
-            spaces=(pltpu.SMEM,) + (pltpu.VMEM,) * 12 + (pl.ANY,) * len(after),
+            spaces=(pltpu.SMEM,) + (pltpu.VMEM,) * 15 + (pl.ANY,) * len(after),
         )
-        pieces += [*outs, *backs[half]]
+        pieces.append((*outs, *backs[half]))
+    whole = [sds((rows, width), BF16)] * 4
+    outs = call(
+        functools.partial(finish_first_kernel, nb), "finish_first", whole, (lists, *pieces[0], *pieces[1][:4])
+    )
     return call(
-        functools.partial(finish_kernel, nb), "finish", [sds((rows, width), BF16)] * 4, (lists, *pieces),
-        scratch=tuple(pltpu.VMEM((2, rows, HD), F32) for _ in range(4)),
+        functools.partial(finish_second_kernel, nb), "finish_second", whole, (lists, *outs, *pieces[1][4:]),
+        scratch=(pltpu.VMEM((16, BLOCK, HD), BF16), pltpu.SemaphoreType.DMA((16,))),
+        spaces=(pltpu.SMEM,) + (pl.ANY,) * 4 + (pltpu.VMEM,) * 5, out=pl.ANY,
+        aliases={i + 1: i for i in range(4)},
     )
 
 

time: 61.7 us -> 60.2 us (0.976)
  the two profiles are of different devices: /device:TPU:8 before, /device:TPU:2 now
where the time goes in v4:
time: 60.2 us; the launch traced here: 60 us
  Pallas kernels  23.2 us (39%)
  starting transfers between devices  19.7 us (33%)
  waiting for transfers between devices  16 us (27%)
  between operations  1.01 us (2%)
    pallas_call x8, Pallas kernels, call(): pl.pallas_call(kernel, out_shape=tuple(outs), in_specs=[pl.BlockSpec(memo...  23.2 us
    ppermute x5, starting transfers between devices, swap(): lax.ppermute(to_b, 'seq', pairs(1))  19.4 us
    ppermute x5, waiting for transfers between devices, swap(): lax.ppermute(to_a, 'seq', pairs(0))  15 us
  transfers between devices with their start and end apart: 10, of which 5 were waited for; matrix products, arithmetic and copies ran while one was open for 0% of the time, Pallas kernels for 31%

profile of v4, /device:TPU:2, one launch (start us, length us, event | category | flops | bytes accessed | tf_op | source)
XLA Modules:
  0.0 60.0 jit_solution(8948058037150680383)
XLA Ops:
  0.6 0.0 copy-start
  0.6 0.0 copy-start.1
  0.7 0.0 copy-start.2
  0.7 0.0 copy-start.3
  0.7 2.8 %pack.1 = (bf16[8,128,128]{2,1,0:T(8,128)(2,1)}, bf16[8,128,128]{2,1,0:T(8,128)(2,1)}) custom-call(s32[4,6]{1,0:T(4,128)} %lists.15, bf16[512,512]{1,0:T(8,128)(2,1)} %q.11, bf16[512,512]{1,0:T(8,128)(2,1)} %k.11, bf16[512,512]{1,0:T(8,128)(2,1)} %v.11, bf16[512,512]{1,0:T(8,128)(2,1)} %g.11), custom_call_target="tpu_custom_call" | custom-call | bytes 1 | tf_op jit(solution)/shard_map/pack/pallas_call | solution.py:334
  3.4 0.0 copy-start.4
  3.5 0.1 collective-permute-start
  3.5 4.9 %collective-permute-start.1 = (bf16[8,128,128]{2,1,0:T(8,128)(2,1)}, bf16[8,128,128]{2,1,0:T(8,128)(2,1)S(1)}, u32[]{:S(2)}, u32[]{:S(2)}) collective-permute-start(bf16[8,128,128]{2,1,0:T(8,128)(2,1)} %get-tuple-element.47), channel_id=1, source_target_pairs={{1,2},{2,1},{3,4},{4,3},{5,6},{6,5},{7,8},{8,7},{9,10},{10,9},{11,... | collective-permute-start | bytes 786440 | tf_op jit(solution)/shard_map/ppermute | solution.py:360
  8.4 0.0 copy-done
  8.4 0.0 copy-done.1
  8.4 0.0 copy-done.2
  8.4 0.0 copy-done.3
  8.4 0.0 copy-done.4
  8.5 3.1 %own_forward.1 = (f32[4,8,512]{2,1,0:T(8,128)S(1)}, f32[4,128,512]{2,1,0:T(8,128)S(1)}, bf16[8,128,128]{2,1,0:T(8,128)(2,1)S(1)}, bf16[8,128,128]{2,1,0:T(8,128)(2,1)S(1)}) custom-call(s32[4,6]{1,0:T(4,128)S(1)} %copy-done.4, bf16[512,512]{1,0:T(8,128)(2,1)S(1)} %copy-done, bf16[512,512]{1,0:T(8,128)(2,1)S(1)} %copy-done.1, bf16[512,512]{1,0:T(8,128)(2,1)S(1)} %copy-done.2, ...), custom_call_target="tpu_custom_call" | custom-call | flops 6442450944 | bytes 3735648 | tf_op jit(solution)/shard_map/own_forward/pallas_call | solution.py:334
  11.6 0.1 collective-permute-start.4
  11.6 4.9 %collective-permute-start.5 = (bf16[8,128,128]{2,1,0:T(8,128)(2,1)S(1)}, bf16[8,128,128]{2,1,0:T(8,128)(2,1)S(1)}, u32[]{:S(2)}, u32[]{:S(2)}) collective-permute-start(bf16[8,128,128]{2,1,0:T(8,128)(2,1)S(1)} %get-tuple-element.67), channel_id=1, source_target_pairs={{1,2},{2,1},{3,4},{4,3},{5,6},{6,5},{7,8},{8,7},{9,10},{10,9},{11,... | collective-permute-start | bytes 786440 | tf_op jit(solution)/shard_map/ppermute | solution.py:360
  16.5 7.7 %collective-permute-done.in_a = bf16[8,128,128]{2,1,0:T(8,128)(2,1)S(1)} collective-permute-done((bf16[8,128,128]{2,1,0:T(8,128)(2,1)}, bf16[8,128,128]{2,1,0:T(8,128)(2,1)S(1)}, u32[]{:S(2)}, u32[]{:S(2)}) %collective-permute-start) | collective-permute-done | bytes 262176 | tf_op jit(solution)/shard_map/ppermute | solution.py:360
  24.2 0.0 collective-permute-done.1.in_b
  24.2 3.9 %guest.2 = (f32[2,8,512]{2,1,0:T(8,128)S(1)}, f32[2,128,512]{2,1,0:T(8,128)S(1)}, bf16[1312,128]{1,0:T(8,128)(2,1)S(1)}, bf16[1312,128]{1,0:T(8,128)(2,1)S(1)}, ...) custom-call(s32[4,6]{1,0:T(4,128)S(1)} %copy-done.4, ...), custom_call_target="tpu_custom_call" | custom-call | flops 4294967296 | bytes 7069792 | tf_op jit(solution)/shard_map/guest/pallas_call | solution.py:334
  28.1 0.1 collective-permute-start.2
  28.1 1.9 %collective-permute-start.3 = (bf16[1312,128]{1,0:T(8,128)(2,1)S(1)}, bf16[1312,128]{1,0:T(8,128)(2,1)S(1)}, u32[]{:S(2)}, u32[]{:S(2)}) collective-permute-start(bf16[1312,128]{1,0:T(8,128)(2,1)S(1)} %get-tuple-element.58), channel_id=1, source_target_pairs={{1,2},{2,1},{3,4},{4,3},{5,6},{6,5},{7,8},{8,7},{9,10},{10,9},{11,... | collective-permute-start | bytes 1007624 | tf_op jit(solution)/shard_map/ppermute | solution.py:360
  30.1 3.3 %collective-permute-done.4.in_a = bf16[8,128,128]{2,1,0:T(8,128)(2,1)S(1)} collective-permute-done((bf16[8,128,128]{2,1,0:T(8,128)(2,1)S(1)}, bf16[8,128,128]{2,1,0:T(8,128)(2,1)S(1)}, u32[]{:S(2)}, u32[]{:S(2)}) %collective-permute-start.4) | collective-permute-done | bytes 262176 | tf_op jit(solution)/shard_map/ppermute | solution.py:360
  33.4 0.0 collective-permute-done.5.in_b
  33.4 3.9 %guest.3 = (f32[2,8,512]{2,1,0:T(8,128)S(1)}, f32[2,128,512]{2,1,0:T(8,128)S(1)}, bf16[1280,128]{1,0:T(8,128)(2,1)S(1)}, bf16[1280,128]{1,0:T(8,128)(2,1)S(1)}, ...) custom-call(s32[4,6]{1,0:T(4,128)S(1)} %copy-done.4, ...), custom_call_target="tpu_custom_call" | custom-call | flops 4294967296 | bytes 7053408 | tf_op jit(solution)/shard_map/guest/pallas_call | solution.py:334
  37.3 0.1 collective-permute-start.6
  37.4 4.5 %collective-permute-start.7 = (f32[8,128]{1,0:T(8,128)S(1)}, f32[8,128]{1,0:T(8,128)S(1)}, u32[]{:S(2)}, u32[]{:S(2)}) collective-permute-start(f32[8,128]{1,0:T(8,128)S(1)} %get-tuple-element.71.st_b), channel_id=1, source_target_pairs={{1,2},{2,1},{3,4},{4,3},{5,6},{6,5},{7,8},{8,7},{9,10},{10,9},{11,... | collective-permute-start | bytes 12296 | tf_op jit(solution)/shard_map/ppermute | solution.py:360
  41.9 0.1 collective-permute-start.8
  42.0 2.2 %collective-permute-done.2.came_a.refs_7_ = bf16[1312,128]{1,0:T(8,128)(2,1)S(1)} collective-permute-done((bf16[1312,128]{1,0:T(8,128)(2,1)S(1)}, bf16[1312,128]{1,0:T(8,128)(2,1)S(1)}, u32[]{:S(2)}, u32[]{:S(2)}) %collective-permute-start.2) | collective-permute-done | bytes 335904 | tf_op jit(solution)/shard_map/ppermute | solution.py:360
  44.2 3.2 %collective-permute-start.9 = (bf16[1280,128]{1,0:T(8,128)(2,1)S(1)}, bf16[1280,128]{1,0:T(8,128)(2,1)S(1)}, u32[]{:S(2)}, u32[]{:S(2)}) collective-permute-start(bf16[1280,128]{1,0:T(8,128)(2,1)S(1)} %get-tuple-element.87), channel_id=1, source_target_pairs={{1,2},{2,1},{3,4},{4,3},{5,6},{6,5},{7,8},{8,7},{9,10},{10,9},{11,... | collective-permute-start | bytes 983048 | tf_op jit(solution)/shard_map/ppermute | solution.py:360
  47.4 0.0 collective-permute-done.3.came_b.refs_8_
  47.4 2.9 %backward.2 = (bf16[512,256]{1,0:T(8,128)(2,1)S(1)}, bf16[512,256]{1,0:T(8,128)(2,1)S(1)}, bf16[512,256]{1,0:T(8,128)(2,1)S(1)}, bf16[512,256]{1,0:T(8,128)(2,1)...) custom-call(s32[4,6]{1,0:T(4,128)S(1)} %copy-done.4, bf16[512,512]{1,0:T(8,128)(2,1)S(1)} %copy-done, ...), custom_call_target="tpu_custom_call" | custom-call | flops 42949672960 | bytes 8061024 | tf_op jit(solution)/shard_map/backward/pallas_call | solution.py:334
  50.3 0.0 collective-permute-done.6.came_a
  50.3 0.0 collective-permute-done.7.came_b
  50.3 2.9 %backward.3 = (bf16[512,256]{1,0:T(8,128)(2,1)S(1)}, bf16[512,256]{1,0:T(8,128)(2,1)S(1)}, bf16[512,256]{1,0:T(8,128)(2,1)S(1)}, bf16[512,256]{1,0:T(8,128)(2,1)...) custom-call(s32[4,6]{1,0:T(4,128)S(1)} %copy-done.4, bf16[512,512]{1,0:T(8,128)(2,1)S(1)} %copy-done, ...), custom_call_target="tpu_custom_call" | custom-call | flops 1073741824 | bytes 7405664 | tf_op jit(solution)/shard_map/backward/pallas_call | solution.py:334
  53.2 2.2 %finish_first.1 = (bf16[512,512]{1,0:T(8,128)(2,1)}, bf16[512,512]{1,0:T(8,128)(2,1)}, bf16[512,512]{1,0:T(8,128)(2,1)}, bf16[512,512]{1,0:T(8,128)(2,1)}) custom-call(s32[4,6]{1,0:T(4,128)S(1)} %copy-done.4, bf16[512,256]{1,0:T(8,128)(2,1)S(1)} %get-tuple-element.59.refs_0_, bf16[512,256]{1,0:T(8,128)(2,1)S(1)} %get-tuple-element.60.refs_1_, ...), custom_call_target="tpu_custom_call" | custom-call | bytes 1 | tf_op jit(solution)/shard_map/finish_first/pallas_call | solution.py:334
  55.4 1.8 %collective-permute-done.8.refs_7_ = bf16[1280,128]{1,0:T(8,128)(2,1)S(1)} collective-permute-done((bf16[1280,128]{1,0:T(8,128)(2,1)S(1)}, bf16[1280,128]{1,0:T(8,128)(2,1)S(1)}, u32[]{:S(2)}, u32[]{:S(2)}) %collective-permute-start.8) | collective-permute-done | bytes 327712 | tf_op jit(solution)/shard_map/ppermute | solution.py:360
  57.2 1.0 %collective-permute-done.9.refs_8_ = bf16[1280,128]{1,0:T(8,128)(2,1)S(1)} collective-permute-done((bf16[1280,128]{1,0:T(8,128)(2,1)S(1)}, bf16[1280,128]{1,0:T(8,128)(2,1)S(1)}, u32[]{:S(2)}, u32[]{:S(2)}) %collective-permute-start.9) | collective-permute-done | bytes 327712 | tf_op jit(solution)/shard_map/ppermute | solution.py:360
  58.2 1.6 %finish_second.1 = (bf16[512,512]{1,0:T(8,128)(2,1)}, bf16[512,512]{1,0:T(8,128)(2,1)}, bf16[512,512]{1,0:T(8,128)(2,1)}, bf16[512,512]{1,0:T(8,128)(2,1)}) custom-call(s32[4,6]{1,0:T(4,128)S(1)} %copy-done.4, bf16[512,512]{1,0:T(8,128)(2,1)} %get-tuple-element.79.refs_0_, ...), custom_call_target="tpu_custom_call", output_to_operand_aliasing={{0}: (1, {}), {1}: (2, {}), {2}: (3, {}), {3}: (4, {})} | custom-call | bytes 1 | tf_op jit(solution)/shard_map/finish_second/pallas_call | solution.py:334
Async XLA Ops:
  0.6 7.8 %copy-start = (bf16[512,512]{1,0:T(8,128)(2,1)S(1)}, bf16[512,512]{1,0:T(8,128)(2,1)}, u32[]{:S(2)}) copy-start(bf16[512,512]{1,0:T(8,128)(2,1)} %q.11) | copy-start | bytes 1572868
  0.6 7.8 %copy-start.1 = (bf16[512,512]{1,0:T(8,128)(2,1)S(1)}, bf16[512,512]{1,0:T(8,128)(2,1)}, u32[]{:S(2)}) copy-start(bf16[512,512]{1,0:T(8,128)(2,1)} %k.11) | copy-start | bytes 1572868
  0.7 7.8 %copy-start.2 = (bf16[512,512]{1,0:T(8,128)(2,1)S(1)}, bf16[512,512]{1,0:T(8,128)(2,1)}, u32[]{:S(2)}) copy-start(bf16[512,512]{1,0:T(8,128)(2,1)} %v.11) | copy-start | bytes 1572868
  0.7 7.8 %copy-start.3 = (bf16[512,512]{1,0:T(8,128)(2,1)S(1)}, bf16[512,512]{1,0:T(8,128)(2,1)}, u32[]{:S(2)}) copy-start(bf16[512,512]{1,0:T(8,128)(2,1)} %g.11) | copy-start | bytes 1572868
  3.4 5.0 %copy-start.4 = (s32[4,6]{1,0:T(4,128)S(1)}, s32[4,6]{1,0:T(4,128)}, u32[]{:S(2)}) copy-start(s32[4,6]{1,0:T(4,128)} %lists.15) | copy-start | bytes 292
  3.5 20.7 %collective-permute-start = (bf16[8,128,128]{2,1,0:T(8,128)(2,1)}, bf16[8,128,128]{2,1,0:T(8,128)(2,1)S(1)}, u32[]{:S(2)}, u32[]{:S(2)}) collective-permute-start(bf16[8,128,128]{2,1,0:T(8,128)(2,1)} %get-tuple-element.46), channel_id=1, source_target_pairs={{0,1},{1,0},{2,3},{3,2},{4,5},{5,4},{6,7},{7,6},{8,9},{9,8},{10,11... | collective-permute-start | bytes 786440 | tf_op jit(solution)/shard_map/ppermute | solution.py:360
  3.5 20.6 %collective-permute-start.1 = (bf16[8,128,128]{2,1,0:T(8,128)(2,1)}, bf16[8,128,128]{2,1,0:T(8,128)(2,1)S(1)}, u32[]{:S(2)}, u32[]{:S(2)}) collective-permute-start(bf16[8,128,128]{2,1,0:T(8,128)(2,1)} %get-tuple-element.47), channel_id=1, source_target_pairs={{1,2},{2,1},{3,4},{4,3},{5,6},{6,5},{7,8},{8,7},{9,10},{10,9},{11,... | collective-permute-start | bytes 786440 | tf_op jit(solution)/shard_map/ppermute | solution.py:360
  11.6 21.8 %collective-permute-start.4 = (bf16[8,128,128]{2,1,0:T(8,128)(2,1)S(1)}, bf16[8,128,128]{2,1,0:T(8,128)(2,1)S(1)}, u32[]{:S(2)}, u32[]{:S(2)}) collective-permute-start(bf16[8,128,128]{2,1,0:T(8,128)(2,1)S(1)} %get-tuple-element.66), channel_id=1, source_target_pairs={{0,1},{1,0},{2,3},{3,2},{4,5},{5,4},{6,7},{7,6},{8,9},{9,8},{10,11... | collective-permute-start | bytes 786440 | tf_op jit(solution)/shard_map/ppermute | solution.py:360
  11.6 21.7 %collective-permute-start.5 = (bf16[8,128,128]{2,1,0:T(8,128)(2,1)S(1)}, bf16[8,128,128]{2,1,0:T(8,128)(2,1)S(1)}, u32[]{:S(2)}, u32[]{:S(2)}) collective-permute-start(bf16[8,128,128]{2,1,0:T(8,128)(2,1)S(1)} %get-tuple-element.67), channel_id=1, source_target_pairs={{1,2},{2,1},{3,4},{4,3},{5,6},{6,5},{7,8},{8,7},{9,10},{10,9},{11,... | collective-permute-start | bytes 786440 | tf_op jit(solution)/shard_map/ppermute | solution.py:360
  28.1 16.2 %collective-permute-start.2 = (bf16[1312,128]{1,0:T(8,128)(2,1)S(1)}, bf16[1312,128]{1,0:T(8,128)(2,1)S(1)}, u32[]{:S(2)}, u32[]{:S(2)}) collective-permute-start(bf16[1312,128]{1,0:T(8,128)(2,1)S(1)} %get-tuple-element.57), channel_id=1, source_target_pairs={{0,1},{1,0},{2,3},{3,2},{4,5},{5,4},{6,7},{7,6},{8,9},{9,8},{10,11... | collective-permute-start | bytes 1007624 | tf_op jit(solution)/shard_map/ppermute | solution.py:360
  28.1 19.2 %collective-permute-start.3 = (bf16[1312,128]{1,0:T(8,128)(2,1)S(1)}, bf16[1312,128]{1,0:T(8,128)(2,1)S(1)}, u32[]{:S(2)}, u32[]{:S(2)}) collective-permute-start(bf16[1312,128]{1,0:T(8,128)(2,1)S(1)} %get-tuple-element.58), channel_id=1, source_target_pairs={{1,2},{2,1},{3,4},{4,3},{5,6},{6,5},{7,8},{8,7},{9,10},{10,9},{11,... | collective-permute-start | bytes 1007624 | tf_op jit(solution)/shard_map/ppermute | solution.py:360
  37.3 13.0 %collective-permute-start.6 = (f32[8,128]{1,0:T(8,128)S(1)}, f32[8,128]{1,0:T(8,128)S(1)}, u32[]{:S(2)}, u32[]{:S(2)}) collective-permute-start(f32[8,128]{1,0:T(8,128)S(1)} %get-tuple-element.70.st_a), channel_id=1, source_target_pairs={{0,1},{1,0},{2,3},{3,2},{4,5},{5,4},{6,7},{7,6},{8,9},{9,8},{10,11... | collective-permute-start | bytes 12296 | tf_op jit(solution)/shard_map/ppermute | solution.py:360
  37.4 13.0 %collective-permute-start.7 = (f32[8,128]{1,0:T(8,128)S(1)}, f32[8,128]{1,0:T(8,128)S(1)}, u32[]{:S(2)}, u32[]{:S(2)}) collective-permute-start(f32[8,128]{1,0:T(8,128)S(1)} %get-tuple-element.71.st_b), channel_id=1, source_target_pairs={{1,2},{2,1},{3,4},{4,3},{5,6},{6,5},{7,8},{8,7},{9,10},{10,9},{11,... | collective-permute-start | bytes 12296 | tf_op jit(solution)/shard_map/ppermute | solution.py:360
  41.9 15.3 %collective-permute-start.8 = (bf16[1280,128]{1,0:T(8,128)(2,1)S(1)}, bf16[1280,128]{1,0:T(8,128)(2,1)S(1)}, u32[]{:S(2)}, u32[]{:S(2)}) collective-permute-start(bf16[1280,128]{1,0:T(8,128)(2,1)S(1)} %get-tuple-element.86), channel_id=1, source_target_pairs={{0,1},{1,0},{2,3},{3,2},{4,5},{5,4},{6,7},{7,6},{8,9},{9,8},{10,11... | collective-permute-start | bytes 983048 | tf_op jit(solution)/shard_map/ppermute | solution.py:360
  44.2 14.0 %collective-permute-start.9 = (bf16[1280,128]{1,0:T(8,128)(2,1)S(1)}, bf16[1280,128]{1,0:T(8,128)(2,1)S(1)}, u32[]{:S(2)}, u32[]{:S(2)}) collective-permute-start(bf16[1280,128]{1,0:T(8,128)(2,1)S(1)} %get-tuple-element.87), channel_id=1, source_target_pairs={{1,2},{2,1},{3,4},{4,3},{5,6},{6,5},{7,8},{8,7},{9,10},{10,9},{11,... | collective-permute-start | bytes 983048 | tf_op jit(solution)/shard_map/ppermute | solution.py:360

commit v5 on v4

--- a/solution.py
+++ b/solution.py
@@ -154,7 +154,7 @@
     return parts
 
 
-TILES = 10 * BLOCK
+TILES = 6 * BLOCK
 
 
 def guest_kernel(nb, half, lists, q, k, v, g, in_a, in_b, stats0, ot0,
@@ -186,37 +186,37 @@
             pg[2 * n + slot] = p
             dpg[2 * n + slot] = dp
             out[rows_of(slot), :] = dot(vh, weights, 0, 0).astype(BF16)
-            out[rows_of(2 + slot), :] = dot(kh, (p * (dp - delta)).astype(BF16), 0, 0).astype(BF16)
-            out[rows_of(4 + slot), :] = dot(kh, weights, 0, 0).astype(BF16)
             s = across(dot(kg, qh, 1, 1), free)
-            old = stats[h, 0:1, span]
-            m = jnp.maximum(old, jnp.max(s, axis=0, keepdims=True))
-            shrink = jnp.exp2(old - m)
-            p = jnp.exp2(s - m)
+            top = jnp.max(s, axis=0, keepdims=True)
+            p = jnp.exp2(s - top)
             dp = dot(vg, gh, 1, 1)
-            stats[h, 0:1, span] = m
-            stats[h, 1:2, span] = stats[h, 1:2, span] * shrink + total_of(p)
-            stats[h, 2:3, span] = stats[h, 2:3, span] * shrink + total_of(p * dp)
-            ot[h, :, span] = ot[h, :, span] * shrink + dot(vg, p.astype(BF16), 0, 0)
-            kept.append((s, dp, qh, gh, kg))
+            sums = top, total_of(p), total_of(p * dp), dot(vg, p.astype(BF16), 0, 0)
+            kept.append((h, partner.span, sums, s, dp, qh, gh, kg))
+    for h, span, (top, count, product, out), *_ in kept:
+        old = stats[h, 0:1, span]
+        m = jnp.maximum(old, top)
+        shrink, grow = jnp.exp2(old - m), jnp.exp2(top - m)
+        stats[h, 0:1, span] = m
+        stats[h, 1:2, span] = stats[h, 1:2, span] * shrink + count * grow
+        stats[h, 2:3, span] = stats[h, 2:3, span] * shrink + product * grow
+        ot[h, :, span] = ot[h, :, span] * shrink + out * grow
     for h in range(2):
         total = stats[h, 1:2, :]
         stats[h, 3:4, :] = stats[h, 0:1, :] + jnp.log2(total)
         stats[h, 4:5, :] = stats[h, 2:3, :] / total
     for partner, out, st in zip(at.partners, (out_a, out_b), (st_a, st_b)):
         for slot, (h, near, free) in enumerate(partner.guests):
-            s, dp, qh, gh, kg = kept.pop(0)
+            *_, s, dp, qh, gh, kg = kept.pop(0)
             p = jnp.exp2(s - stats[h, 3:4, partner.span])
             ds = (p * (dp - stats[h, 4:5, partner.span])).astype(BF16)
-            out[rows_of(6 + slot), :] = dot(ds, qh, 1, 0).astype(BF16)
+            out[rows_of(2 + slot), :] = dot(ds, qh, 1, 0).astype(BF16)
             aq[h, partner.span, :] += dot(ds, kg, 0, 0)
-            out[rows_of(8 + slot), :] = dot(p.astype(BF16), gh, 1, 0).astype(BF16)
+            out[rows_of(4 + slot), :] = dot(p.astype(BF16), gh, 1, 0).astype(BF16)
         for slot, (h, b) in enumerate(partner.sent):
             st[4 + 2 * slot : 5 + 2 * slot, :] = stats[h, 3:4, rows_of(b)]
             st[5 + 2 * slot : 6 + 2 * slot, :] = stats[h, 4:5, rows_of(b)]
-        if half == 0:
-            for i, part in enumerate(split(st[...])):
-                out[TILES + 8 * i : TILES + 8 * i + 8, :] = part
+        for i, part in enumerate(split(st[...])):
+            out[TILES + 8 * i : TILES + 8 * i + 8, :] = part
 
 
 def merged(l1, d1, l2, d2):
@@ -226,31 +226,58 @@
     return m + jnp.log2(total), (w1 * d1 + w2 * d2) / total
 
 
+def arrived(came):
+    parts = [came[TILES + 8 * i : TILES + 8 * i + 8, :].astype(F32) for i in range(3)]
+    return parts[0] + (parts[1] + parts[2])
+
+
+def whole_guest(slot, mine, got):
+    part = mine[2 * slot : 2 * slot + 1, :]
+    total, delta = merged(
+        part,
+        mine[2 * slot + 1 : 2 * slot + 2, :],
+        got[4 + 2 * slot : 5 + 2 * slot, :],
+        got[5 + 2 * slot : 6 + 2 * slot, :],
+    )
+    return jnp.exp2(part - total), delta
+
+
+def return_kernel(nb, half, lists, k, st_a, st_b, pg, dpg, came_a, came_b, *refs):
+    back_a, back_b, got_a, got_b = refs[-4:]
+    at = Place(lists, nb)
+    got_a[...], got_b[...] = arrived(came_a), arrived(came_b)
+    for n, (partner, mine, got, back) in enumerate(
+        zip(at.partners, (st_a, st_b), (got_a, got_b), (back_a, back_b))
+    ):
+        if half == 1:
+            back[: 2 * BLOCK, :] = refs[n][...]
+        for slot, (h, near, free) in enumerate(partner.guests):
+            shrink, delta = whole_guest(slot, mine, got)
+            ds = (pg[2 * n + slot] * shrink * (dpg[2 * n + slot] - delta)).astype(BF16)
+            back[rows_of(2 * half + slot), :] = dot(ds, k[partner.span, lane(h, half)], 0, 0).astype(BF16)
+
+
 def backward_kernel(
     nb, half, lists, q, k, v, g, in_a, in_b, stats, ot, st_a, st_b, aq0, pg, dpg, came_a, came_b, *refs
 ):
-    att_out, q_out, k_out, v_out, kept, mix_a, mix_b = refs[-16:-9]
-    att, aq, ak, av, fin, ps, dss, got_a, got_b = refs[-9:]
-    for came, got in ((came_a, got_a), (came_b, got_b)):
-        if half == 0:
-            parts = [came[TILES + 8 * i : TILES + 8 * i + 8, :].astype(F32) for i in range(3)]
-            got[...] = parts[0] + (parts[1] + parts[2])
-        else:
-            got[...] = came[...]
+    outs, kept = refs[-16:-12], refs[-12]
+    att, aq, ak, av, fin, ps, dss, got_a, got_b, staged, sems = refs[-11:]
+    got_a[...], got_b[...] = arrived(came_a), arrived(came_b)
     at = Place(lists, nb)
     biases = at.biases()
     fin[:, 0:2, :] = stats[:, 3:5, :]
-    for partner, got, mix in zip(at.partners, (got_a, got_b), (mix_a, mix_b)):
+    weights = []
+    for partner, got in zip(at.partners, (got_a, got_b)):
         gone = bias_of(partner.there)
         for slot, (h, b) in enumerate(partner.sent):
             rows = rows_of(b)
             part = got[2 * slot : 2 * slot + 1, :] + gone
-            part_delta = got[2 * slot + 1 : 2 * slot + 2, :]
-            total, delta = merged(fin[h, 0:1, rows], fin[h, 1:2, rows], part, part_delta)
+            total, delta = merged(
+                fin[h, 0:1, rows], fin[h, 1:2, rows], part, got[2 * slot + 1 : 2 * slot + 2, :]
+            )
             fin[h, 0:1, rows] = total
             fin[h, 1:2, rows] = delta
-            mix[2 * slot : 2 * slot + 1, :] = jnp.exp2(part - total)
-            mix[2 * slot + 1 : 2 * slot + 2, :] = delta - part_delta
+            weights.append(jnp.exp2(part - total))
     for h in range(2):
         cols = lane(h, half)
         kh = k[:, cols]
@@ -271,59 +298,43 @@
     ):
         for slot, (h, near, free) in enumerate(partner.guests):
             qg, gg = message[slot], message[6 + slot]
-            part = mine[2 * slot : 2 * slot + 1, :]
-            total, delta = merged(
-                part,
-                mine[2 * slot + 1 : 2 * slot + 2, :],
-                got[4 + 2 * slot : 5 + 2 * slot, :],
-                got[5 + 2 * slot : 6 + 2 * slot, :],
-            )
-            p = pg[2 * n + slot] * jnp.exp2(part - total)
+            shrink, delta = whole_guest(slot, mine, got)
+            p = pg[2 * n + slot] * shrink
             ds = (p * (dpg[2 * n + slot] - delta)).astype(BF16)
             ak[h, partner.span, :] += dot(ds, qg, 1, 0)
             av[h, partner.span, :] += dot(p.astype(BF16), gg, 1, 0)
-    for h in range(2):
-        cols = lane(h, 0)
-        att_out[:, cols] = att[h].astype(BF16)
-        q_out[:, cols] = (aq[h] * SCALE).astype(BF16)
-        k_out[:, cols] = (ak[h] * SCALE).astype(BF16)
-        v_out[:, cols] = av[h].astype(BF16)
-    for n, partner in enumerate(at.partners):
+    for n, (partner, came) in enumerate(zip(at.partners, (came_a, came_b))):
         for slot, (h, b) in enumerate(partner.sent):
-            for i, total in enumerate((att, aq, ak, av)):
-                kept[8 * n + 4 * slot + i] = total[h, rows_of(b), :]
-
-
-def patches(at, kept, mixes, backs):
-    for n, (partner, mix, back) in enumerate(zip(at.partners, mixes, backs)):
-        for slot, (h, b) in enumerate(partner.sent):
-            o, u, w, dk, dv = (back[rows_of(2 * i + slot), :].astype(F32) for i in range(5))
-            weight = mix[2 * slot : 2 * slot + 1, :]
-            more = mix[2 * slot + 1 : 2 * slot + 2, :]
-            whole = ((o * weight).T, ((u - w * more) * weight).T, dk, dv)
-            for i, scale in enumerate((1.0, SCALE, SCALE, 1.0)):
-                yield h, b, i, ((kept[8 * n + 4 * slot + i] + whole[i]) * scale).astype(BF16)
-
-
-def finish_first_kernel(nb, lists, *refs):
-    at = Place(lists, nb)
-    parts, kept, mixes, backs, others, outs = refs[:4], refs[4], refs[5:7], refs[7:9], refs[9:13], refs[13:17]
-    for out, part, other in zip(outs, parts, others):
-        out[:, : 2 * HD] = part[...]
-        out[:, 2 * HD :] = other[...]
-    for h, b, i, value in patches(at, kept, mixes, backs):
-        outs[i][rows_of(b), lane(h, 0)] = value
-
-
-def finish_second_kernel(nb, lists, *refs):
-    at = Place(lists, nb)
-    kept, mixes, backs, outs, tiles, sems = refs[4], refs[5:7], refs[7:9], refs[9:13], refs[13], refs[14]
+            rows = rows_of(b)
+            o, dk, dv = (came[rows_of(2 * i + slot), :].astype(F32) for i in range(3))
+            att[h, rows, :] += (o * weights[2 * n + slot]).T
+            ak[h, rows, :] += dk
+            av[h, rows, :] += dv
+            kept[2 * n + slot] = aq[h, rows, :]
     copies = []
-    for h, b, i, value in patches(at, kept, mixes, backs):
-        n = len(copies)
-        tiles[n] = value
-        copies.append(pltpu.make_async_copy(tiles.at[n], outs[i].at[rows_of(b), lane(h, 1)], sems.at[n]))
+    for i, (total, scale) in enumerate(((att, 1.0), (aq, SCALE), (ak, SCALE), (av, 1.0))):
+        for h in range(2):
+            staged[i, :, lane(h, 0)] = (total[h] * scale).astype(BF16)
+        there = outs[i].at[:, pl.ds(2 * half * HD, 2 * HD)]
+        copies.append(pltpu.make_async_copy(staged.at[i], there, sems.at[i]))
         copies[-1].start()
+    for copy in copies:
+        copy.wait()
+
+
+def finish_kernel(nb, lists, before, kept_a, kept_b, last_a, last_b, out, tiles, sems):
+    at = Place(lists, nb)
+    copies = []
+    for n, (partner, last) in enumerate(zip(at.partners, (last_a, last_b))):
+        for half, kept in enumerate((kept_a, kept_b)):
+            for slot, (h, b) in enumerate(partner.sent):
+                value = kept[2 * n + slot] + last[rows_of(2 * half + slot), :].astype(F32)
+                i = len(copies)
+                tiles[i] = (value * SCALE).astype(BF16)
+                copies.append(
+                    pltpu.make_async_copy(tiles.at[i], out.at[rows_of(b), lane(h, half)], sems.at[i])
+                )
+                copies[-1].start()
     for copy in copies:
         copy.wait()
 
@@ -335,7 +346,7 @@
         kernel,
         out_shape=tuple(outs),
         in_specs=[pl.BlockSpec(memory_space=space) for space in spaces],
-        out_specs=tuple([pl.BlockSpec(memory_space=out)] * len(outs)),
+        out_specs=tuple(pl.BlockSpec(memory_space=o) for o in (out if isinstance(out, tuple) else (out,) * len(outs))),
         scratch_shapes=scratch,
         input_output_aliases=aliases or {},
         cost_estimate=pl.CostEstimate(flops=flops, bytes_accessed=moved if flops else 1, transcendentals=0),
@@ -376,7 +387,7 @@
     guests.append(swap(*second))
     forward, backs = [], []
     for half in range(2):
-        result = sds((TILES + 32 * (1 - half), HD), BF16)
+        result = sds((TILES + 32, HD), BF16)
         span = (4, 3 * BLOCK, BLOCK)
         *kept, out_a, out_b, st_a, st_b, aq, pg, dpg = call(
             functools.partial(guest_kernel, nb, half), "guest",
@@ -386,34 +397,41 @@
             ],
             (*arrays, *guests[half], stats0, ot0), flops=4 << 30,
         )
-        got = () if half == 0 else swap(st_a, st_b)
         backs.append(swap(out_a, out_b))
-        forward.append((*kept, st_a, st_b, aq, pg, dpg, *(got or backs[0])))
-    pieces, outs = [], ()
+        forward.append((*kept, st_a, st_b, aq, pg, dpg, *backs[half]))
+    whole, kepts, returns, outs = sds((rows, width), BF16), [], (), ()
     for half in range(2):
-        after = outs[-2:]
+        _, _, st_a, st_b, _, pg, dpg, came_a, came_b = forward[half]
+        ours = sds((2 * (1 + half) * BLOCK, HD), BF16)
+        returns = call(
+            functools.partial(return_kernel, nb, half), "return", [ours, ours],
+            (lists, k, st_a, st_b, pg, dpg, came_a, came_b, *returns, *outs[-1:]),
+            scratch=(pltpu.VMEM((8, HD), F32), pltpu.VMEM((8, HD), F32)), flops=(40 << 30, 0)[half],
+            spaces=(pltpu.SMEM,) + (pltpu.VMEM,) * (7 + len(returns)) + (pl.ANY,) * len(outs[-1:]),
+        )
+        if half == 1:
+            last = swap(*returns)
+        before = (returns[0], *outs[:4])
         outs = call(
             functools.partial(backward_kernel, nb, half), "backward",
-            [sds((rows, 2 * HD), BF16)] * 4 + [sds((16, BLOCK, HD), F32), st, st],
-            (*arrays, *guests[half], *forward[half], *after),
+            [whole] * 4 + [sds((4, BLOCK, HD), F32)], (*arrays, *guests[half], *forward[half], *before),
             scratch=(
                 *(pltpu.VMEM((2, rows, HD), F32) for _ in range(4)), pltpu.VMEM((2, 8, rows), F32),
                 pltpu.VMEM((rows, rows), BF16), pltpu.VMEM((rows, rows), BF16),
                 pltpu.VMEM((8, HD), F32), pltpu.VMEM((8, HD), F32),
-            ), flops=(40 << 30, 1 << 30)[half],
-            spaces=(pltpu.SMEM,) + (pltpu.VMEM,) * 15 + (pl.ANY,) * len(after),
+                pltpu.VMEM((4, rows, 2 * HD), BF16), pltpu.SemaphoreType.DMA((4,)),
+            ), flops=0,
+            spaces=(pltpu.SMEM,) + (pltpu.VMEM,) * 15 + (pl.ANY,) * len(before),
+            out=(pl.ANY,) * 4 + (pltpu.VMEM,), aliases={17 + i: i for i in range(4)} if half else None,
         )
-        pieces.append((*outs, *backs[half]))
-    whole = [sds((rows, width), BF16)] * 4
-    outs = call(
-        functools.partial(finish_first_kernel, nb), "finish_first", whole, (lists, *pieces[0], *pieces[1][:4])
-    )
-    return call(
-        functools.partial(finish_second_kernel, nb), "finish_second", whole, (lists, *outs, *pieces[1][4:]),
-        scratch=(pltpu.VMEM((16, BLOCK, HD), BF16), pltpu.SemaphoreType.DMA((16,))),
-        spaces=(pltpu.SMEM,) + (pl.ANY,) * 4 + (pltpu.VMEM,) * 5, out=pl.ANY,
-        aliases={i + 1: i for i in range(4)},
-    )
+        kepts.append(outs[4])
+    att, dq, dk, dv, _ = outs
+    (dq,) = call(
+        functools.partial(finish_kernel, nb), "finish", [whole], (lists, dq, *kepts, *last),
+        scratch=(pltpu.VMEM((8, BLOCK, HD), BF16), pltpu.SemaphoreType.DMA((8,))),
+        spaces=(pltpu.SMEM, pl.ANY) + (pltpu.VMEM,) * 4, out=pl.ANY, aliases={1: 0},
+    )
+    return att, dq, dk, dv
 
 
 def solution(mesh):

time: 60.2 us -> 60.1 us (level)
  the two profiles are of different devices: /device:TPU:2 before, /device:TPU:8 now
where the time goes in v5:
time: 60.1 us; the launch traced here: 59.8 us
  starting transfers between devices  24 us (40%)
  Pallas kernels  23.8 us (40%)
  waiting for transfers between devices  10.9 us (18%)
  between operations  1.01 us (2%)
    pallas_call x9, Pallas kernels, call(): pl.pallas_call(kernel, out_shape=tuple(outs), in_specs=[pl.BlockSpec(memo...  23.8 us
    ppermute x5, starting transfers between devices, swap(): lax.ppermute(to_b, 'seq', pairs(1))  13.8 us
    ppermute x5, starting transfers between devices, swap(): lax.ppermute(to_a, 'seq', pairs(0))  10.2 us
    ppermute x5, waiting for transfers between devices, swap(): lax.ppermute(to_a, 'seq', pairs(0))  7.63 us
    ppermute x5, waiting for transfers between devices, swap(): lax.ppermute(to_b, 'seq', pairs(1))  3.31 us
  transfers between devices with their start and end apart: 10, of which 4 were waited for; matrix products, arithmetic and copies ran while one was open for 0% of the time, Pallas kernels for 31%

profile of v5, /device:TPU:8, one launch (start us, length us, event | category | flops | bytes accessed | tf_op | source)
XLA Modules:
  0.0 59.8 jit_solution(2038825888651650902)
XLA Ops:
  0.6 0.0 copy-start.1
  0.6 0.0 copy-start
  0.7 0.0 copy-start.2
  0.7 0.0 copy-start.3
  0.7 2.8 %pack.1 = (bf16[8,128,128]{2,1,0:T(8,128)(2,1)}, bf16[8,128,128]{2,1,0:T(8,128)(2,1)}) custom-call(s32[4,6]{1,0:T(4,128)} %lists.17, bf16[512,512]{1,0:T(8,128)(2,1)} %q.11, bf16[512,512]{1,0:T(8,128)(2,1)} %k.15, bf16[512,512]{1,0:T(8,128)(2,1)} %v.11, bf16[512,512]{1,0:T(8,128)(2,1)} %g.11), custom_call_target="tpu_custom_call" | custom-call | bytes 1 | tf_op jit(solution)/shard_map/pack/pallas_call | solution.py:345
  3.4 0.0 copy-start.4
  3.5 1.6 %collective-permute-start.4 = (bf16[8,128,128]{2,1,0:T(8,128)(2,1)}, bf16[8,128,128]{2,1,0:T(8,128)(2,1)S(1)}, u32[]{:S(2)}, u32[]{:S(2)}) collective-permute-start(bf16[8,128,128]{2,1,0:T(8,128)(2,1)} %get-tuple-element.55), channel_id=1, source_target_pairs={{0,1},{1,0},{2,3},{3,2},{4,5},{5,4},{6,7},{7,6},{8,9},{9,8},{10,11... | collective-permute-start | bytes 786440 | tf_op jit(solution)/shard_map/ppermute | solution.py:371
  5.0 3.3 %collective-permute-start.5 = (bf16[8,128,128]{2,1,0:T(8,128)(2,1)}, bf16[8,128,128]{2,1,0:T(8,128)(2,1)S(1)}, u32[]{:S(2)}, u32[]{:S(2)}) collective-permute-start(bf16[8,128,128]{2,1,0:T(8,128)(2,1)} %get-tuple-element.56), channel_id=1, source_target_pairs={{1,2},{2,1},{3,4},{4,3},{5,6},{6,5},{7,8},{8,7},{9,10},{10,9},{11,... | collective-permute-start | bytes 786440 | tf_op jit(solution)/shard_map/ppermute | solution.py:371
  8.3 0.0 copy-done.1
  8.3 0.0 copy-done
  8.3 0.0 copy-done.2
  8.3 0.0 copy-done.3
  8.3 0.0 copy-done.4
  8.3 3.1 %own_forward.1 = (f32[4,8,512]{2,1,0:T(8,128)S(1)}, f32[4,128,512]{2,1,0:T(8,128)S(1)}, bf16[8,128,128]{2,1,0:T(8,128)(2,1)S(1)}, bf16[8,128,128]{2,1,0:T(8,128)(2,1)S(1)}) custom-call(s32[4,6]{1,0:T(4,128)S(1)} %copy-done.4, bf16[512,512]{1,0:T(8,128)(2,1)S(1)} %copy-done.1, bf16[512,512]{1,0:T(8,128)(2,1)S(1)} %copy-done, bf16[512,512]{1,0:T(8,128)(2,1)S(1)} %copy-done.2, ...), custom_call_target="tpu_custom_call" | custom-call | flops 6442450944 | bytes 3735648 | tf_op jit(solution)/shard_map/own_forward/pallas_call | solution.py:345
  11.4 1.7 %collective-permute-start = (bf16[8,128,128]{2,1,0:T(8,128)(2,1)S(1)}, bf16[8,128,128]{2,1,0:T(8,128)(2,1)S(1)}, u32[]{:S(2)}, u32[]{:S(2)}) collective-permute-start(bf16[8,128,128]{2,1,0:T(8,128)(2,1)S(1)} %get-tuple-element.42), channel_id=1, source_target_pairs={{0,1},{1,0},{2,3},{3,2},{4,5},{5,4},{6,7},{7,6},{8,9},{9,8},{10,11... | collective-permute-start | bytes 786440 | tf_op jit(solution)/shard_map/ppermute | solution.py:371
  13.1 2.8 %collective-permute-start.1 = (bf16[8,128,128]{2,1,0:T(8,128)(2,1)S(1)}, bf16[8,128,128]{2,1,0:T(8,128)(2,1)S(1)}, u32[]{:S(2)}, u32[]{:S(2)}) collective-permute-start(bf16[8,128,128]{2,1,0:T(8,128)(2,1)S(1)} %get-tuple-element.43), channel_id=1, source_target_pairs={{1,2},{2,1},{3,4},{4,3},{5,6},{6,5},{7,8},{8,7},{9,10},{10,9},{11,... | collective-permute-start | bytes 786440 | tf_op jit(solution)/shard_map/ppermute | solution.py:371
  15.9 7.4 %collective-permute-done.4.in_a = bf16[8,128,128]{2,1,0:T(8,128)(2,1)S(1)} collective-permute-done((bf16[8,128,128]{2,1,0:T(8,128)(2,1)}, bf16[8,128,128]{2,1,0:T(8,128)(2,1)S(1)}, u32[]{:S(2)}, u32[]{:S(2)}) %collective-permute-start.4) | collective-permute-done | bytes 262176 | tf_op jit(solution)/shard_map/ppermute | solution.py:371
  23.3 0.0 collective-permute-done.5.in_b
  23.3 3.4 %guest.3 = (f32[2,8,512]{2,1,0:T(8,128)S(1)}, f32[2,128,512]{2,1,0:T(8,128)S(1)}, bf16[800,128]{1,0:T(8,128)(2,1)S(1)}, bf16[800,128]{1,0:T(8,128)(2,1)S(1)}, f3...) custom-call(s32[4,6]{1,0:T(4,128)S(1)} %copy-done.4, ...), custom_call_target="tpu_custom_call" | custom-call | flops 4294967296 | bytes 6807648 | tf_op jit(solution)/shard_map/guest/pallas_call | solution.py:345
  26.7 2.4 %collective-permute-start.6 = (bf16[800,128]{1,0:T(8,128)(2,1)S(1)}, bf16[800,128]{1,0:T(8,128)(2,1)S(1)}, u32[]{:S(2)}, u32[]{:S(2)}) collective-permute-start(bf16[800,128]{1,0:T(8,128)(2,1)S(1)} %get-tuple-element.61), channel_id=1, source_target_pairs={{0,1},{1,0},{2,3},{3,2},{4,5},{5,4},{6,7},{7,6},{8,9},{9,8},{10,11... | collective-permute-start | bytes 614408 | tf_op jit(solution)/shard_map/ppermute | solution.py:371
  29.2 1.9 %collective-permute-start.7 = (bf16[800,128]{1,0:T(8,128)(2,1)S(1)}, bf16[800,128]{1,0:T(8,128)(2,1)S(1)}, u32[]{:S(2)}, u32[]{:S(2)}) collective-permute-start(bf16[800,128]{1,0:T(8,128)(2,1)S(1)} %get-tuple-element.62), channel_id=1, source_target_pairs={{1,2},{2,1},{3,4},{4,3},{5,6},{6,5},{7,8},{8,7},{9,10},{10,9},{11,... | collective-permute-start | bytes 614408 | tf_op jit(solution)/shard_map/ppermute | solution.py:371
  31.1 0.0 collective-permute-done.in_a
  31.1 0.0 collective-permute-done.1.in_b
  31.1 3.5 %guest.2 = (f32[2,8,512]{2,1,0:T(8,128)S(1)}, f32[2,128,512]{2,1,0:T(8,128)S(1)}, bf16[800,128]{1,0:T(8,128)(2,1)S(1)}, bf16[800,128]{1,0:T(8,128)(2,1)S(1)}, f3...) custom-call(s32[4,6]{1,0:T(4,128)S(1)} %copy-done.4, ...), custom_call_target="tpu_custom_call" | custom-call | flops 4294967296 | bytes 6807648 | tf_op jit(solution)/shard_map/guest/pallas_call | solution.py:345
  34.6 2.4 %collective-permute-start.2 = (bf16[800,128]{1,0:T(8,128)(2,1)S(1)}, bf16[800,128]{1,0:T(8,128)(2,1)S(1)}, u32[]{:S(2)}, u32[]{:S(2)}) collective-permute-start(bf16[800,128]{1,0:T(8,128)(2,1)S(1)} %get-tuple-element.53), channel_id=1, source_target_pairs={{0,1},{1,0},{2,3},{3,2},{4,5},{5,4},{6,7},{7,6},{8,9},{9,8},{10,11... | collective-permute-start | bytes 614408 | tf_op jit(solution)/shard_map/ppermute | solution.py:371
  37.0 3.4 %collective-permute-start.3 = (bf16[800,128]{1,0:T(8,128)(2,1)S(1)}, bf16[800,128]{1,0:T(8,128)(2,1)S(1)}, u32[]{:S(2)}, u32[]{:S(2)}) collective-permute-start(bf16[800,128]{1,0:T(8,128)(2,1)S(1)} %get-tuple-element.54), channel_id=1, source_target_pairs={{1,2},{2,1},{3,4},{4,3},{5,6},{6,5},{7,8},{8,7},{9,10},{10,9},{11,... | collective-permute-start | bytes 614408 | tf_op jit(solution)/shard_map/ppermute | solution.py:371
  40.4 0.0 collective-permute-done.6.came_a
  40.4 0.0 collective-permute-done.7.came_b
  40.4 0.9 %return.2 = (bf16[256,128]{1,0:T(8,128)(2,1)S(1)}, bf16[256,128]{1,0:T(8,128)(2,1)S(1)}) custom-call(s32[4,6]{1,0:T(4,128)S(1)} %copy-done.4, bf16[512,512]{1,0:T(8,128)(2,1)S(1)} %copy-done, f32[8,128]{1,0:T(8,128)S(1)} %get-tuple-element.57.st_a, f32[8,128]{1,0:T(8,128)S(1)} %get-tuple-element.58.st_b, f32[4,384,128]{2,1,0:T(8,128)S(1)} %get-tuple-element.59.pg, ...), custom_call_target="tpu_custom_call" | custom-call | flops 42949672960 | bytes 2646112 | tf_op jit(solution)/shard_map/return/pallas_call | solution.py:345
  41.4 3.9 %backward.2 = (bf16[512,512]{1,0:T(8,128)(2,1)}, bf16[512,512]{1,0:T(8,128)(2,1)}, bf16[512,512]{1,0:T(8,128)(2,1)}, bf16[512,512]{1,0:T(8,128)(2,1)}, f32[4,128,128]{2,1,0:T(8,128)S(1)}) custom-call(s32[4,6]{1,0:T(4,128)S(1)} %copy-done.4, bf16[512,512]{1,0:T(8,128)(2,1)S(1)} %copy-done.1, bf16[512,512]{1,0:T(8,128)(2,1)S(1)} %copy-done, ...), custom_call_target="tpu_custom_call" | custom-call | bytes 1 | tf_op jit(solution)/shard_map/backward/pallas_call | solution.py:345
  45.3 0.2 collective-permute-done.2.came_a
  45.5 1.1 %collective-permute-done.3.came_b = bf16[800,128]{1,0:T(8,128)(2,1)S(1)} collective-permute-done((bf16[800,128]{1,0:T(8,128)(2,1)S(1)}, bf16[800,128]{1,0:T(8,128)(2,1)S(1)}, u32[]{:S(2)}, u32[]{:S(2)}) %collective-permute-start.3) | collective-permute-done | bytes 204832 | tf_op jit(solution)/shard_map/ppermute | solution.py:371
  46.6 0.9 %return.3 = (bf16[512,128]{1,0:T(8,128)(2,1)S(1)}, bf16[512,128]{1,0:T(8,128)(2,1)S(1)}) custom-call(s32[4,6]{1,0:T(4,128)S(1)} %copy-done.4, bf16[512,512]{1,0:T(8,128)(2,1)S(1)} %copy-done, f32[8,128]{1,0:T(8,128)S(1)} %get-tuple-element.48.st_a, f32[8,128]{1,0:T(8,128)S(1)} %get-tuple-element.49.st_b, f32[4,384,128]{2,1,0:T(8,128)S(1)} %get-tuple-element.51.pg, ...), custom_call_target="tpu_custom_call" | custom-call | bytes 1 | tf_op jit(solution)/shard_map/return/pallas_call | solution.py:345
  47.5 2.2 %collective-permute-start.8 = (bf16[512,128]{1,0:T(8,128)(2,1)S(1)}, bf16[512,128]{1,0:T(8,128)(2,1)S(1)}, u32[]{:S(2)}, u32[]{:S(2)}) collective-permute-start(bf16[512,128]{1,0:T(8,128)(2,1)S(1)} %get-tuple-element.69.refs_0_), channel_id=1, source_target_pairs={{0,1},{1,0},{2,3},{3,2},{4,5},{5,4},{6,7},{7,6},{8,9},{9,8},{10,11... | collective-permute-start | bytes 393224 | tf_op jit(solution)/shard_map/ppermute | solution.py:371
  49.6 2.5 %collective-permute-start.9 = (bf16[512,128]{1,0:T(8,128)(2,1)S(1)}, bf16[512,128]{1,0:T(8,128)(2,1)S(1)}, u32[]{:S(2)}, u32[]{:S(2)}) collective-permute-start(bf16[512,128]{1,0:T(8,128)(2,1)S(1)} %get-tuple-element.77), channel_id=1, source_target_pairs={{1,2},{2,1},{3,4},{4,3},{5,6},{6,5},{7,8},{8,7},{9,10},{10,9},{11,... | collective-permute-start | bytes 393224 | tf_op jit(solution)/shard_map/ppermute | solution.py:371
  52.1 3.9 %backward.3 = (bf16[512,512]{1,0:T(8,128)(2,1)}, bf16[512,512]{1,0:T(8,128)(2,1)}, bf16[512,512]{1,0:T(8,128)(2,1)}, bf16[512,512]{1,0:T(8,128)(2,1)}, f32[4,128,128]{2,1,0:T(8,128)S(1)}) custom-call(s32[4,6]{1,0:T(4,128)S(1)} %copy-done.4, ...), custom_call_target="tpu_custom_call", output_to_operand_aliasing={{0}: (17, {}), {1}: (18, {}), {2}: (19, {}), {3}: (20, {})} | custom-call | bytes 1 | tf_op jit(solution)/shard_map/backward/pallas_call | solution.py:345
  56.0 0.0 collective-permute-done.8.last_a
  56.0 2.2 %collective-permute-done.9.last_b = bf16[512,128]{1,0:T(8,128)(2,1)S(1)} collective-permute-done((bf16[512,128]{1,0:T(8,128)(2,1)S(1)}, bf16[512,128]{1,0:T(8,128)(2,1)S(1)}, u32[]{:S(2)}, u32[]{:S(2)}) %collective-permute-start.9) | collective-permute-done | bytes 131104 | tf_op jit(solution)/shard_map/ppermute | solution.py:371
  58.3 1.4 %finish.1 = bf16[512,512]{1,0:T(8,128)(2,1)} custom-call(s32[4,6]{1,0:T(4,128)S(1)} %copy-done.4, bf16[512,512]{1,0:T(8,128)(2,1)} %get-tuple-element.75.before, f32[4,128,128]{2,1,0:T(8,128)S(1)} %get-tuple-element.68.refs_2_.kept_a, f32[4,128,128]{2,1,0:T(8,128)S(1)} %get-tuple-element.76.kept_b, ...), custom_call_target="tpu_custom_call", output_to_operand_aliasing={{}: (1, {})} | custom-call | bytes 1 | tf_op jit(solution)/shard_map/finish/pallas_call | solution.py:345
Async XLA Ops:
  0.6 7.7 %copy-start.1 = (bf16[512,512]{1,0:T(8,128)(2,1)S(1)}, bf16[512,512]{1,0:T(8,128)(2,1)}, u32[]{:S(2)}) copy-start(bf16[512,512]{1,0:T(8,128)(2,1)} %q.11) | copy-start | bytes 1572868
  0.6 7.7 %copy-start = (bf16[512,512]{1,0:T(8,128)(2,1)S(1)}, bf16[512,512]{1,0:T(8,128)(2,1)}, u32[]{:S(2)}) copy-start(bf16[512,512]{1,0:T(8,128)(2,1)} %k.15) | copy-start | bytes 1572868
  0.7 7.7 %copy-start.2 = (bf16[512,512]{1,0:T(8,128)(2,1)S(1)}, bf16[512,512]{1,0:T(8,128)(2,1)}, u32[]{:S(2)}) copy-start(bf16[512,512]{1,0:T(8,128)(2,1)} %v.11) | copy-start | bytes 1572868
  0.7 7.7 %copy-start.3 = (bf16[512,512]{1,0:T(8,128)(2,1)S(1)}, bf16[512,512]{1,0:T(8,128)(2,1)}, u32[]{:S(2)}) copy-start(bf16[512,512]{1,0:T(8,128)(2,1)} %g.11) | copy-start | bytes 1572868
  3.4 4.9 %copy-start.4 = (s32[4,6]{1,0:T(4,128)S(1)}, s32[4,6]{1,0:T(4,128)}, u32[]{:S(2)}) copy-start(s32[4,6]{1,0:T(4,128)} %lists.17) | copy-start | bytes 292
  3.5 19.8 %collective-permute-start.4 = (bf16[8,128,128]{2,1,0:T(8,128)(2,1)}, bf16[8,128,128]{2,1,0:T(8,128)(2,1)S(1)}, u32[]{:S(2)}, u32[]{:S(2)}) collective-permute-start(bf16[8,128,128]{2,1,0:T(8,128)(2,1)} %get-tuple-element.55), channel_id=1, source_target_pairs={{0,1},{1,0},{2,3},{3,2},{4,5},{5,4},{6,7},{7,6},{8,9},{9,8},{10,11... | collective-permute-start | bytes 786440 | tf_op jit(solution)/shard_map/ppermute | solution.py:371
  5.0 18.3 %collective-permute-start.5 = (bf16[8,128,128]{2,1,0:T(8,128)(2,1)}, bf16[8,128,128]{2,1,0:T(8,128)(2,1)S(1)}, u32[]{:S(2)}, u32[]{:S(2)}) collective-permute-start(bf16[8,128,128]{2,1,0:T(8,128)(2,1)} %get-tuple-element.56), channel_id=1, source_target_pairs={{1,2},{2,1},{3,4},{4,3},{5,6},{6,5},{7,8},{8,7},{9,10},{10,9},{11,... | collective-permute-start | bytes 786440 | tf_op jit(solution)/shard_map/ppermute | solution.py:371
  11.4 19.6 %collective-permute-start = (bf16[8,128,128]{2,1,0:T(8,128)(2,1)S(1)}, bf16[8,128,128]{2,1,0:T(8,128)(2,1)S(1)}, u32[]{:S(2)}, u32[]{:S(2)}) collective-permute-start(bf16[8,128,128]{2,1,0:T(8,128)(2,1)S(1)} %get-tuple-element.42), channel_id=1, source_target_pairs={{0,1},{1,0},{2,3},{3,2},{4,5},{5,4},{6,7},{7,6},{8,9},{9,8},{10,11... | collective-permute-start | bytes 786440 | tf_op jit(solution)/shard_map/ppermute | solution.py:371
  13.1 18.0 %collective-permute-start.1 = (bf16[8,128,128]{2,1,0:T(8,128)(2,1)S(1)}, bf16[8,128,128]{2,1,0:T(8,128)(2,1)S(1)}, u32[]{:S(2)}, u32[]{:S(2)}) collective-permute-start(bf16[8,128,128]{2,1,0:T(8,128)(2,1)S(1)} %get-tuple-element.43), channel_id=1, source_target_pairs={{1,2},{2,1},{3,4},{4,3},{5,6},{6,5},{7,8},{8,7},{9,10},{10,9},{11,... | collective-permute-start | bytes 786440 | tf_op jit(solution)/shard_map/ppermute | solution.py:371
  26.7 13.7 %collective-permute-start.6 = (bf16[800,128]{1,0:T(8,128)(2,1)S(1)}, bf16[800,128]{1,0:T(8,128)(2,1)S(1)}, u32[]{:S(2)}, u32[]{:S(2)}) collective-permute-start(bf16[800,128]{1,0:T(8,128)(2,1)S(1)} %get-tuple-element.61), channel_id=1, source_target_pairs={{0,1},{1,0},{2,3},{3,2},{4,5},{5,4},{6,7},{7,6},{8,9},{9,8},{10,11... | collective-permute-start | bytes 614408 | tf_op jit(solution)/shard_map/ppermute | solution.py:371
  29.2 11.3 %collective-permute-start.7 = (bf16[800,128]{1,0:T(8,128)(2,1)S(1)}, bf16[800,128]{1,0:T(8,128)(2,1)S(1)}, u32[]{:S(2)}, u32[]{:S(2)}) collective-permute-start(bf16[800,128]{1,0:T(8,128)(2,1)S(1)} %get-tuple-element.62), channel_id=1, source_target_pairs={{1,2},{2,1},{3,4},{4,3},{5,6},{6,5},{7,8},{8,7},{9,10},{10,9},{11,... | collective-permute-start | bytes 614408 | tf_op jit(solution)/shard_map/ppermute | solution.py:371
  34.6 10.9 %collective-permute-start.2 = (bf16[800,128]{1,0:T(8,128)(2,1)S(1)}, bf16[800,128]{1,0:T(8,128)(2,1)S(1)}, u32[]{:S(2)}, u32[]{:S(2)}) collective-permute-start(bf16[800,128]{1,0:T(8,128)(2,1)S(1)} %get-tuple-element.53), channel_id=1, source_target_pairs={{0,1},{1,0},{2,3},{3,2},{4,5},{5,4},{6,7},{7,6},{8,9},{9,8},{10,11... | collective-permute-start | bytes 614408 | tf_op jit(solution)/shard_map/ppermute | solution.py:371
  37.0 9.5 %collective-permute-start.3 = (bf16[800,128]{1,0:T(8,128)(2,1)S(1)}, bf16[800,128]{1,0:T(8,128)(2,1)S(1)}, u32[]{:S(2)}, u32[]{:S(2)}) collective-permute-start(bf16[800,128]{1,0:T(8,128)(2,1)S(1)} %get-tuple-element.54), channel_id=1, source_target_pairs={{1,2},{2,1},{3,4},{4,3},{5,6},{6,5},{7,8},{8,7},{9,10},{10,9},{11,... | collective-permute-start | bytes 614408 | tf_op jit(solution)/shard_map/ppermute | solution.py:371
  47.5 8.5 %collective-permute-start.8 = (bf16[512,128]{1,0:T(8,128)(2,1)S(1)}, bf16[512,128]{1,0:T(8,128)(2,1)S(1)}, u32[]{:S(2)}, u32[]{:S(2)}) collective-permute-start(bf16[512,128]{1,0:T(8,128)(2,1)S(1)} %get-tuple-element.69.refs_0_), channel_id=1, source_target_pairs={{0,1},{1,0},{2,3},{3,2},{4,5},{5,4},{6,7},{7,6},{8,9},{9,8},{10,11... | collective-permute-start | bytes 393224 | tf_op jit(solution)/shard_map/ppermute | solution.py:371
  49.6 8.6 %collective-permute-start.9 = (bf16[512,128]{1,0:T(8,128)(2,1)S(1)}, bf16[512,128]{1,0:T(8,128)(2,1)S(1)}, u32[]{:S(2)}, u32[]{:S(2)}) collective-permute-start(bf16[512,128]{1,0:T(8,128)(2,1)S(1)} %get-tuple-element.77), channel_id=1, source_target_pairs={{1,2},{2,1},{3,4},{4,3},{5,6},{6,5},{7,8},{8,7},{9,10},{10,9},{11,... | collective-permute-start | bytes 393224 | tf_op jit(solution)/shard_map/ppermute | solution.py:371

commit v6 on v5

--- a/solution.py
+++ b/solution.py
@@ -154,11 +154,11 @@
     return parts
 
 
-TILES = 6 * BLOCK
+TILES = (6 * BLOCK, 4 * BLOCK)
 
 
 def guest_kernel(nb, half, lists, q, k, v, g, in_a, in_b, stats0, ot0,
-                 stats, ot, out_a, out_b, st_a, st_b, aq, pg, dpg):
+                 stats, ot, out_a, out_b, st_a, st_b, aq, pg, dpg, *late):
     at = Place(lists, nb)
     for h in range(2):
         stats[h] = stats0[2 * half + h]
@@ -204,19 +204,23 @@
         total = stats[h, 1:2, :]
         stats[h, 3:4, :] = stats[h, 0:1, :] + jnp.log2(total)
         stats[h, 4:5, :] = stats[h, 2:3, :] / total
-    for partner, out, st in zip(at.partners, (out_a, out_b), (st_a, st_b)):
+    for n, (partner, out, st) in enumerate(zip(at.partners, (out_a, out_b), (st_a, st_b))):
         for slot, (h, near, free) in enumerate(partner.guests):
             *_, s, dp, qh, gh, kg = kept.pop(0)
             p = jnp.exp2(s - stats[h, 3:4, partner.span])
             ds = (p * (dp - stats[h, 4:5, partner.span])).astype(BF16)
             out[rows_of(2 + slot), :] = dot(ds, qh, 1, 0).astype(BF16)
             aq[h, partner.span, :] += dot(ds, kg, 0, 0)
-            out[rows_of(4 + slot), :] = dot(p.astype(BF16), gh, 1, 0).astype(BF16)
+            dv = dot(p.astype(BF16), gh, 1, 0).astype(BF16)
+            if half == 0:
+                out[rows_of(4 + slot), :] = dv
+            else:
+                late[n][rows_of(slot), :] = dv
         for slot, (h, b) in enumerate(partner.sent):
             st[4 + 2 * slot : 5 + 2 * slot, :] = stats[h, 3:4, rows_of(b)]
             st[5 + 2 * slot : 6 + 2 * slot, :] = stats[h, 4:5, rows_of(b)]
         for i, part in enumerate(split(st[...])):
-            out[TILES + 8 * i : TILES + 8 * i + 8, :] = part
+            out[TILES[half] + 8 * i : TILES[half] + 8 * i + 8, :] = part
 
 
 def merged(l1, d1, l2, d2):
@@ -226,8 +230,9 @@
     return m + jnp.log2(total), (w1 * d1 + w2 * d2) / total
 
 
-def arrived(came):
-    parts = [came[TILES + 8 * i : TILES + 8 * i + 8, :].astype(F32) for i in range(3)]
+def arrived(half, came):
+    first = TILES[half]
+    parts = [came[first + 8 * i : first + 8 * i + 8, :].astype(F32) for i in range(3)]
     return parts[0] + (parts[1] + parts[2])
 
 
@@ -245,12 +250,13 @@
 def return_kernel(nb, half, lists, k, st_a, st_b, pg, dpg, came_a, came_b, *refs):
     back_a, back_b, got_a, got_b = refs[-4:]
     at = Place(lists, nb)
-    got_a[...], got_b[...] = arrived(came_a), arrived(came_b)
+    got_a[...], got_b[...] = arrived(half, came_a), arrived(half, came_b)
     for n, (partner, mine, got, back) in enumerate(
         zip(at.partners, (st_a, st_b), (got_a, got_b), (back_a, back_b))
     ):
         if half == 1:
             back[: 2 * BLOCK, :] = refs[n][...]
+            back[4 * BLOCK :, :] = refs[2 + n][...]
         for slot, (h, near, free) in enumerate(partner.guests):
             shrink, delta = whole_guest(slot, mine, got)
             ds = (pg[2 * n + slot] * shrink * (dpg[2 * n + slot] - delta)).astype(BF16)
@@ -262,7 +268,7 @@
 ):
     outs, kept = refs[-16:-12], refs[-12]
     att, aq, ak, av, fin, ps, dss, got_a, got_b, staged, sems = refs[-11:]
-    got_a[...], got_b[...] = arrived(came_a), arrived(came_b)
+    got_a[...], got_b[...] = arrived(half, came_a), arrived(half, came_b)
     at = Place(lists, nb)
     biases = at.biases()
     fin[:, 0:2, :] = stats[:, 3:5, :]
@@ -306,11 +312,14 @@
     for n, (partner, came) in enumerate(zip(at.partners, (came_a, came_b))):
         for slot, (h, b) in enumerate(partner.sent):
             rows = rows_of(b)
-            o, dk, dv = (came[rows_of(2 * i + slot), :].astype(F32) for i in range(3))
+            o, dk = (came[rows_of(2 * i + slot), :].astype(F32) for i in range(2))
             att[h, rows, :] += (o * weights[2 * n + slot]).T
             ak[h, rows, :] += dk
-            av[h, rows, :] += dv
             kept[2 * n + slot] = aq[h, rows, :]
+            if half == 0:
+                av[h, rows, :] += came[rows_of(4 + slot), :].astype(F32)
+            else:
+                kept[4 + 2 * n + slot] = av[h, rows, :]
     copies = []
     for i, (total, scale) in enumerate(((att, 1.0), (aq, SCALE), (ak, SCALE), (av, 1.0))):
         for h in range(2):
@@ -322,17 +331,21 @@
         copy.wait()
 
 
-def finish_kernel(nb, lists, before, kept_a, kept_b, last_a, last_b, out, tiles, sems):
+def finish_kernel(nb, lists, dq, dv, kept_a, kept_b, last_a, last_b, dq_out, dv_out, tiles, sems):
     at = Place(lists, nb)
     copies = []
     for n, (partner, last) in enumerate(zip(at.partners, (last_a, last_b))):
-        for half, kept in enumerate((kept_a, kept_b)):
-            for slot, (h, b) in enumerate(partner.sent):
-                value = kept[2 * n + slot] + last[rows_of(2 * half + slot), :].astype(F32)
-                i = len(copies)
-                tiles[i] = (value * SCALE).astype(BF16)
+        for slot, (h, b) in enumerate(partner.sent):
+            i = 2 * n + slot
+            for half, own, row, scale, out in (
+                (0, kept_a[i], slot, SCALE, dq_out),
+                (1, kept_b[i], 2 + slot, SCALE, dq_out),
+                (1, kept_b[4 + i], 4 + slot, 1.0, dv_out),
+            ):
+                c = len(copies)
+                tiles[c] = ((own + last[rows_of(row), :].astype(F32)) * scale).astype(BF16)
                 copies.append(
-                    pltpu.make_async_copy(tiles.at[i], out.at[rows_of(b), lane(h, half)], sems.at[i])
+                    pltpu.make_async_copy(tiles.at[c], out.at[rows_of(b), lane(h, half)], sems.at[c])
                 )
                 copies[-1].start()
     for copy in copies:
@@ -387,22 +400,23 @@
     guests.append(swap(*second))
     forward, backs = [], []
     for half in range(2):
-        result = sds((TILES + 32, HD), BF16)
+        result, pair = sds((TILES[half] + 32, HD), BF16), sds((2 * BLOCK, HD), BF16)
         span = (4, 3 * BLOCK, BLOCK)
-        *kept, out_a, out_b, st_a, st_b, aq, pg, dpg = call(
+        fwd, ot, out_a, out_b, st_a, st_b, aq, pg, dpg, *late = call(
             functools.partial(guest_kernel, nb, half), "guest",
             [
                 sds((2, 8, rows), F32), sds((2, HD, rows), F32), result, result, st, st,
-                acc, sds(span, F32), sds(span, F32),
+                acc, sds(span, F32), sds(span, F32), *[pair] * (2 * half),
             ],
             (*arrays, *guests[half], stats0, ot0), flops=4 << 30,
         )
         backs.append(swap(out_a, out_b))
-        forward.append((*kept, st_a, st_b, aq, pg, dpg, *backs[half]))
+        forward.append((fwd, ot, st_a, st_b, aq, pg, dpg, *backs[half]))
     whole, kepts, returns, outs = sds((rows, width), BF16), [], (), ()
     for half in range(2):
         _, _, st_a, st_b, _, pg, dpg, came_a, came_b = forward[half]
-        ours = sds((2 * (1 + half) * BLOCK, HD), BF16)
+        ours = sds(((2, 6)[half] * BLOCK, HD), BF16)
+        returns = (*returns, *late) if half else ()
         returns = call(
             functools.partial(return_kernel, nb, half), "return", [ours, ours],
             (lists, k, st_a, st_b, pg, dpg, came_a, came_b, *returns, *outs[-1:]),
@@ -414,7 +428,7 @@
         before = (returns[0], *outs[:4])
         outs = call(
             functools.partial(backward_kernel, nb, half), "backward",
-            [whole] * 4 + [sds((4, BLOCK, HD), F32)], (*arrays, *guests[half], *forward[half], *before),
+            [whole] * 4 + [sds((8, BLOCK, HD), F32)], (*arrays, *guests[half], *forward[half], *before),
             scratch=(
                 *(pltpu.VMEM((2, rows, HD), F32) for _ in range(4)), pltpu.VMEM((2, 8, rows), F32),
                 pltpu.VMEM((rows, rows), BF16), pltpu.VMEM((rows, rows), BF16),
@@ -426,10 +440,10 @@
         )
         kepts.append(outs[4])
     att, dq, dk, dv, _ = outs
-    (dq,) = call(
-        functools.partial(finish_kernel, nb), "finish", [whole], (lists, dq, *kepts, *last),
-        scratch=(pltpu.VMEM((8, BLOCK, HD), BF16), pltpu.SemaphoreType.DMA((8,))),
-        spaces=(pltpu.SMEM, pl.ANY) + (pltpu.VMEM,) * 4, out=pl.ANY, aliases={1: 0},
+    dq, dv = call(
+        functools.partial(finish_kernel, nb), "finish", [whole] * 2, (lists, dq, dv, *kepts, *last),
+        scratch=(pltpu.VMEM((12, BLOCK, HD), BF16), pltpu.SemaphoreType.DMA((12,))),
+        spaces=(pltpu.SMEM, pl.ANY, pl.ANY) + (pltpu.VMEM,) * 4, out=pl.ANY, aliases={1: 0, 2: 1},
     )
     return att, dq, dk, dv
 

time: 60.1 us -> 59.6 us (level)
  transfers between devices with their start and end apart: 10 -> 10, of which waited for: 4 -> 3; matrix products, arithmetic and copies ran while one was open for 0% -> 0% of each run, Pallas kernels for 31% -> 32%
where the time goes in v6:
time: 59.6 us; the launch traced here: 59.4 us
  starting transfers between devices  24.1 us (40%)
  Pallas kernels  23.8 us (40%)
  waiting for transfers between devices  10.3 us (17%)
  between operations  1.02 us (2%)
    pallas_call x9, Pallas kernels, call(): pl.pallas_call(kernel, out_shape=tuple(outs), in_specs=[pl.BlockSpec(memo...  23.8 us
    ppermute x5, starting transfers between devices, swap(): lax.ppermute(to_b, 'seq', pairs(1))  14.3 us
    ppermute x5, starting transfers between devices, swap(): lax.ppermute(to_a, 'seq', pairs(0))  9.8 us
    ppermute x5, waiting for transfers between devices, swap(): lax.ppermute(to_a, 'seq', pairs(0))  7.4 us
    ppermute x5, waiting for transfers between devices, swap(): lax.ppermute(to_b, 'seq', pairs(1))  2.92 us
  transfers between devices with their start and end apart: 10, of which 3 were waited for; matrix products, arithmetic and copies ran while one was open for 0% of the time, Pallas kernels for 32%

profile of v6, /device:TPU:8, one launch (start us, length us, event | category | flops | bytes accessed | tf_op | source)
XLA Modules:
  0.0 59.4 jit_solution(11117756705172027939)
XLA Ops:
  0.6 0.0 copy-start.1
  0.6 0.0 copy-start
  0.7 0.0 copy-start.2
  0.7 0.0 copy-start.3
  0.7 2.8 %pack.1 = (bf16[8,128,128]{2,1,0:T(8,128)(2,1)}, bf16[8,128,128]{2,1,0:T(8,128)(2,1)}) custom-call(s32[4,6]{1,0:T(4,128)} %lists.17, bf16[512,512]{1,0:T(8,128)(2,1)} %q.11, bf16[512,512]{1,0:T(8,128)(2,1)} %k.15, bf16[512,512]{1,0:T(8,128)(2,1)} %v.11, bf16[512,512]{1,0:T(8,128)(2,1)} %g.11), custom_call_target="tpu_custom_call" | custom-call | bytes 1 | tf_op jit(solution)/shard_map/pack/pallas_call | solution.py:358
  3.4 0.0 copy-start.4
  3.5 1.6 %collective-permute-start.4 = (bf16[8,128,128]{2,1,0:T(8,128)(2,1)}, bf16[8,128,128]{2,1,0:T(8,128)(2,1)S(1)}, u32[]{:S(2)}, u32[]{:S(2)}) collective-permute-start(bf16[8,128,128]{2,1,0:T(8,128)(2,1)} %get-tuple-element.59), channel_id=1, source_target_pairs={{0,1},{1,0},{2,3},{3,2},{4,5},{5,4},{6,7},{7,6},{8,9},{9,8},{10,11... | collective-permute-start | bytes 786440 | tf_op jit(solution)/shard_map/ppermute | solution.py:384
  5.0 3.3 %collective-permute-start.5 = (bf16[8,128,128]{2,1,0:T(8,128)(2,1)}, bf16[8,128,128]{2,1,0:T(8,128)(2,1)S(1)}, u32[]{:S(2)}, u32[]{:S(2)}) collective-permute-start(bf16[8,128,128]{2,1,0:T(8,128)(2,1)} %get-tuple-element.60), channel_id=1, source_target_pairs={{1,2},{2,1},{3,4},{4,3},{5,6},{6,5},{7,8},{8,7},{9,10},{10,9},{11,... | collective-permute-start | bytes 786440 | tf_op jit(solution)/shard_map/ppermute | solution.py:384
  8.3 0.0 copy-done.1
  8.3 0.0 copy-done
  8.3 0.0 copy-done.2
  8.3 0.0 copy-done.3
  8.3 0.0 copy-done.4
  8.3 3.1 %own_forward.1 = (f32[4,8,512]{2,1,0:T(8,128)S(1)}, f32[4,128,512]{2,1,0:T(8,128)S(1)}, bf16[8,128,128]{2,1,0:T(8,128)(2,1)S(1)}, bf16[8,128,128]{2,1,0:T(8,128)(2,1)S(1)}) custom-call(s32[4,6]{1,0:T(4,128)S(1)} %copy-done.4, bf16[512,512]{1,0:T(8,128)(2,1)S(1)} %copy-done.1, bf16[512,512]{1,0:T(8,128)(2,1)S(1)} %copy-done, bf16[512,512]{1,0:T(8,128)(2,1)S(1)} %copy-done.2, ...), custom_call_target="tpu_custom_call" | custom-call | flops 6442450944 | bytes 3735648 | tf_op jit(solution)/shard_map/own_forward/pallas_call | solution.py:358
  11.4 1.7 %collective-permute-start = (bf16[8,128,128]{2,1,0:T(8,128)(2,1)S(1)}, bf16[8,128,128]{2,1,0:T(8,128)(2,1)S(1)}, u32[]{:S(2)}, u32[]{:S(2)}) collective-permute-start(bf16[8,128,128]{2,1,0:T(8,128)(2,1)S(1)} %get-tuple-element.46), channel_id=1, source_target_pairs={{0,1},{1,0},{2,3},{3,2},{4,5},{5,4},{6,7},{7,6},{8,9},{9,8},{10,11... | collective-permute-start | bytes 786440 | tf_op jit(solution)/shard_map/ppermute | solution.py:384
  13.1 2.8 %collective-permute-start.1 = (bf16[8,128,128]{2,1,0:T(8,128)(2,1)S(1)}, bf16[8,128,128]{2,1,0:T(8,128)(2,1)S(1)}, u32[]{:S(2)}, u32[]{:S(2)}) collective-permute-start(bf16[8,128,128]{2,1,0:T(8,128)(2,1)S(1)} %get-tuple-element.47), channel_id=1, source_target_pairs={{1,2},{2,1},{3,4},{4,3},{5,6},{6,5},{7,8},{8,7},{9,10},{10,9},{11,... | collective-permute-start | bytes 786440 | tf_op jit(solution)/shard_map/ppermute | solution.py:384
  15.9 7.4 %collective-permute-done.4.in_a = bf16[8,128,128]{2,1,0:T(8,128)(2,1)S(1)} collective-permute-done((bf16[8,128,128]{2,1,0:T(8,128)(2,1)}, bf16[8,128,128]{2,1,0:T(8,128)(2,1)S(1)}, u32[]{:S(2)}, u32[]{:S(2)}) %collective-permute-start.4) | collective-permute-done | bytes 262176 | tf_op jit(solution)/shard_map/ppermute | solution.py:384
  23.3 0.0 collective-permute-done.5.in_b
  23.3 3.4 %guest.3 = (f32[2,8,512]{2,1,0:T(8,128)S(1)}, f32[2,128,512]{2,1,0:T(8,128)S(1)}, bf16[800,128]{1,0:T(8,128)(2,1)S(1)}, bf16[800,128]{1,0:T(8,128)(2,1)S(1)}, f3...) custom-call(s32[4,6]{1,0:T(4,128)S(1)} %copy-done.4, ...), custom_call_target="tpu_custom_call" | custom-call | flops 4294967296 | bytes 6807648 | tf_op jit(solution)/shard_map/guest/pallas_call | solution.py:358
  26.7 2.4 %collective-permute-start.6 = (bf16[800,128]{1,0:T(8,128)(2,1)S(1)}, bf16[800,128]{1,0:T(8,128)(2,1)S(1)}, u32[]{:S(2)}, u32[]{:S(2)}) collective-permute-start(bf16[800,128]{1,0:T(8,128)(2,1)S(1)} %get-tuple-element.65), channel_id=1, source_target_pairs={{0,1},{1,0},{2,3},{3,2},{4,5},{5,4},{6,7},{7,6},{8,9},{9,8},{10,11... | collective-permute-start | bytes 614408 | tf_op jit(solution)/shard_map/ppermute | solution.py:384
  29.2 1.9 %collective-permute-start.7 = (bf16[800,128]{1,0:T(8,128)(2,1)S(1)}, bf16[800,128]{1,0:T(8,128)(2,1)S(1)}, u32[]{:S(2)}, u32[]{:S(2)}) collective-permute-start(bf16[800,128]{1,0:T(8,128)(2,1)S(1)} %get-tuple-element.66), channel_id=1, source_target_pairs={{1,2},{2,1},{3,4},{4,3},{5,6},{6,5},{7,8},{8,7},{9,10},{10,9},{11,... | collective-permute-start | bytes 614408 | tf_op jit(solution)/shard_map/ppermute | solution.py:384
  31.1 0.0 collective-permute-done.in_a
  31.1 0.0 collective-permute-done.1.in_b
  31.1 3.5 %guest.2 = (f32[2,8,512]{2,1,0:T(8,128)S(1)}, f32[2,128,512]{2,1,0:T(8,128)S(1)}, bf16[544,128]{1,0:T(8,128)(2,1)S(1)}, bf16[544,128]{1,0:T(8,128)(2,1)S(1)}, f3...) custom-call(s32[4,6]{1,0:T(4,128)S(1)} %copy-done.4, ...), custom_call_target="tpu_custom_call" | custom-call | flops 4294967296 | bytes 6807648 | tf_op jit(solution)/shard_map/guest/pallas_call | solution.py:358
  34.6 2.4 %collective-permute-start.2 = (bf16[544,128]{1,0:T(8,128)(2,1)S(1)}, bf16[544,128]{1,0:T(8,128)(2,1)S(1)}, u32[]{:S(2)}, u32[]{:S(2)}) collective-permute-start(bf16[544,128]{1,0:T(8,128)(2,1)S(1)} %get-tuple-element.57), channel_id=1, source_target_pairs={{0,1},{1,0},{2,3},{3,2},{4,5},{5,4},{6,7},{7,6},{8,9},{9,8},{10,11... | collective-permute-start | bytes 417800 | tf_op jit(solution)/shard_map/ppermute | solution.py:384
  37.0 3.4 %collective-permute-start.3 = (bf16[544,128]{1,0:T(8,128)(2,1)S(1)}, bf16[544,128]{1,0:T(8,128)(2,1)S(1)}, u32[]{:S(2)}, u32[]{:S(2)}) collective-permute-start(bf16[544,128]{1,0:T(8,128)(2,1)S(1)} %get-tuple-element.58), channel_id=1, source_target_pairs={{1,2},{2,1},{3,4},{4,3},{5,6},{6,5},{7,8},{8,7},{9,10},{10,9},{11,... | collective-permute-start | bytes 417800 | tf_op jit(solution)/shard_map/ppermute | solution.py:384
  40.4 0.0 collective-permute-done.6.came_a
  40.4 0.0 collective-permute-done.7.came_b
  40.4 0.9 %return.2 = (bf16[256,128]{1,0:T(8,128)(2,1)S(1)}, bf16[256,128]{1,0:T(8,128)(2,1)S(1)}) custom-call(s32[4,6]{1,0:T(4,128)S(1)} %copy-done.4, bf16[512,512]{1,0:T(8,128)(2,1)S(1)} %copy-done, f32[8,128]{1,0:T(8,128)S(1)} %get-tuple-element.61.st_a, f32[8,128]{1,0:T(8,128)S(1)} %get-tuple-element.62.st_b, f32[4,384,128]{2,1,0:T(8,128)S(1)} %get-tuple-element.63.pg, ...), custom_call_target="tpu_custom_call" | custom-call | flops 42949672960 | bytes 2646112 | tf_op jit(solution)/shard_map/return/pallas_call | solution.py:358
  41.4 3.9 %backward.2 = (bf16[512,512]{1,0:T(8,128)(2,1)}, bf16[512,512]{1,0:T(8,128)(2,1)}, bf16[512,512]{1,0:T(8,128)(2,1)}, bf16[512,512]{1,0:T(8,128)(2,1)}, f32[8,128,128]{2,1,0:T(8,128)S(1)}) custom-call(s32[4,6]{1,0:T(4,128)S(1)} %copy-done.4, bf16[512,512]{1,0:T(8,128)(2,1)S(1)} %copy-done.1, bf16[512,512]{1,0:T(8,128)(2,1)S(1)} %copy-done, ...), custom_call_target="tpu_custom_call" | custom-call | bytes 1 | tf_op jit(solution)/shard_map/backward/pallas_call | solution.py:358
  45.3 0.0 collective-permute-done.2.came_a
  45.3 0.5 collective-permute-done.3.came_b
  45.7 0.9 %return.3 = (bf16[768,128]{1,0:T(8,128)(2,1)S(1)}, bf16[768,128]{1,0:T(8,128)(2,1)S(1)}) custom-call(s32[4,6]{1,0:T(4,128)S(1)} %copy-done.4, bf16[512,512]{1,0:T(8,128)(2,1)S(1)} %copy-done, f32[8,128]{1,0:T(8,128)S(1)} %get-tuple-element.52.st_a, f32[8,128]{1,0:T(8,128)S(1)} %get-tuple-element.53.st_b, f32[4,384,128]{2,1,0:T(8,128)S(1)} %get-tuple-element.55.pg, ...), custom_call_target="tpu_custom_call" | custom-call | bytes 1 | tf_op jit(solution)/shard_map/return/pallas_call | solution.py:358
  46.7 1.7 %collective-permute-start.8 = (bf16[768,128]{1,0:T(8,128)(2,1)S(1)}, bf16[768,128]{1,0:T(8,128)(2,1)S(1)}, u32[]{:S(2)}, u32[]{:S(2)}) collective-permute-start(bf16[768,128]{1,0:T(8,128)(2,1)S(1)} %get-tuple-element.75.refs_0_), channel_id=1, source_target_pairs={{0,1},{1,0},{2,3},{3,2},{4,5},{5,4},{6,7},{7,6},{8,9},{9,8},{10,11... | collective-permute-start | bytes 589832 | tf_op jit(solution)/shard_map/ppermute | solution.py:384
  48.4 3.0 %collective-permute-start.9 = (bf16[768,128]{1,0:T(8,128)(2,1)S(1)}, bf16[768,128]{1,0:T(8,128)(2,1)S(1)}, u32[]{:S(2)}, u32[]{:S(2)}) collective-permute-start(bf16[768,128]{1,0:T(8,128)(2,1)S(1)} %get-tuple-element.84), channel_id=1, source_target_pairs={{1,2},{2,1},{3,4},{4,3},{5,6},{6,5},{7,8},{8,7},{9,10},{10,9},{11,... | collective-permute-start | bytes 589832 | tf_op jit(solution)/shard_map/ppermute | solution.py:384
  51.4 3.9 %backward.3 = (bf16[512,512]{1,0:T(8,128)(2,1)}, bf16[512,512]{1,0:T(8,128)(2,1)}, bf16[512,512]{1,0:T(8,128)(2,1)}, bf16[512,512]{1,0:T(8,128)(2,1)}, f32[8,128,128]{2,1,0:T(8,128)S(1)}) custom-call(s32[4,6]{1,0:T(4,128)S(1)} %copy-done.4, ...), custom_call_target="tpu_custom_call", output_to_operand_aliasing={{0}: (17, {}), {1}: (18, {}), {2}: (19, {}), {3}: (20, {})} | custom-call | bytes 1 | tf_op jit(solution)/shard_map/backward/pallas_call | solution.py:358
  55.3 0.0 collective-permute-done.8.last_a
  55.3 2.4 %collective-permute-done.9.last_b = bf16[768,128]{1,0:T(8,128)(2,1)S(1)} collective-permute-done((bf16[768,128]{1,0:T(8,128)(2,1)S(1)}, bf16[768,128]{1,0:T(8,128)(2,1)S(1)}, u32[]{:S(2)}, u32[]{:S(2)}) %collective-permute-start.9) | collective-permute-done | bytes 196640 | tf_op jit(solution)/shard_map/ppermute | solution.py:384
  57.7 1.5 %finish.1 = (bf16[512,512]{1,0:T(8,128)(2,1)}, bf16[512,512]{1,0:T(8,128)(2,1)}) custom-call(s32[4,6]{1,0:T(4,128)S(1)} %copy-done.4, bf16[512,512]{1,0:T(8,128)(2,1)} %get-tuple-element.81.dq, bf16[512,512]{1,0:T(8,128)(2,1)} %get-tuple-element.82.dv, ...), custom_call_target="tpu_custom_call", output_to_operand_aliasing={{0}: (1, {}), {1}: (2, {})} | custom-call | bytes 1 | tf_op jit(solution)/shard_map/finish/pallas_call | solution.py:358
Async XLA Ops:
  0.6 7.7 %copy-start.1 = (bf16[512,512]{1,0:T(8,128)(2,1)S(1)}, bf16[512,512]{1,0:T(8,128)(2,1)}, u32[]{:S(2)}) copy-start(bf16[512,512]{1,0:T(8,128)(2,1)} %q.11) | copy-start | bytes 1572868
  0.6 7.7 %copy-start = (bf16[512,512]{1,0:T(8,128)(2,1)S(1)}, bf16[512,512]{1,0:T(8,128)(2,1)}, u32[]{:S(2)}) copy-start(bf16[512,512]{1,0:T(8,128)(2,1)} %k.15) | copy-start | bytes 1572868
  0.7 7.7 %copy-start.2 = (bf16[512,512]{1,0:T(8,128)(2,1)S(1)}, bf16[512,512]{1,0:T(8,128)(2,1)}, u32[]{:S(2)}) copy-start(bf16[512,512]{1,0:T(8,128)(2,1)} %v.11) | copy-start | bytes 1572868
  0.7 7.7 %copy-start.3 = (bf16[512,512]{1,0:T(8,128)(2,1)S(1)}, bf16[512,512]{1,0:T(8,128)(2,1)}, u32[]{:S(2)}) copy-start(bf16[512,512]{1,0:T(8,128)(2,1)} %g.11) | copy-start | bytes 1572868
  3.4 4.9 %copy-start.4 = (s32[4,6]{1,0:T(4,128)S(1)}, s32[4,6]{1,0:T(4,128)}, u32[]{:S(2)}) copy-start(s32[4,6]{1,0:T(4,128)} %lists.17) | copy-start | bytes 292
  3.5 19.8 %collective-permute-start.4 = (bf16[8,128,128]{2,1,0:T(8,128)(2,1)}, bf16[8,128,128]{2,1,0:T(8,128)(2,1)S(1)}, u32[]{:S(2)}, u32[]{:S(2)}) collective-permute-start(bf16[8,128,128]{2,1,0:T(8,128)(2,1)} %get-tuple-element.59), channel_id=1, source_target_pairs={{0,1},{1,0},{2,3},{3,2},{4,5},{5,4},{6,7},{7,6},{8,9},{9,8},{10,11... | collective-permute-start | bytes 786440 | tf_op jit(solution)/shard_map/ppermute | solution.py:384
  5.0 18.3 %collective-permute-start.5 = (bf16[8,128,128]{2,1,0:T(8,128)(2,1)}, bf16[8,128,128]{2,1,0:T(8,128)(2,1)S(1)}, u32[]{:S(2)}, u32[]{:S(2)}) collective-permute-start(bf16[8,128,128]{2,1,0:T(8,128)(2,1)} %get-tuple-element.60), channel_id=1, source_target_pairs={{1,2},{2,1},{3,4},{4,3},{5,6},{6,5},{7,8},{8,7},{9,10},{10,9},{11,... | collective-permute-start | bytes 786440 | tf_op jit(solution)/shard_map/ppermute | solution.py:384
  11.4 19.6 %collective-permute-start = (bf16[8,128,128]{2,1,0:T(8,128)(2,1)S(1)}, bf16[8,128,128]{2,1,0:T(8,128)(2,1)S(1)}, u32[]{:S(2)}, u32[]{:S(2)}) collective-permute-start(bf16[8,128,128]{2,1,0:T(8,128)(2,1)S(1)} %get-tuple-element.46), channel_id=1, source_target_pairs={{0,1},{1,0},{2,3},{3,2},{4,5},{5,4},{6,7},{7,6},{8,9},{9,8},{10,11... | collective-permute-start | bytes 786440 | tf_op jit(solution)/shard_map/ppermute | solution.py:384
  13.1 18.0 %collective-permute-start.1 = (bf16[8,128,128]{2,1,0:T(8,128)(2,1)S(1)}, bf16[8,128,128]{2,1,0:T(8,128)(2,1)S(1)}, u32[]{:S(2)}, u32[]{:S(2)}) collective-permute-start(bf16[8,128,128]{2,1,0:T(8,128)(2,1)S(1)} %get-tuple-element.47), channel_id=1, source_target_pairs={{1,2},{2,1},{3,4},{4,3},{5,6},{6,5},{7,8},{8,7},{9,10},{10,9},{11,... | collective-permute-start | bytes 786440 | tf_op jit(solution)/shard_map/ppermute | solution.py:384
  26.7 13.7 %collective-permute-start.6 = (bf16[800,128]{1,0:T(8,128)(2,1)S(1)}, bf16[800,128]{1,0:T(8,128)(2,1)S(1)}, u32[]{:S(2)}, u32[]{:S(2)}) collective-permute-start(bf16[800,128]{1,0:T(8,128)(2,1)S(1)} %get-tuple-element.65), channel_id=1, source_target_pairs={{0,1},{1,0},{2,3},{3,2},{4,5},{5,4},{6,7},{7,6},{8,9},{9,8},{10,11... | collective-permute-start | bytes 614408 | tf_op jit(solution)/shard_map/ppermute | solution.py:384
  29.2 11.3 %collective-permute-start.7 = (bf16[800,128]{1,0:T(8,128)(2,1)S(1)}, bf16[800,128]{1,0:T(8,128)(2,1)S(1)}, u32[]{:S(2)}, u32[]{:S(2)}) collective-permute-start(bf16[800,128]{1,0:T(8,128)(2,1)S(1)} %get-tuple-element.66), channel_id=1, source_target_pairs={{1,2},{2,1},{3,4},{4,3},{5,6},{6,5},{7,8},{8,7},{9,10},{10,9},{11,... | collective-permute-start | bytes 614408 | tf_op jit(solution)/shard_map/ppermute | solution.py:384
  34.6 10.7 %collective-permute-start.2 = (bf16[544,128]{1,0:T(8,128)(2,1)S(1)}, bf16[544,128]{1,0:T(8,128)(2,1)S(1)}, u32[]{:S(2)}, u32[]{:S(2)}) collective-permute-start(bf16[544,128]{1,0:T(8,128)(2,1)S(1)} %get-tuple-element.57), channel_id=1, source_target_pairs={{0,1},{1,0},{2,3},{3,2},{4,5},{5,4},{6,7},{7,6},{8,9},{9,8},{10,11... | collective-permute-start | bytes 417800 | tf_op jit(solution)/shard_map/ppermute | solution.py:384
  37.0 8.7 %collective-permute-start.3 = (bf16[544,128]{1,0:T(8,128)(2,1)S(1)}, bf16[544,128]{1,0:T(8,128)(2,1)S(1)}, u32[]{:S(2)}, u32[]{:S(2)}) collective-permute-start(bf16[544,128]{1,0:T(8,128)(2,1)S(1)} %get-tuple-element.58), channel_id=1, source_target_pairs={{1,2},{2,1},{3,4},{4,3},{5,6},{6,5},{7,8},{8,7},{9,10},{10,9},{11,... | collective-permute-start | bytes 417800 | tf_op jit(solution)/shard_map/ppermute | solution.py:384
  46.7 8.6 %collective-permute-start.8 = (bf16[768,128]{1,0:T(8,128)(2,1)S(1)}, bf16[768,128]{1,0:T(8,128)(2,1)S(1)}, u32[]{:S(2)}, u32[]{:S(2)}) collective-permute-start(bf16[768,128]{1,0:T(8,128)(2,1)S(1)} %get-tuple-element.75.refs_0_), channel_id=1, source_target_pairs={{0,1},{1,0},{2,3},{3,2},{4,5},{5,4},{6,7},{7,6},{8,9},{9,8},{10,11... | collective-permute-start | bytes 589832 | tf_op jit(solution)/shard_map/ppermute | solution.py:384
  48.4 9.3 %collective-permute-start.9 = (bf16[768,128]{1,0:T(8,128)(2,1)S(1)}, bf16[768,128]{1,0:T(8,128)(2,1)S(1)}, u32[]{:S(2)}, u32[]{:S(2)}) collective-permute-start(bf16[768,128]{1,0:T(8,128)(2,1)S(1)} %get-tuple-element.84), channel_id=1, source_target_pairs={{1,2},{2,1},{3,4},{4,3},{5,6},{6,5},{7,8},{8,7},{9,10},{10,9},{11,... | collective-permute-start | bytes 589832 | tf_op jit(solution)/shard_map/ppermute | solution.py:384

commit v7 on v6

--- a/solution.py
+++ b/solution.py
@@ -299,6 +299,22 @@
         av[h] = dot(ps[...], g[:, cols], 1, 0)
         ak[h] = dot(dss[...], q[:, cols], 1, 0)
         aq[h] = aq0[h] + dot(dss[...], kh, 0, 0)
+    copies = []
+
+    def ship(i, total, scale):
+        for h in range(2):
+            staged[i, :, lane(h, 0)] = (total[h] * scale).astype(BF16)
+        there = outs[i].at[:, pl.ds(2 * half * HD, 2 * HD)]
+        copies.append(pltpu.make_async_copy(staged.at[i], there, sems.at[i]))
+        copies[-1].start()
+
+    for n, (partner, came) in enumerate(zip(at.partners, (came_a, came_b))):
+        for slot, (h, b) in enumerate(partner.sent):
+            rows = rows_of(b)
+            att[h, rows, :] += (came[rows_of(slot), :].astype(F32) * weights[2 * n + slot]).T
+            kept[2 * n + slot] = aq[h, rows, :]
+    ship(0, att, 1.0)
+    ship(1, aq, SCALE)
     for n, (partner, message, mine, got) in enumerate(
         zip(at.partners, (in_a, in_b), (st_a, st_b), (got_a, got_b))
     ):
@@ -312,21 +328,13 @@
     for n, (partner, came) in enumerate(zip(at.partners, (came_a, came_b))):
         for slot, (h, b) in enumerate(partner.sent):
             rows = rows_of(b)
-            o, dk = (came[rows_of(2 * i + slot), :].astype(F32) for i in range(2))
-            att[h, rows, :] += (o * weights[2 * n + slot]).T
-            ak[h, rows, :] += dk
-            kept[2 * n + slot] = aq[h, rows, :]
+            ak[h, rows, :] += came[rows_of(2 + slot), :].astype(F32)
             if half == 0:
                 av[h, rows, :] += came[rows_of(4 + slot), :].astype(F32)
             else:
                 kept[4 + 2 * n + slot] = av[h, rows, :]
-    copies = []
-    for i, (total, scale) in enumerate(((att, 1.0), (aq, SCALE), (ak, SCALE), (av, 1.0))):
-        for h in range(2):
-            staged[i, :, lane(h, 0)] = (total[h] * scale).astype(BF16)
-        there = outs[i].at[:, pl.ds(2 * half * HD, 2 * HD)]
-        copies.append(pltpu.make_async_copy(staged.at[i], there, sems.at[i]))
-        copies[-1].start()
+    ship(2, ak, SCALE)
+    ship(3, av, 1.0)
     for copy in copies:
         copy.wait()
 

time: 59.6 us -> 59.6 us (level)
  no operation moved by 1% of the time
where the time goes in v7:
time: 59.6 us; the launch traced here: 59.4 us
  starting transfers between devices  24.1 us (40%)
  Pallas kernels  23.8 us (40%)
  waiting for transfers between devices  10.3 us (17%)
  between operations  1.02 us (2%)
    pallas_call x9, Pallas kernels, call(): pl.pallas_call(kernel, out_shape=tuple(outs), in_specs=[pl.BlockSpec(memo...  23.8 us
    ppermute x5, starting transfers between devices, swap(): lax.ppermute(to_b, 'seq', pairs(1))  14.3 us
    ppermute x5, starting transfers between devices, swap(): lax.ppermute(to_a, 'seq', pairs(0))  9.8 us
    ppermute x5, waiting for transfers between devices, swap(): lax.ppermute(to_a, 'seq', pairs(0))  7.4 us
    ppermute x5, waiting for transfers between devices, swap(): lax.ppermute(to_b, 'seq', pairs(1))  2.92 us
  transfers between devices with their start and end apart: 10, of which 3 were waited for; matrix products, arithmetic and copies ran while one was open for 0% of the time, Pallas kernels for 32%

profile of v7, /device:TPU:8, one launch (start us, length us, event | category | flops | bytes accessed | tf_op | source)
XLA Modules:
  0.0 59.4 jit_solution(3276919176343856081)
XLA Ops:
  0.6 0.0 copy-start.1
  0.6 0.0 copy-start
  0.7 0.0 copy-start.2
  0.7 0.0 copy-start.3
  0.7 2.8 %pack.1 = (bf16[8,128,128]{2,1,0:T(8,128)(2,1)}, bf16[8,128,128]{2,1,0:T(8,128)(2,1)}) custom-call(s32[4,6]{1,0:T(4,128)} %lists.17, bf16[512,512]{1,0:T(8,128)(2,1)} %q.11, bf16[512,512]{1,0:T(8,128)(2,1)} %k.15, bf16[512,512]{1,0:T(8,128)(2,1)} %v.11, bf16[512,512]{1,0:T(8,128)(2,1)} %g.11), custom_call_target="tpu_custom_call" | custom-call | bytes 1 | tf_op jit(solution)/shard_map/pack/pallas_call | solution.py:366
  3.4 0.0 copy-start.4
  3.5 1.6 %collective-permute-start.4 = (bf16[8,128,128]{2,1,0:T(8,128)(2,1)}, bf16[8,128,128]{2,1,0:T(8,128)(2,1)S(1)}, u32[]{:S(2)}, u32[]{:S(2)}) collective-permute-start(bf16[8,128,128]{2,1,0:T(8,128)(2,1)} %get-tuple-element.59), channel_id=1, source_target_pairs={{0,1},{1,0},{2,3},{3,2},{4,5},{5,4},{6,7},{7,6},{8,9},{9,8},{10,11... | collective-permute-start | bytes 786440 | tf_op jit(solution)/shard_map/ppermute | solution.py:392
  5.0 3.3 %collective-permute-start.5 = (bf16[8,128,128]{2,1,0:T(8,128)(2,1)}, bf16[8,128,128]{2,1,0:T(8,128)(2,1)S(1)}, u32[]{:S(2)}, u32[]{:S(2)}) collective-permute-start(bf16[8,128,128]{2,1,0:T(8,128)(2,1)} %get-tuple-element.60), channel_id=1, source_target_pairs={{1,2},{2,1},{3,4},{4,3},{5,6},{6,5},{7,8},{8,7},{9,10},{10,9},{11,... | collective-permute-start | bytes 786440 | tf_op jit(solution)/shard_map/ppermute | solution.py:392
  8.3 0.0 copy-done.1
  8.3 0.0 copy-done
  8.3 0.0 copy-done.2
  8.3 0.0 copy-done.3
  8.3 0.0 copy-done.4
  8.3 3.1 %own_forward.1 = (f32[4,8,512]{2,1,0:T(8,128)S(1)}, f32[4,128,512]{2,1,0:T(8,128)S(1)}, bf16[8,128,128]{2,1,0:T(8,128)(2,1)S(1)}, bf16[8,128,128]{2,1,0:T(8,128)(2,1)S(1)}) custom-call(s32[4,6]{1,0:T(4,128)S(1)} %copy-done.4, bf16[512,512]{1,0:T(8,128)(2,1)S(1)} %copy-done.1, bf16[512,512]{1,0:T(8,128)(2,1)S(1)} %copy-done, bf16[512,512]{1,0:T(8,128)(2,1)S(1)} %copy-done.2, ...), custom_call_target="tpu_custom_call" | custom-call | flops 6442450944 | bytes 3735648 | tf_op jit(solution)/shard_map/own_forward/pallas_call | solution.py:366
  11.4 1.7 %collective-permute-start = (bf16[8,128,128]{2,1,0:T(8,128)(2,1)S(1)}, bf16[8,128,128]{2,1,0:T(8,128)(2,1)S(1)}, u32[]{:S(2)}, u32[]{:S(2)}) collective-permute-start(bf16[8,128,128]{2,1,0:T(8,128)(2,1)S(1)} %get-tuple-element.46), channel_id=1, source_target_pairs={{0,1},{1,0},{2,3},{3,2},{4,5},{5,4},{6,7},{7,6},{8,9},{9,8},{10,11... | collective-permute-start | bytes 786440 | tf_op jit(solution)/shard_map/ppermute | solution.py:392
  13.1 2.8 %collective-permute-start.1 = (bf16[8,128,128]{2,1,0:T(8,128)(2,1)S(1)}, bf16[8,128,128]{2,1,0:T(8,128)(2,1)S(1)}, u32[]{:S(2)}, u32[]{:S(2)}) collective-permute-start(bf16[8,128,128]{2,1,0:T(8,128)(2,1)S(1)} %get-tuple-element.47), channel_id=1, source_target_pairs={{1,2},{2,1},{3,4},{4,3},{5,6},{6,5},{7,8},{8,7},{9,10},{10,9},{11,... | collective-permute-start | bytes 786440 | tf_op jit(solution)/shard_map/ppermute | solution.py:392
  15.9 7.4 %collective-permute-done.4.in_a = bf16[8,128,128]{2,1,0:T(8,128)(2,1)S(1)} collective-permute-done((bf16[8,128,128]{2,1,0:T(8,128)(2,1)}, bf16[8,128,128]{2,1,0:T(8,128)(2,1)S(1)}, u32[]{:S(2)}, u32[]{:S(2)}) %collective-permute-start.4) | collective-permute-done | bytes 262176 | tf_op jit(solution)/shard_map/ppermute | solution.py:392
  23.3 0.0 collective-permute-done.5.in_b
  23.3 3.4 %guest.3 = (f32[2,8,512]{2,1,0:T(8,128)S(1)}, f32[2,128,512]{2,1,0:T(8,128)S(1)}, bf16[800,128]{1,0:T(8,128)(2,1)S(1)}, bf16[800,128]{1,0:T(8,128)(2,1)S(1)}, f3...) custom-call(s32[4,6]{1,0:T(4,128)S(1)} %copy-done.4, ...), custom_call_target="tpu_custom_call" | custom-call | flops 4294967296 | bytes 6807648 | tf_op jit(solution)/shard_map/guest/pallas_call | solution.py:366
  26.7 2.4 %collective-permute-start.6 = (bf16[800,128]{1,0:T(8,128)(2,1)S(1)}, bf16[800,128]{1,0:T(8,128)(2,1)S(1)}, u32[]{:S(2)}, u32[]{:S(2)}) collective-permute-start(bf16[800,128]{1,0:T(8,128)(2,1)S(1)} %get-tuple-element.65), channel_id=1, source_target_pairs={{0,1},{1,0},{2,3},{3,2},{4,5},{5,4},{6,7},{7,6},{8,9},{9,8},{10,11... | collective-permute-start | bytes 614408 | tf_op jit(solution)/shard_map/ppermute | solution.py:392
  29.2 1.9 %collective-permute-start.7 = (bf16[800,128]{1,0:T(8,128)(2,1)S(1)}, bf16[800,128]{1,0:T(8,128)(2,1)S(1)}, u32[]{:S(2)}, u32[]{:S(2)}) collective-permute-start(bf16[800,128]{1,0:T(8,128)(2,1)S(1)} %get-tuple-element.66), channel_id=1, source_target_pairs={{1,2},{2,1},{3,4},{4,3},{5,6},{6,5},{7,8},{8,7},{9,10},{10,9},{11,... | collective-permute-start | bytes 614408 | tf_op jit(solution)/shard_map/ppermute | solution.py:392
  31.1 0.0 collective-permute-done.in_a
  31.1 0.0 collective-permute-done.1.in_b
  31.1 3.5 %guest.2 = (f32[2,8,512]{2,1,0:T(8,128)S(1)}, f32[2,128,512]{2,1,0:T(8,128)S(1)}, bf16[544,128]{1,0:T(8,128)(2,1)S(1)}, bf16[544,128]{1,0:T(8,128)(2,1)S(1)}, f3...) custom-call(s32[4,6]{1,0:T(4,128)S(1)} %copy-done.4, ...), custom_call_target="tpu_custom_call" | custom-call | flops 4294967296 | bytes 6807648 | tf_op jit(solution)/shard_map/guest/pallas_call | solution.py:366
  34.6 2.4 %collective-permute-start.2 = (bf16[544,128]{1,0:T(8,128)(2,1)S(1)}, bf16[544,128]{1,0:T(8,128)(2,1)S(1)}, u32[]{:S(2)}, u32[]{:S(2)}) collective-permute-start(bf16[544,128]{1,0:T(8,128)(2,1)S(1)} %get-tuple-element.57), channel_id=1, source_target_pairs={{0,1},{1,0},{2,3},{3,2},{4,5},{5,4},{6,7},{7,6},{8,9},{9,8},{10,11... | collective-permute-start | bytes 417800 | tf_op jit(solution)/shard_map/ppermute | solution.py:392
  37.0 3.4 %collective-permute-start.3 = (bf16[544,128]{1,0:T(8,128)(2,1)S(1)}, bf16[544,128]{1,0:T(8,128)(2,1)S(1)}, u32[]{:S(2)}, u32[]{:S(2)}) collective-permute-start(bf16[544,128]{1,0:T(8,128)(2,1)S(1)} %get-tuple-element.58), channel_id=1, source_target_pairs={{1,2},{2,1},{3,4},{4,3},{5,6},{6,5},{7,8},{8,7},{9,10},{10,9},{11,... | collective-permute-start | bytes 417800 | tf_op jit(solution)/shard_map/ppermute | solution.py:392
  40.4 0.0 collective-permute-done.6.came_a
  40.4 0.0 collective-permute-done.7.came_b
  40.4 0.9 %return.2 = (bf16[256,128]{1,0:T(8,128)(2,1)S(1)}, bf16[256,128]{1,0:T(8,128)(2,1)S(1)}) custom-call(s32[4,6]{1,0:T(4,128)S(1)} %copy-done.4, bf16[512,512]{1,0:T(8,128)(2,1)S(1)} %copy-done, f32[8,128]{1,0:T(8,128)S(1)} %get-tuple-element.61.st_a, f32[8,128]{1,0:T(8,128)S(1)} %get-tuple-element.62.st_b, f32[4,384,128]{2,1,0:T(8,128)S(1)} %get-tuple-element.63.pg, ...), custom_call_target="tpu_custom_call" | custom-call | flops 42949672960 | bytes 2646112 | tf_op jit(solution)/shard_map/return/pallas_call | solution.py:366
  41.4 3.9 %backward.2 = (bf16[512,512]{1,0:T(8,128)(2,1)}, bf16[512,512]{1,0:T(8,128)(2,1)}, bf16[512,512]{1,0:T(8,128)(2,1)}, bf16[512,512]{1,0:T(8,128)(2,1)}, f32[8,128,128]{2,1,0:T(8,128)S(1)}) custom-call(s32[4,6]{1,0:T(4,128)S(1)} %copy-done.4, bf16[512,512]{1,0:T(8,128)(2,1)S(1)} %copy-done.1, bf16[512,512]{1,0:T(8,128)(2,1)S(1)} %copy-done, ...), custom_call_target="tpu_custom_call" | custom-call | bytes 1 | tf_op jit(solution)/shard_map/backward/pallas_call | solution.py:366
  45.3 0.0 collective-permute-done.2.came_a
  45.3 0.5 collective-permute-done.3.came_b
  45.7 0.9 %return.3 = (bf16[768,128]{1,0:T(8,128)(2,1)S(1)}, bf16[768,128]{1,0:T(8,128)(2,1)S(1)}) custom-call(s32[4,6]{1,0:T(4,128)S(1)} %copy-done.4, bf16[512,512]{1,0:T(8,128)(2,1)S(1)} %copy-done, f32[8,128]{1,0:T(8,128)S(1)} %get-tuple-element.52.st_a, f32[8,128]{1,0:T(8,128)S(1)} %get-tuple-element.53.st_b, f32[4,384,128]{2,1,0:T(8,128)S(1)} %get-tuple-element.55.pg, ...), custom_call_target="tpu_custom_call" | custom-call | bytes 1 | tf_op jit(solution)/shard_map/return/pallas_call | solution.py:366
  46.7 1.7 %collective-permute-start.8 = (bf16[768,128]{1,0:T(8,128)(2,1)S(1)}, bf16[768,128]{1,0:T(8,128)(2,1)S(1)}, u32[]{:S(2)}, u32[]{:S(2)}) collective-permute-start(bf16[768,128]{1,0:T(8,128)(2,1)S(1)} %get-tuple-element.75.refs_0_), channel_id=1, source_target_pairs={{0,1},{1,0},{2,3},{3,2},{4,5},{5,4},{6,7},{7,6},{8,9},{9,8},{10,11... | collective-permute-start | bytes 589832 | tf_op jit(solution)/shard_map/ppermute | solution.py:392
  48.4 3.0 %collective-permute-start.9 = (bf16[768,128]{1,0:T(8,128)(2,1)S(1)}, bf16[768,128]{1,0:T(8,128)(2,1)S(1)}, u32[]{:S(2)}, u32[]{:S(2)}) collective-permute-start(bf16[768,128]{1,0:T(8,128)(2,1)S(1)} %get-tuple-element.84), channel_id=1, source_target_pairs={{1,2},{2,1},{3,4},{4,3},{5,6},{6,5},{7,8},{8,7},{9,10},{10,9},{11,... | collective-permute-start | bytes 589832 | tf_op jit(solution)/shard_map/ppermute | solution.py:392
  51.4 3.9 %backward.3 = (bf16[512,512]{1,0:T(8,128)(2,1)}, bf16[512,512]{1,0:T(8,128)(2,1)}, bf16[512,512]{1,0:T(8,128)(2,1)}, bf16[512,512]{1,0:T(8,128)(2,1)}, f32[8,128,128]{2,1,0:T(8,128)S(1)}) custom-call(s32[4,6]{1,0:T(4,128)S(1)} %copy-done.4, ...), custom_call_target="tpu_custom_call", output_to_operand_aliasing={{0}: (17, {}), {1}: (18, {}), {2}: (19, {}), {3}: (20, {})} | custom-call | bytes 1 | tf_op jit(solution)/shard_map/backward/pallas_call | solution.py:366
  55.3 0.0 collective-permute-done.8.last_a
  55.3 2.5 %collective-permute-done.9.last_b = bf16[768,128]{1,0:T(8,128)(2,1)S(1)} collective-permute-done((bf16[768,128]{1,0:T(8,128)(2,1)S(1)}, bf16[768,128]{1,0:T(8,128)(2,1)S(1)}, u32[]{:S(2)}, u32[]{:S(2)}) %collective-permute-start.9) | collective-permute-done | bytes 196640 | tf_op jit(solution)/shard_map/ppermute | solution.py:392
  57.7 1.5 %finish.1 = (bf16[512,512]{1,0:T(8,128)(2,1)}, bf16[512,512]{1,0:T(8,128)(2,1)}) custom-call(s32[4,6]{1,0:T(4,128)S(1)} %copy-done.4, bf16[512,512]{1,0:T(8,128)(2,1)} %get-tuple-element.81.dq, bf16[512,512]{1,0:T(8,128)(2,1)} %get-tuple-element.82.dv, ...), custom_call_target="tpu_custom_call", output_to_operand_aliasing={{0}: (1, {}), {1}: (2, {})} | custom-call | bytes 1 | tf_op jit(solution)/shard_map/finish/pallas_call | solution.py:366
Async XLA Ops:
  0.6 7.7 %copy-start.1 = (bf16[512,512]{1,0:T(8,128)(2,1)S(1)}, bf16[512,512]{1,0:T(8,128)(2,1)}, u32[]{:S(2)}) copy-start(bf16[512,512]{1,0:T(8,128)(2,1)} %q.11) | copy-start | bytes 1572868
  0.6 7.7 %copy-start = (bf16[512,512]{1,0:T(8,128)(2,1)S(1)}, bf16[512,512]{1,0:T(8,128)(2,1)}, u32[]{:S(2)}) copy-start(bf16[512,512]{1,0:T(8,128)(2,1)} %k.15) | copy-start | bytes 1572868
  0.7 7.7 %copy-start.2 = (bf16[512,512]{1,0:T(8,128)(2,1)S(1)}, bf16[512,512]{1,0:T(8,128)(2,1)}, u32[]{:S(2)}) copy-start(bf16[512,512]{1,0:T(8,128)(2,1)} %v.11) | copy-start | bytes 1572868
  0.7 7.7 %copy-start.3 = (bf16[512,512]{1,0:T(8,128)(2,1)S(1)}, bf16[512,512]{1,0:T(8,128)(2,1)}, u32[]{:S(2)}) copy-start(bf16[512,512]{1,0:T(8,128)(2,1)} %g.11) | copy-start | bytes 1572868
  3.4 4.9 %copy-start.4 = (s32[4,6]{1,0:T(4,128)S(1)}, s32[4,6]{1,0:T(4,128)}, u32[]{:S(2)}) copy-start(s32[4,6]{1,0:T(4,128)} %lists.17) | copy-start | bytes 292
  3.5 19.8 %collective-permute-start.4 = (bf16[8,128,128]{2,1,0:T(8,128)(2,1)}, bf16[8,128,128]{2,1,0:T(8,128)(2,1)S(1)}, u32[]{:S(2)}, u32[]{:S(2)}) collective-permute-start(bf16[8,128,128]{2,1,0:T(8,128)(2,1)} %get-tuple-element.59), channel_id=1, source_target_pairs={{0,1},{1,0},{2,3},{3,2},{4,5},{5,4},{6,7},{7,6},{8,9},{9,8},{10,11... | collective-permute-start | bytes 786440 | tf_op jit(solution)/shard_map/ppermute | solution.py:392
  5.0 18.3 %collective-permute-start.5 = (bf16[8,128,128]{2,1,0:T(8,128)(2,1)}, bf16[8,128,128]{2,1,0:T(8,128)(2,1)S(1)}, u32[]{:S(2)}, u32[]{:S(2)}) collective-permute-start(bf16[8,128,128]{2,1,0:T(8,128)(2,1)} %get-tuple-element.60), channel_id=1, source_target_pairs={{1,2},{2,1},{3,4},{4,3},{5,6},{6,5},{7,8},{8,7},{9,10},{10,9},{11,... | collective-permute-start | bytes 786440 | tf_op jit(solution)/shard_map/ppermute | solution.py:392
  11.4 19.6 %collective-permute-start = (bf16[8,128,128]{2,1,0:T(8,128)(2,1)S(1)}, bf16[8,128,128]{2,1,0:T(8,128)(2,1)S(1)}, u32[]{:S(2)}, u32[]{:S(2)}) collective-permute-start(bf16[8,128,128]{2,1,0:T(8,128)(2,1)S(1)} %get-tuple-element.46), channel_id=1, source_target_pairs={{0,1},{1,0},{2,3},{3,2},{4,5},{5,4},{6,7},{7,6},{8,9},{9,8},{10,11... | collective-permute-start | bytes 786440 | tf_op jit(solution)/shard_map/ppermute | solution.py:392
  13.1 18.0 %collective-permute-start.1 = (bf16[8,128,128]{2,1,0:T(8,128)(2,1)S(1)}, bf16[8,128,128]{2,1,0:T(8,128)(2,1)S(1)}, u32[]{:S(2)}, u32[]{:S(2)}) collective-permute-start(bf16[8,128,128]{2,1,0:T(8,128)(2,1)S(1)} %get-tuple-element.47), channel_id=1, source_target_pairs={{1,2},{2,1},{3,4},{4,3},{5,6},{6,5},{7,8},{8,7},{9,10},{10,9},{11,... | collective-permute-start | bytes 786440 | tf_op jit(solution)/shard_map/ppermute | solution.py:392
  26.7 13.7 %collective-permute-start.6 = (bf16[800,128]{1,0:T(8,128)(2,1)S(1)}, bf16[800,128]{1,0:T(8,128)(2,1)S(1)}, u32[]{:S(2)}, u32[]{:S(2)}) collective-permute-start(bf16[800,128]{1,0:T(8,128)(2,1)S(1)} %get-tuple-element.65), channel_id=1, source_target_pairs={{0,1},{1,0},{2,3},{3,2},{4,5},{5,4},{6,7},{7,6},{8,9},{9,8},{10,11... | collective-permute-start | bytes 614408 | tf_op jit(solution)/shard_map/ppermute | solution.py:392
  29.2 11.3 %collective-permute-start.7 = (bf16[800,128]{1,0:T(8,128)(2,1)S(1)}, bf16[800,128]{1,0:T(8,128)(2,1)S(1)}, u32[]{:S(2)}, u32[]{:S(2)}) collective-permute-start(bf16[800,128]{1,0:T(8,128)(2,1)S(1)} %get-tuple-element.66), channel_id=1, source_target_pairs={{1,2},{2,1},{3,4},{4,3},{5,6},{6,5},{7,8},{8,7},{9,10},{10,9},{11,... | collective-permute-start | bytes 614408 | tf_op jit(solution)/shard_map/ppermute | solution.py:392
  34.6 10.7 %collective-permute-start.2 = (bf16[544,128]{1,0:T(8,128)(2,1)S(1)}, bf16[544,128]{1,0:T(8,128)(2,1)S(1)}, u32[]{:S(2)}, u32[]{:S(2)}) collective-permute-start(bf16[544,128]{1,0:T(8,128)(2,1)S(1)} %get-tuple-element.57), channel_id=1, source_target_pairs={{0,1},{1,0},{2,3},{3,2},{4,5},{5,4},{6,7},{7,6},{8,9},{9,8},{10,11... | collective-permute-start | bytes 417800 | tf_op jit(solution)/shard_map/ppermute | solution.py:392
  37.0 8.7 %collective-permute-start.3 = (bf16[544,128]{1,0:T(8,128)(2,1)S(1)}, bf16[544,128]{1,0:T(8,128)(2,1)S(1)}, u32[]{:S(2)}, u32[]{:S(2)}) collective-permute-start(bf16[544,128]{1,0:T(8,128)(2,1)S(1)} %get-tuple-element.58), channel_id=1, source_target_pairs={{1,2},{2,1},{3,4},{4,3},{5,6},{6,5},{7,8},{8,7},{9,10},{10,9},{11,... | collective-permute-start | bytes 417800 | tf_op jit(solution)/shard_map/ppermute | solution.py:392
  46.7 8.6 %collective-permute-start.8 = (bf16[768,128]{1,0:T(8,128)(2,1)S(1)}, bf16[768,128]{1,0:T(8,128)(2,1)S(1)}, u32[]{:S(2)}, u32[]{:S(2)}) collective-permute-start(bf16[768,128]{1,0:T(8,128)(2,1)S(1)} %get-tuple-element.75.refs_0_), channel_id=1, source_target_pairs={{0,1},{1,0},{2,3},{3,2},{4,5},{5,4},{6,7},{7,6},{8,9},{9,8},{10,11... | collective-permute-start | bytes 589832 | tf_op jit(solution)/shard_map/ppermute | solution.py:392
  48.4 9.3 %collective-permute-start.9 = (bf16[768,128]{1,0:T(8,128)(2,1)S(1)}, bf16[768,128]{1,0:T(8,128)(2,1)S(1)}, u32[]{:S(2)}, u32[]{:S(2)}) collective-permute-start(bf16[768,128]{1,0:T(8,128)(2,1)S(1)} %get-tuple-element.84), channel_id=1, source_target_pairs={{1,2},{2,1},{3,4},{4,3},{5,6},{6,5},{7,8},{8,7},{9,10},{10,9},{11,... | collective-permute-start | bytes 589832 | tf_op jit(solution)/shard_map/ppermute | solution.py:392
